TPU v7x, 256 devices: a whole 4x4x8 slice. The times are simulated.
256 devices in a mesh: blk: 128 (over z, y, x_hi, core), map: 2 (over x_lo).
Axes of the slice: x: 4 (x_hi: 2, x_lo: 2; x = x_hi * 2 + x_lo), y: 4, z: 8, core: 2. Of those that a mesh axis runs over, the one named last changes fastest.
Arguments:
- phase_history: bfloat16 [128, 2, 128, 1024], P('blk', 'map'), may hold values from -6 to 6
- tile_curvature: float32 [128], P('blk'), may hold values from 20 to 80
- interp_weights: bfloat16 [128, 512, 512], P('blk'), may hold values from -0.25 to 0.25
- strip_tiles: int32 [128, 2, 256, 1], P('blk', 'map'), may hold values from 0 to 127; in each aligned block of 256 rows (0 to 255, 256 to 511, ..., all dimensions but the last counted through in order) at most 4 rows name the same one
- row_offsets: int32 [128, 2, 256], P('blk', 'map'), may hold values from 0 to 255
- tile_owner: int32 [128], replicated, may hold values from 0 to 127, each once
Outputs:
- map_power: float32 [128, 2, 256, 512], P('blk', 'map')
Inputs may be any that keep to these rules, and one draw needn't show every extreme that they name: `strip_tiles`: among the rows of one device no map tile is named more than 4 times, and in every draw some device names some tile exactly 4 times. `tile_owner`: every blk index holds exactly one map tile.
All inputs are finite; a program needn't handle non-finite values.
Results may differ from a plain program's by a relative error of at most 0.0055.
Values may be sent and summed in bfloat16 or wider, within the bound.
No kernel may reach another device: no remote copies, remote signals or barrier semaphores. Data moves between devices by JAX's collectives and lax.ppermute only.
A program may use at most 64 MiB of HBM per device.

v0:
```python
import math

import jax
import jax.numpy as jnp
from jax import lax
from jax.sharding import PartitionSpec as P

STOPS = 8
MAPH = 256


def from_behind(block, axis, distance):
    devices = range(lax.axis_size(axis))
    route = [((i - distance) % len(devices), i) for i in devices]
    return lax.ppermute(block, axis, route)


def range_matrix(freq_count, column_count):
    freq_index = jnp.arange(freq_count, dtype=jnp.int32)[:, None]
    column_index = jnp.arange(column_count, dtype=jnp.int32)[None, :]
    angle = (freq_index * column_index % freq_count).astype(jnp.float32) * (
        2.0 * math.pi / freq_count
    )
    factor = 1.0 / math.sqrt(freq_count)
    real_part = jnp.cos(angle) * factor
    imag_part = -jnp.sin(angle) * factor
    upper = jnp.concatenate([real_part, imag_part], axis=1)
    lower = jnp.concatenate([-imag_part, real_part], axis=1)
    return jnp.concatenate([upper, lower], axis=0).astype(jnp.bfloat16)


def cross_rows(stop_index, map_index, row_index, map_count, pulse_count, span):
    pulse_index = jnp.arange(pulse_count, dtype=jnp.int32)[None, :]
    along = (stop_index * map_count + map_index) * pulse_count + pulse_index
    angle = (row_index[:, None] * along % span).astype(jnp.float32) * (2.0 * math.pi / span)
    factor = 1.0 / math.sqrt(span)
    return jnp.concatenate([jnp.cos(angle) * factor, -jnp.sin(angle) * factor], axis=1).astype(
        jnp.bfloat16
    )


def apply_phase(
    source_block, curvature, stop_index, map_index, map_count, pulse_count, freq_count, span
):
    pulse_index = jnp.arange(pulse_count, dtype=jnp.int32)
    along = ((stop_index * map_count + map_index) * pulse_count + pulse_index).astype(
        jnp.float32
    ) / span - 0.5
    relative = jnp.arange(freq_count, dtype=jnp.int32).astype(jnp.float32) / freq_count - 0.5
    phase_angle = curvature * (along * along)[:, None] * (1.0 + relative[None, :])
    cosine = jnp.cos(phase_angle)
    sine = jnp.sin(phase_angle)
    values = source_block.astype(jnp.float32)
    real_part = values[:, :freq_count]
    imag_part = values[:, freq_count:]
    return jnp.concatenate(
        [real_part * cosine - imag_part * sine, real_part * sine + imag_part * cosine], axis=1
    ).astype(jnp.bfloat16)


def stack_spectrum(spectrum_now):
    half_width = spectrum_now.shape[1] // 2
    real_part = spectrum_now[:, :half_width]
    imag_part = spectrum_now[:, half_width:]
    upper = jnp.concatenate([real_part, imag_part], axis=1)
    lower = jnp.concatenate([-imag_part, real_part], axis=1)
    return jnp.concatenate([upper, lower], axis=0)


def body(phase_history, tile_curvature, interp_weights, strip_tiles, row_offsets, tile_owner):
    blk_count = lax.axis_size("blk")
    map_count = lax.axis_size("map")
    here_map = lax.axis_index("map")
    own_block = phase_history[0, 0]
    pulse_count = own_block.shape[0]
    freq_count = own_block.shape[1] // 2
    columns = interp_weights.shape[2]
    rows_here = strip_tiles.shape[2]
    tile_rows = rows_here * map_count
    span = STOPS * map_count * pulse_count
    curvature = tile_curvature[0]
    ranges = range_matrix(freq_count, columns)
    lead_count = STOPS // 2 - 1
    every_row = jnp.arange(tile_rows, dtype=jnp.int32)
    running = jnp.zeros((tile_rows, 2 * columns), jnp.float32)
    current = from_behind(own_block, "blk", lead_count)
    for stop_index in range(STOPS):
        if stop_index > 0:
            current = from_behind(current, "blk", -1)
        phased = apply_phase(
            current, curvature, stop_index, here_map, map_count, pulse_count, freq_count, span
        )
        spectrum_now = jnp.dot(phased, ranges, preferred_element_type=jnp.float32).astype(
            jnp.bfloat16
        )
        left_side = cross_rows(stop_index, here_map, every_row, map_count, pulse_count, span)
        right_side = stack_spectrum(spectrum_now)
        running = running + jnp.dot(left_side, right_side, preferred_element_type=jnp.float32)
    image_rows = lax.psum_scatter(running, "map", scatter_dimension=0, tiled=True).astype(
        jnp.bfloat16
    )
    capacity = max(2, 2 * rows_here // blk_count)
    holder_index = jnp.arange(blk_count, dtype=jnp.int32)
    row_tiles = strip_tiles[0, 0, :, 0]
    own_offsets = row_offsets[0, 0]
    tile_match = row_tiles[:, None] == holder_index[None, :]
    destination = jnp.sum(jnp.where(tile_match, tile_owner[None, :], 0), axis=1)
    dest_hot = (destination[:, None] == holder_index[None, :]).astype(jnp.int32)
    rank_within = jnp.sum(jnp.cumsum(dest_hot, axis=0) * dest_hot, axis=1) - 1
    slot_index = destination * capacity + rank_within
    slot_hot = jnp.arange(blk_count * capacity, dtype=jnp.int32)[:, None] == slot_index[None, :]
    packed = jnp.dot(
        slot_hot.astype(jnp.bfloat16), image_rows, preferred_element_type=jnp.float32
    ).astype(jnp.bfloat16)
    slot_offsets = jnp.sum(jnp.where(slot_hot, own_offsets[None, :] + 1, 0), axis=1) - 1
    packed = packed.reshape(blk_count, capacity, 2 * columns)
    slot_offsets = slot_offsets.reshape(blk_count, capacity)
    weights = interp_weights[0]
    arrived_rows = lax.all_to_all(packed, "blk", split_axis=0, concat_axis=0, tiled=True)
    arrived_offsets = lax.all_to_all(slot_offsets, "blk", split_axis=0, concat_axis=0, tiled=True)
    split_rows = arrived_rows.reshape(arrived_rows.shape[0], arrived_rows.shape[1], 2, columns)
    mapped = jnp.einsum("sikc,cd->sikd", split_rows, weights, preferred_element_type=jnp.float32)
    power_rows = jnp.sum(mapped * mapped, axis=2)
    flat_power = power_rows.reshape(-1, columns)
    flat_offsets = arrived_offsets.reshape(-1)
    place_hot = (jnp.arange(MAPH, dtype=jnp.int32)[:, None] == flat_offsets[None, :]).astype(
        jnp.float32
    )
    tile_map = jnp.dot(
        place_hot, flat_power, precision=lax.Precision.HIGHEST, preferred_element_type=jnp.float32
    )
    return tile_map.reshape(1, 1, MAPH, columns)


def solution(mesh):
    in_specs = (
        P("blk", "map", None, None),
        P("blk"),
        P("blk", None, None),
        P("blk", "map", None, None),
        P("blk", "map", None),
        P(),
    )
    out_specs = P("blk", "map", None, None)
    return jax.shard_map(body, mesh=mesh, in_specs=in_specs, out_specs=out_specs, check_vma=False)
```

profile of v0, /device:TPU:32, one launch (start us, length us, event | category | flops | bytes accessed | tf_op | source)
XLA Modules:
  0.0 218.5 jit_solution(12205805466895590928)
XLA Ops:
  6.5 2.5 %collective-permute-start = (bf16[128,1024]{1,0:T(8,128)(2,1)}, bf16[128,1024]{1,0:T(8,128)(2,1)}, u32[]{:S(2)}, u32[]{:S(2)}) collective-permute-start(bf16[128,1024]{1,0:T(8,128)(2,1)} %bitcast.41), channel_id=1, source_target_pairs={{250,0},{252,2},{254,4},{0,6},{2,8},{4,10},{6,12},{8,14},{10,16},{... | collective-permute-start | bytes 786440 | tf_op jit(solution)/shard_map/ppermute | solution.py:15
  9.0 4.0 %fusion.6 = bf16[512,512]{1,0:T(8,128)(2,1)S(1)} fusion(), kind=kLoop, calls=%fused_computation.25 | loop fusion | flops 4456448 | bytes 524288 | tf_op jit(solution)/shard_map/convert.33
  13.0 4.4 %negate_convert_fusion = (bf16[512,512]{1,0:T(8,128)(2,1)S(1)}, bf16[512,512]{1,0:T(8,128)(2,1)S(1)}) fusion(), kind=kLoop, calls=%fused_computation.19 | loop fusion | flops 5242880 | bytes 1048576 | tf_op jit(solution)/shard_map/convert.30
  25.1 3.9 %collective-permute-start.1 = (bf16[128,1024]{1,0:T(8,128)(2,1)}, bf16[128,1024]{1,0:T(8,128)(2,1)S(1)}, u32[]{:S(2)}, u32[]{:S(2)}) collective-permute-start(bf16[128,1024]{1,0:T(8,128)(2,1)} %collective-permute-done), channel_id=1, source_target_pairs={{2,0},{4,2},{6,4},{8,6},{10,8},{12,10},{14,12},{16,14},{18,16},{20... | collective-permute-start | bytes 786440 | tf_op jit(solution)/shard_map/ppermute | solution.py:15
  30.1 3.1 %collective-permute-done.1 = bf16[128,1024]{1,0:T(8,128)(2,1)S(1)} collective-permute-done((bf16[128,1024]{1,0:T(8,128)(2,1)}, bf16[128,1024]{1,0:T(8,128)(2,1)S(1)}, u32[]{:S(2)}, u32[]{:S(2)}) %collective-permute-start.1) | collective-permute-done | bytes 262176 | tf_op jit(solution)/shard_map/ppermute | solution.py:15
  33.2 6.3 %collective-permute-start.2 = (bf16[128,1024]{1,0:T(8,128)(2,1)S(1)}, bf16[128,1024]{1,0:T(8,128)(2,1)S(1)}, u32[]{:S(2)}, u32[]{:S(2)}) collective-permute-start(bf16[128,1024]{1,0:T(8,128)(2,1)S(1)} %collective-permute-done.1), channel_id=1, source_target_pairs={{2,0},{4,2},{6,4},{8,6},{10,8},{12,10},{14,12},{16,14},{18,16},{20... | collective-permute-start | bytes 786440 | tf_op jit(solution)/shard_map/ppermute | solution.py:15
  43.5 2.3 %fusion.117 = (bf16[128,512]{1,0:T(8,128)(2,1)S(1)}, bf16[128,512]{1,0:T(8,128)(2,1)S(1)}, bf16[128,512]{1,0:T(8,128)(2,1)S(1)}, bf16[128,512]{1,0:T(8,128)(2,1)S(1)}) fusion(f32[128,1024]{1,0:T(8,128)S(1)} %convert_element_type.197, f32[512]{0:T(512)S(1)} %multiply_add_fusion, f32[128]{0:T(128)S(1)} %get-tuple-element.68, ...), kind=kLoop, calls=%fused_computation.179 | loop fusion | flops 1179648 | bytes 1575936 | tf_op jit(solution)/shard_map/convert.34
  46.3 6.5 %collective-permute-start.3 = (bf16[128,1024]{1,0:T(8,128)(2,1)S(1)}, bf16[128,1024]{1,0:T(8,128)(2,1)S(1)}, u32[]{:S(2)}, u32[]{:S(2)}) collective-permute-start(bf16[128,1024]{1,0:T(8,128)(2,1)S(1)} %collective-permute-done.2), channel_id=1, source_target_pairs={{2,0},{4,2},{6,4},{8,6},{10,8},{12,10},{14,12},{16,14},{18,16},{20... | collective-permute-start | bytes 786440 | tf_op jit(solution)/shard_map/ppermute | solution.py:15
  53.2 3.4 %collective-permute-done.3 = bf16[128,1024]{1,0:T(8,128)(2,1)S(1)} collective-permute-done((bf16[128,1024]{1,0:T(8,128)(2,1)S(1)}, bf16[128,1024]{1,0:T(8,128)(2,1)S(1)}, u32[]{:S(2)}, u32[]{:S(2)}) %collective-permute-start.3) | collective-permute-done | bytes 262176 | tf_op jit(solution)/shard_map/ppermute | solution.py:15
  56.6 6.4 %collective-permute-start.4 = (bf16[128,1024]{1,0:T(8,128)(2,1)S(1)}, bf16[128,1024]{1,0:T(8,128)(2,1)S(1)}, u32[]{:S(2)}, u32[]{:S(2)}) collective-permute-start(bf16[128,1024]{1,0:T(8,128)(2,1)S(1)} %collective-permute-done.3), channel_id=1, source_target_pairs={{2,0},{4,2},{6,4},{8,6},{10,8},{12,10},{14,12},{16,14},{18,16},{20... | collective-permute-start | bytes 786440 | tf_op jit(solution)/shard_map/ppermute | solution.py:15
  64.0 2.9 %collective-permute-done.4 = bf16[128,1024]{1,0:T(8,128)(2,1)S(1)} collective-permute-done((bf16[128,1024]{1,0:T(8,128)(2,1)S(1)}, bf16[128,1024]{1,0:T(8,128)(2,1)S(1)}, u32[]{:S(2)}, u32[]{:S(2)}) %collective-permute-start.4) | collective-permute-done | bytes 262176 | tf_op jit(solution)/shard_map/ppermute | solution.py:15
  67.0 3.3 %fusion.113 = (bf16[128,512]{1,0:T(8,128)(2,1)S(1)}, bf16[128,512]{1,0:T(8,128)(2,1)S(1)}, bf16[128,512]{1,0:T(8,128)(2,1)S(1)}, bf16[128,512]{1,0:T(8,128)(2,1)...) fusion(f32[128,1024]{1,0:T(8,128)S(1)} %convert_element_type.203, f32[128]{0:T(128)S(1)} %multiply_multiply_fusion.6, ...), kind=kLoop, calls=%fused_computation.175 | loop fusion | flops 1769472 | bytes 2362880 | tf_op jit(solution)/shard_map/convert.24
  71.2 6.5 %collective-permute-start.5 = (bf16[128,1024]{1,0:T(8,128)(2,1)S(1)}, bf16[128,1024]{1,0:T(8,128)(2,1)S(1)}, u32[]{:S(2)}, u32[]{:S(2)}) collective-permute-start(bf16[128,1024]{1,0:T(8,128)(2,1)S(1)} %collective-permute-done.4), channel_id=1, source_target_pairs={{2,0},{4,2},{6,4},{8,6},{10,8},{12,10},{14,12},{16,14},{18,16},{20... | collective-permute-start | bytes 786440 | tf_op jit(solution)/shard_map/ppermute | solution.py:15
  78.2 3.4 %collective-permute-done.5 = bf16[128,1024]{1,0:T(8,128)(2,1)S(1)} collective-permute-done((bf16[128,1024]{1,0:T(8,128)(2,1)S(1)}, bf16[128,1024]{1,0:T(8,128)(2,1)S(1)}, u32[]{:S(2)}, u32[]{:S(2)}) %collective-permute-start.5) | collective-permute-done | bytes 262176 | tf_op jit(solution)/shard_map/ppermute | solution.py:15
  81.6 6.4 %collective-permute-start.6 = (bf16[128,1024]{1,0:T(8,128)(2,1)S(1)}, bf16[128,1024]{1,0:T(8,128)(2,1)S(1)}, u32[]{:S(2)}, u32[]{:S(2)}) collective-permute-start(bf16[128,1024]{1,0:T(8,128)(2,1)S(1)} %collective-permute-done.5), channel_id=1, source_target_pairs={{2,0},{4,2},{6,4},{8,6},{10,8},{12,10},{14,12},{16,14},{18,16},{20... | collective-permute-start | bytes 786440 | tf_op jit(solution)/shard_map/ppermute | solution.py:15
  88.5 3.4 %collective-permute-done.6 = bf16[128,1024]{1,0:T(8,128)(2,1)S(1)} collective-permute-done((bf16[128,1024]{1,0:T(8,128)(2,1)S(1)}, bf16[128,1024]{1,0:T(8,128)(2,1)S(1)}, u32[]{:S(2)}, u32[]{:S(2)}) %collective-permute-start.6) | collective-permute-done | bytes 262176 | tf_op jit(solution)/shard_map/ppermute | solution.py:15
  91.9 6.4 %collective-permute-start.7 = (bf16[128,1024]{1,0:T(8,128)(2,1)S(1)}, bf16[128,1024]{1,0:T(8,128)(2,1)S(1)}, u32[]{:S(2)}, u32[]{:S(2)}) collective-permute-start(bf16[128,1024]{1,0:T(8,128)(2,1)S(1)} %collective-permute-done.6), channel_id=1, source_target_pairs={{2,0},{4,2},{6,4},{8,6},{10,8},{12,10},{14,12},{16,14},{18,16},{20... | collective-permute-start | bytes 786440 | tf_op jit(solution)/shard_map/ppermute | solution.py:15
  99.4 2.9 %collective-permute-done.7 = bf16[128,1024]{1,0:T(8,128)(2,1)S(1)} collective-permute-done((bf16[128,1024]{1,0:T(8,128)(2,1)S(1)}, bf16[128,1024]{1,0:T(8,128)(2,1)S(1)}, u32[]{:S(2)}, u32[]{:S(2)}) %collective-permute-start.7) | collective-permute-done | bytes 262176 | tf_op jit(solution)/shard_map/ppermute | solution.py:15
  102.3 3.3 %fusion.89 = (bf16[128,512]{1,0:T(8,128)(2,1)S(1)}, bf16[128,512]{1,0:T(8,128)(2,1)S(1)}, bf16[128,512]{1,0:T(8,128)(2,1)S(1)}, bf16[128,512]{1,0:T(8,128)(2,1)S...) fusion(f32[128,1024]{1,0:T(8,128)S(1)} %convert_element_type.227, f32[128]{0:T(128)S(1)} %get-tuple-element.63, ...), kind=kLoop, calls=%fused_computation.151 | loop fusion | flops 1769472 | bytes 2362880 | tf_op jit(solution)/shard_map/convert
  107.9 2.1 add_add_fusion
  112.5 23.4 %all-to-all-start = ((s32[128,1,4]{2,1,0:T(1,128)}), s32[128,1,4]{2,1,0:T(1,128)S(1)}, u32[]{:S(2)}, u32[]{:S(2)}) async-start(s32[128,1,4]{2,1,0:T(1,128)} %bitcast.6), calls=%async_computation | async-start | bytes 131072 | tf_op jit(solution)/shard_map/all_to_all | solution.py:120
  135.9 23.0 %reduce-scatter.2.cloned.1.call-done = f32[256,1024]{1,0:T(8,128)} async-done(((f32[512,1024]{1,0:T(8,128)}), f32[256,1024]{1,0:T(8,128)}) %reduce-scatter.2.cloned.1.call-update) | async-done | bytes 1048592 | tf_op jit(solution)/shard_map/reduce_scatter | solution.py:99
  161.8 13.4 %all-to-all-start.1 = ((bf16[128,4,1024]{2,1,0:T(4,128)(2,1)}), bf16[128,4,1024]{2,1,0:T(4,128)(2,1)S(1)}, u32[]{:S(2)}, u32[]{:S(2)}) async-start(bf16[128,4,1024]{2,1,0:T(4,128)(2,1)} %reshape.192), calls=%async_computation.2 | async-start | bytes 2097152 | tf_op jit(solution)/shard_map/all_to_all | solution.py:119
  176.6 30.8 %all-to-all-done.1 = bf16[128,4,1024]{2,1,0:T(4,128)(2,1)S(1)} async-done(((bf16[128,4,1024]{2,1,0:T(4,128)(2,1)}), bf16[128,4,1024]{2,1,0:T(4,128)(2,1)S(1)}, u32[]{:S(2)}, u32[]{:S(2)}) %all-to-all-start.1) | async-done | bytes 1048608 | tf_op jit(solution)/shard_map/all_to_all | solution.py:119
  (91 shorter events, 29.8 us)
Async XLA Ops:
  6.5 201.8 %copy-start = (bf16[1,512,512]{2,1,0:T(8,128)(2,1)S(1)}, bf16[1,512,512]{2,1,0:T(8,128)(2,1)}, u32[]{:S(2)}) copy-start(bf16[1,512,512]{2,1,0:T(8,128)(2,1)} %param.8) | copy-start | bytes 1572868
  6.5 152.3 %reduce-scatter.2.cloned.1.call-start = ((), (), s32[]{:S(2)}) async-start(), calls=%async_computation.3 | async-start | bytes 3145728 | tf_op jit(solution)/shard_map/reduce_scatter | solution.py:99
  6.5 18.5 %collective-permute-start = (bf16[128,1024]{1,0:T(8,128)(2,1)}, bf16[128,1024]{1,0:T(8,128)(2,1)}, u32[]{:S(2)}, u32[]{:S(2)}) collective-permute-start(bf16[128,1024]{1,0:T(8,128)(2,1)} %bitcast.41), channel_id=1, source_target_pairs={{250,0},{252,2},{254,4},{0,6},{2,8},{4,10},{6,12},{8,14},{10,16},{... | collective-permute-start | bytes 786440 | tf_op jit(solution)/shard_map/ppermute | solution.py:15
  25.1 8.1 %collective-permute-start.1 = (bf16[128,1024]{1,0:T(8,128)(2,1)}, bf16[128,1024]{1,0:T(8,128)(2,1)S(1)}, u32[]{:S(2)}, u32[]{:S(2)}) collective-permute-start(bf16[128,1024]{1,0:T(8,128)(2,1)} %collective-permute-done), channel_id=1, source_target_pairs={{2,0},{4,2},{6,4},{8,6},{10,8},{12,10},{14,12},{16,14},{18,16},{20... | collective-permute-start | bytes 786440 | tf_op jit(solution)/shard_map/ppermute | solution.py:15
  33.2 10.2 %collective-permute-start.2 = (bf16[128,1024]{1,0:T(8,128)(2,1)S(1)}, bf16[128,1024]{1,0:T(8,128)(2,1)S(1)}, u32[]{:S(2)}, u32[]{:S(2)}) collective-permute-start(bf16[128,1024]{1,0:T(8,128)(2,1)S(1)} %collective-permute-done.1), channel_id=1, source_target_pairs={{2,0},{4,2},{6,4},{8,6},{10,8},{12,10},{14,12},{16,14},{18,16},{20... | collective-permute-start | bytes 786440 | tf_op jit(solution)/shard_map/ppermute | solution.py:15
  46.3 10.4 %collective-permute-start.3 = (bf16[128,1024]{1,0:T(8,128)(2,1)S(1)}, bf16[128,1024]{1,0:T(8,128)(2,1)S(1)}, u32[]{:S(2)}, u32[]{:S(2)}) collective-permute-start(bf16[128,1024]{1,0:T(8,128)(2,1)S(1)} %collective-permute-done.2), channel_id=1, source_target_pairs={{2,0},{4,2},{6,4},{8,6},{10,8},{12,10},{14,12},{16,14},{18,16},{20... | collective-permute-start | bytes 786440 | tf_op jit(solution)/shard_map/ppermute | solution.py:15
  56.6 10.3 %collective-permute-start.4 = (bf16[128,1024]{1,0:T(8,128)(2,1)S(1)}, bf16[128,1024]{1,0:T(8,128)(2,1)S(1)}, u32[]{:S(2)}, u32[]{:S(2)}) collective-permute-start(bf16[128,1024]{1,0:T(8,128)(2,1)S(1)} %collective-permute-done.3), channel_id=1, source_target_pairs={{2,0},{4,2},{6,4},{8,6},{10,8},{12,10},{14,12},{16,14},{18,16},{20... | collective-permute-start | bytes 786440 | tf_op jit(solution)/shard_map/ppermute | solution.py:15
  71.2 10.4 %collective-permute-start.5 = (bf16[128,1024]{1,0:T(8,128)(2,1)S(1)}, bf16[128,1024]{1,0:T(8,128)(2,1)S(1)}, u32[]{:S(2)}, u32[]{:S(2)}) collective-permute-start(bf16[128,1024]{1,0:T(8,128)(2,1)S(1)} %collective-permute-done.4), channel_id=1, source_target_pairs={{2,0},{4,2},{6,4},{8,6},{10,8},{12,10},{14,12},{16,14},{18,16},{20... | collective-permute-start | bytes 786440 | tf_op jit(solution)/shard_map/ppermute | solution.py:15
  81.6 10.3 %collective-permute-start.6 = (bf16[128,1024]{1,0:T(8,128)(2,1)S(1)}, bf16[128,1024]{1,0:T(8,128)(2,1)S(1)}, u32[]{:S(2)}, u32[]{:S(2)}) collective-permute-start(bf16[128,1024]{1,0:T(8,128)(2,1)S(1)} %collective-permute-done.5), channel_id=1, source_target_pairs={{2,0},{4,2},{6,4},{8,6},{10,8},{12,10},{14,12},{16,14},{18,16},{20... | collective-permute-start | bytes 786440 | tf_op jit(solution)/shard_map/ppermute | solution.py:15
  91.9 10.3 %collective-permute-start.7 = (bf16[128,1024]{1,0:T(8,128)(2,1)S(1)}, bf16[128,1024]{1,0:T(8,128)(2,1)S(1)}, u32[]{:S(2)}, u32[]{:S(2)}) collective-permute-start(bf16[128,1024]{1,0:T(8,128)(2,1)S(1)} %collective-permute-done.6), channel_id=1, source_target_pairs={{2,0},{4,2},{6,4},{8,6},{10,8},{12,10},{14,12},{16,14},{18,16},{20... | collective-permute-start | bytes 786440 | tf_op jit(solution)/shard_map/ppermute | solution.py:15
  110.1 0.7 copy-start.1
  110.1 0.7 copy-start.3
  110.1 1.5 copy-start.2
  112.5 49.3 %all-to-all-start = ((s32[128,1,4]{2,1,0:T(1,128)}), s32[128,1,4]{2,1,0:T(1,128)S(1)}, u32[]{:S(2)}, u32[]{:S(2)}) async-start(s32[128,1,4]{2,1,0:T(1,128)} %bitcast.6), calls=%async_computation | async-start | bytes 131072 | tf_op jit(solution)/shard_map/all_to_all | solution.py:120
  161.8 45.6 %all-to-all-start.1 = ((bf16[128,4,1024]{2,1,0:T(4,128)(2,1)}), bf16[128,4,1024]{2,1,0:T(4,128)(2,1)S(1)}, u32[]{:S(2)}, u32[]{:S(2)}) async-start(bf16[128,4,1024]{2,1,0:T(4,128)(2,1)} %reshape.192), calls=%async_computation.2 | async-start | bytes 2097152 | tf_op jit(solution)/shard_map/all_to_all | solution.py:119
Sparse Core Ops, SparseCore 0:
  110.2 48.5 reduce-scatter.1
where the time goes:
time: 219 us
  starting transfers between devices  81.7 us (37%)
  waiting for transfers between devices  74.7 us (34%)
  other arithmetic  29.4 us (13%)
  between operations  14.6 us (7%)
  matrix products  12.7 us (6%)
  local copies, waits for them, and re-layouts  5.39 us (2%)
    ppermute x8, starting transfers between devices, from_behind(): return lax.ppermute(block, axis, route)  45 us
    all_to_all x1, waiting for transfers between devices, body(): lax.all_to_all(packed, 'blk', split_axis=0, concat_axis=0, tiled=True)  30.8 us
    another operation x16, other arithmetic  26.6 us
    all_to_all x1, starting transfers between devices, body(): lax.all_to_all(slot_offsets, 'blk', split_axis=0, concat_axis=0, tiled=True)  23.4 us
    reduce_scatter x1, waiting for transfers between devices, body(): lax.psum_scatter(running, 'map', scatter_dimension=0, tiled=True)  23 us
    ppermute x8, waiting for transfers between devices, from_behind(): return lax.ppermute(block, axis, route)  20.9 us
    all_to_all x1, starting transfers between devices, body(): lax.all_to_all(packed, 'blk', split_axis=0, concat_axis=0, tiled=True)  13.4 us
    dot_general x8, matrix products, body(): jnp.dot(left_side, right_side, preferred_element_type=jnp.float32)  5.24 us
  transfers between devices with their start and end apart: 11, of which 9 were waited for; matrix products, arithmetic and copies ran while one was open for 13% of the time, Pallas kernels for 0%

commit v1 on v0

v1 whole, which is shorter than its diff:
```python
import math

import jax
import jax.numpy as jnp
import ml_dtypes
import numpy as np
from jax import lax
from jax.sharding import PartitionSpec as P

STOPS = 8
MAPH = 256
SIDE = 128


def matching(count, distance, parity):
    seen, pairs = set(), []
    for start in range(count):
        cycle, at = [], start
        while at not in seen:
            seen.add(at)
            cycle.append(at)
            at = (at + distance) % count
        for place in range(parity, len(cycle) + parity, 2) if cycle else ():
            a, b = cycle[place % len(cycle)], cycle[(place + 1) % len(cycle)]
            pairs += [(a, b), (b, a)]
    return pairs


def range_table(freq_count):
    index = np.arange(freq_count, dtype=np.int64)
    angle = (index[:, None] * index[None, :] % freq_count).astype(np.float32) * np.float32(
        2.0 * math.pi / freq_count
    )
    factor = np.float32(1.0 / math.sqrt(freq_count))
    real_part, imag_part = np.cos(angle) * factor, -np.sin(angle) * factor
    table = np.block([[real_part, imag_part], [-imag_part, real_part]])
    return table.astype(ml_dtypes.bfloat16)


def cross_table(map_count, row_count, pulse_count):
    span = STOPS * map_count * pulse_count
    rows = np.arange(row_count, dtype=np.int64)[:, None]
    factor = np.float32(1.0 / math.sqrt(span))
    tables = []
    for m in range(map_count):
        along = np.concatenate(
            [(k * map_count + m) * pulse_count + np.arange(pulse_count) for k in range(STOPS)]
        )
        angle = (rows * along[None, :] % span).astype(np.float32) * np.float32(
            2.0 * math.pi / span
        )
        real_part, imag_part = np.cos(angle) * factor, -np.sin(angle) * factor
        tables.append(np.stack([real_part, imag_part]))
    return np.stack(tables).astype(ml_dtypes.bfloat16)


def apply_phase(block, curvature, stop_index, map_index, map_count, pulse_count, freq_count):
    span = STOPS * map_count * pulse_count
    pulse_index = jnp.arange(pulse_count, dtype=jnp.int32)
    along = ((stop_index * map_count + map_index) * pulse_count + pulse_index).astype(
        jnp.float32
    ) / span - 0.5
    relative = jnp.arange(freq_count, dtype=jnp.int32).astype(jnp.float32) / freq_count - 0.5
    phase_angle = curvature * (along * along)[:, None] * (1.0 + relative[None, :])
    cosine = jnp.cos(phase_angle)
    sine = jnp.sin(phase_angle)
    values = block.astype(jnp.float32)
    real_part = values[:, :freq_count]
    imag_part = values[:, freq_count:]
    return jnp.concatenate(
        [real_part * cosine - imag_part * sine, real_part * sine + imag_part * cosine], axis=1
    ).astype(jnp.bfloat16)


def gather_aperture(own_block, blk_count, here):
    core, chip_odd, group_odd = here % 2, (here // 2) % 2, (here // 4) % 2
    sibling = [(i, i ^ 1) for i in range(blk_count)]

    def swap(block):
        return lax.ppermute(block, "blk", sibling)

    near = [lax.ppermute(own_block, "blk", matching(blk_count, 2, p)) for p in (0, 1)]
    far = [lax.ppermute(own_block, "blk", matching(blk_count, 4, p)) for p in (0, 1)]
    twin = swap(own_block)
    twin_near = [swap(block) for block in near]
    far_up = jnp.where(group_odd == 0, far[0], far[1])
    twin_far = swap(jnp.where(core == group_odd, far[0], far[1]))
    up, down = (jnp.where(chip_odd == p, near[0], near[1]) for p in (0, 1))
    twin_up, twin_down = (jnp.where(chip_odd == p, twin_near[0], twin_near[1]) for p in (0, 1))
    return [
        jnp.where(core == 0, twin_far, twin_down),
        down,
        jnp.where(core == 0, twin_down, twin),
        own_block,
        jnp.where(core == 0, twin, twin_up),
        up,
        jnp.where(core == 0, twin_up, twin_far),
        far_up,
    ]


def body(ranges, crosses, phase_history, tile_curvature, interp_weights, strip_tiles, row_offsets, tile_owner):
    blk_count = lax.axis_size("blk")
    map_count = lax.axis_size("map")
    here_blk = lax.axis_index("blk")
    here_map = lax.axis_index("map")
    own_block = phase_history[0, 0]
    pulse_count = own_block.shape[0]
    freq_count = own_block.shape[1] // 2
    columns = interp_weights.shape[2]
    rows_here = strip_tiles.shape[2]

    blocks = gather_aperture(own_block, blk_count, here_blk)
    phased = [
        apply_phase(b, tile_curvature[0], k, here_map, map_count, pulse_count, freq_count)
        for k, b in enumerate(blocks)
    ]
    spectrum = jnp.concatenate(
        [
            jnp.dot(p, ranges, preferred_element_type=jnp.float32).astype(jnp.bfloat16)
            for p in phased
        ],
        axis=0,
    )
    rotated = jnp.concatenate([-spectrum[:, columns:], spectrum[:, :columns]], axis=1)
    cross = lax.dynamic_index_in_dim(crosses, here_map, 0, keepdims=False)

    def contribution(map_index):
        part = lax.dynamic_slice_in_dim(cross, map_index * rows_here, rows_here, 1)
        return jnp.dot(part[0], spectrum, preferred_element_type=jnp.float32) + jnp.dot(
            part[1], rotated, preferred_element_type=jnp.float32
        )

    sent = contribution(1 - here_map).astype(jnp.bfloat16)
    arrived = lax.ppermute(sent, "map", [(0, 1), (1, 0)])
    image_rows = (contribution(here_map) + arrived.astype(jnp.float32)).astype(jnp.bfloat16)

    capacity = max(2, 2 * rows_here // blk_count)
    holder_index = jnp.arange(blk_count, dtype=jnp.int32)
    row_tiles = strip_tiles[0, 0, :, 0]
    own_offsets = row_offsets[0, 0]
    tile_match = row_tiles[:, None] == holder_index[None, :]
    destination = jnp.sum(jnp.where(tile_match, tile_owner[None, :], 0), axis=1)
    row_number = jnp.arange(rows_here, dtype=jnp.int32)
    same_before = (row_tiles[:, None] == row_tiles[None, :]) & (
        row_number[None, :] < row_number[:, None]
    )
    rank_within = jnp.sum(same_before.astype(jnp.int32), axis=1)
    slot_index = destination * capacity + rank_within
    slot_hot = (
        jnp.arange(blk_count * capacity, dtype=jnp.int32)[:, None] == slot_index[None, :]
    ).astype(jnp.bfloat16)
    side = jnp.broadcast_to(own_offsets.astype(jnp.bfloat16)[:, None], (rows_here, SIDE))
    packed = jnp.dot(
        slot_hot, jnp.concatenate([image_rows, side], axis=1), preferred_element_type=jnp.float32
    ).astype(jnp.bfloat16)
    packed = packed.reshape(blk_count, capacity, 2 * columns + SIDE)
    got = lax.all_to_all(packed, "blk", split_axis=0, concat_axis=0, tiled=True)
    got = got.reshape(blk_count * capacity, 2 * columns + SIDE)

    weights = interp_weights[0]
    real_out = jnp.dot(got[:, :columns], weights, preferred_element_type=jnp.float32)
    imag_out = jnp.dot(got[:, columns : 2 * columns], weights, preferred_element_type=jnp.float32)
    power = real_out * real_out + imag_out * imag_out
    offsets = got[:, 2 * columns].astype(jnp.int32)
    place_hot = (jnp.arange(MAPH, dtype=jnp.int32)[:, None] == offsets[None, :]).astype(
        jnp.bfloat16
    )
    high = power.astype(jnp.bfloat16)
    rest = power - high.astype(jnp.float32)
    middle = rest.astype(jnp.bfloat16)
    low = (rest - middle.astype(jnp.float32)).astype(jnp.bfloat16)
    tile_map = sum(
        jnp.dot(place_hot, piece, preferred_element_type=jnp.float32)
        for piece in (low, middle, high)
    )
    return tile_map.reshape(1, 1, MAPH, columns)


def solution(mesh):
    in_specs = (
        P("blk", "map", None, None),
        P("blk"),
        P("blk", None, None),
        P("blk", "map", None, None),
        P("blk", "map", None),
        P(),
    )
    out_specs = P("blk", "map", None, None)

    def run(*args):
        map_count, pulse_count, width = args[0].shape[1:]
        ranges = jnp.asarray(range_table(width // 2))
        crosses = jnp.asarray(
            cross_table(map_count, map_count * args[3].shape[2], pulse_count)
        )
        held = lambda *here: body(ranges, crosses, *here)
        return jax.shard_map(
            held, mesh=mesh, in_specs=in_specs, out_specs=out_specs, check_vma=False
        )(*args)

    return run
```

time: 219 us -> 114 us (0.52)
  starting transfers between devices: 81.7 us -> 10.7 us
  waiting for transfers between devices: 74.7 us -> 16 us
  blocking collectives: 0 us -> 47.8 us
  other arithmetic: 29.4 us -> 4.42 us
  matrix products: 12.7 us -> 30.8 us
  between operations: 14.6 us -> 1.12 us
  local copies, waits for them, and re-layouts: 5.39 us -> 2.76 us
    all_to_all x0 -> x1, blocking collectives: none -> 47.8 us  [body(): got = lax.all_to_all(packed, 'blk', split_axis=0, concat_axis=0, tiled=True)]
    all_to_all x2 -> x0, starting transfers between devices: 36.8 us -> none  [the longest x1 23.4 us: body(): lax.all_to_all(slot_offsets, 'blk', split_axis=0, concat_axis=0, tiled=True)]
    ppermute x8 -> x9, starting transfers between devices: 45 us -> 10.7 us  [the longest x2 5.38 us: gather_aperture(): lax.ppermute(own_block, 'blk', matching(blk_count, 2, p))]
    all_to_all x2 -> x0, waiting for transfers between devices: 30.8 us -> none  [the longest x1 30.8 us: body(): lax.all_to_all(packed, 'blk', split_axis=0, concat_axis=0, tiled=True)]
    another operation x16 -> x0, other arithmetic: 26.6 us -> none
    reduce_scatter x1 -> x0, waiting for transfers between devices: 23 us -> none  [body(): lax.psum_scatter(running, 'map', scatter_dimension=0, tiled=True)]
    dot_general x19 -> x26, matrix products: 12.7 us -> 30.8 us  [the longest x16 24.8 us: body(): jnp.dot(p, ranges, preferred_element_type=jnp.float32).astype(jnp.bfloat16)]
    ppermute x8 -> x9, waiting for transfers between devices: 20.9 us -> 16 us  [the longest x1 12.6 us: body(): arrived = lax.ppermute(sent, 'map', [(0, 1), (1, 0)])]
  transfers between devices with their start and end apart: 11 -> 9, of which waited for: 9 -> 4; matrix products, arithmetic and copies ran while one was open for 13% -> 10% of each run, Pallas kernels for 0% -> 0%
where the time goes in v1:
time: 114 us
  blocking collectives  47.8 us (42%)
  matrix products  30.8 us (27%)
  waiting for transfers between devices  16 us (14%)
  starting transfers between devices  10.7 us (9%)
  other arithmetic  4.42 us (4%)
  local copies, waits for them, and re-layouts  2.76 us (2%)
    all_to_all x1, blocking collectives, body(): got = lax.all_to_all(packed, 'blk', split_axis=0, concat_axis=0, tiled=True)  47.8 us
    dot_general x16, matrix products, body(): jnp.dot(p, ranges, preferred_element_type=jnp.float32).astype(jnp.bfloat16)  24.8 us
    ppermute x1, waiting for transfers between devices, body(): arrived = lax.ppermute(sent, 'map', [(0, 1), (1, 0)])  12.6 us
    ppermute x2, starting transfers between devices, gather_aperture(): lax.ppermute(own_block, 'blk', matching(blk_count, 2, p))  5.38 us
    ppermute x2, starting transfers between devices, gather_aperture(): lax.ppermute(own_block, 'blk', matching(blk_count, 4, p))  3.3 us
    ppermute x2, waiting for transfers between devices, gather_aperture(): lax.ppermute(own_block, 'blk', matching(blk_count, 2, p))  3.26 us
    convert_element_type x4, other arithmetic, apply_phase(): values = block.astype(jnp.float32)  2.32 us
  transfers between devices with their start and end apart: 9, of which 4 were waited for; matrix products, arithmetic and copies ran while one was open for 10% of the time, Pallas kernels for 0%

profile of v1, /device:TPU:32, one launch (start us, length us, event | category | flops | bytes accessed | tf_op | source)
XLA Modules:
  0.0 113.6 jit_solution(305821686968144884)
XLA Ops:
  0.0 1.6 %collective-permute-start = (bf16[128,1024]{1,0:T(8,128)(2,1)}, bf16[128,1024]{1,0:T(8,128)(2,1)}, u32[]{:S(2)}, u32[]{:S(2)}) collective-permute-start(bf16[128,1024]{1,0:T(8,128)(2,1)} %bitcast.49), channel_id=1, source_target_pairs={{0,8},{8,0},{16,24},{24,16},{32,40},{40,32},{48,56},{56,48},{64,72... | collective-permute-start | bytes 786440 | tf_op jit(solution)/shard_map/ppermute | solution.py:83
  1.6 1.7 %collective-permute-start.1 = (bf16[128,1024]{1,0:T(8,128)(2,1)}, bf16[128,1024]{1,0:T(8,128)(2,1)}, u32[]{:S(2)}, u32[]{:S(2)}) collective-permute-start(bf16[128,1024]{1,0:T(8,128)(2,1)} %bitcast.50), channel_id=1, source_target_pairs={{8,16},{16,8},{24,32},{32,24},{40,48},{48,40},{56,64},{64,56},{72,... | collective-permute-start | bytes 786440 | tf_op jit(solution)/shard_map/ppermute | solution.py:83
  3.3 3.0 %collective-permute-start.3 = (bf16[128,1024]{1,0:T(8,128)(2,1)}, bf16[128,1024]{1,0:T(8,128)(2,1)S(1)}, u32[]{:S(2)}, u32[]{:S(2)}) collective-permute-start(bf16[128,1024]{1,0:T(8,128)(2,1)} %bitcast.51), channel_id=1, source_target_pairs={{0,4},{4,0},{8,12},{12,8},{16,20},{20,16},{24,28},{28,24},{32,36},... | collective-permute-start | bytes 786440 | tf_op jit(solution)/shard_map/ppermute | solution.py:82
  6.3 2.4 %collective-permute-start.5 = (bf16[128,1024]{1,0:T(8,128)(2,1)}, bf16[128,1024]{1,0:T(8,128)(2,1)S(1)}, u32[]{:S(2)}, u32[]{:S(2)}) collective-permute-start(bf16[128,1024]{1,0:T(8,128)(2,1)} %bitcast.52), channel_id=1, source_target_pairs={{4,8},{8,4},{12,16},{16,12},{20,24},{24,20},{28,32},{32,28},{36,40... | collective-permute-start | bytes 786440 | tf_op jit(solution)/shard_map/ppermute | solution.py:82
  12.0 2.6 %fusion.131 = f32[128,1024]{1,0:T(8,128)S(1)} fusion(bf16[512,1024]{1,0:T(8,128)(2,1)} %constant.153, f32[128,1024]{1,0:T(8,128)S(1)} %bitcast_convert_fusion, f32[128]{0:T(128)S(1)} %get-tuple-element.19, f32[512]{0:T(512)S(1)} %multiply_add_fusion), kind=kOutput, calls=%fused_computation.176 | convolution fusion | flops 134545408 | bytes 2099712 | tf_op jit(solution)/shard_map/dot_general | solution.py:120
  17.3 2.6 %collective-permute-done.5 = bf16[128,1024]{1,0:T(8,128)(2,1)S(1)} collective-permute-done((bf16[128,1024]{1,0:T(8,128)(2,1)}, bf16[128,1024]{1,0:T(8,128)(2,1)S(1)}, u32[]{:S(2)}, u32[]{:S(2)}) %collective-permute-start.5) | collective-permute-done | bytes 262176 | tf_op jit(solution)/shard_map/ppermute | solution.py:82
  19.9 1.3 %fusion.127 = f32[128,1024]{1,0:T(8,128)S(1)} fusion(bf16[512,1024]{1,0:T(8,128)(2,1)S(1)} %copy-done.1, f32[128,1024]{1,0:T(8,128)S(1)} %get-tuple-element.16, f32[128]{0:T(128)S(1)} %get-tuple-element.20, f32[512]{0:T(512)S(1)} %multiply_add_fusion), kind=kOutput, calls=%fused_computation.174 | convolution fusion | flops 134545408 | bytes 2099712 | tf_op jit(solution)/shard_map/dot_general | solution.py:120
  21.2 1.3 %fusion.135 = f32[128,1024]{1,0:T(8,128)S(1)} fusion(bf16[512,1024]{1,0:T(8,128)(2,1)S(1)} %copy-done.1, f32[128,1024]{1,0:T(8,128)S(1)} %get-tuple-element.15, f32[128]{0:T(128)S(1)} %get-tuple-element.17, f32[512]{0:T(512)S(1)} %multiply_add_fusion), kind=kOutput, calls=%fused_computation.178 | convolution fusion | flops 134545408 | bytes 2099712 | tf_op jit(solution)/shard_map/dot_general | solution.py:120
  23.1 1.3 %fusion.139 = f32[128,1024]{1,0:T(8,128)S(1)} fusion(bf16[512,1024]{1,0:T(8,128)(2,1)S(1)} %copy-done.1, f32[128,1024]{1,0:T(8,128)S(1)} %get-tuple-element.11, f32[128]{0:T(128)S(1)} %multiply_multiply_fusion, f32[512]{0:T(512)S(1)} %multiply_add_fusion), kind=kOutput, calls=%fused_computation.180 | convolution fusion | flops 134545408 | bytes 2099712 | tf_op jit(solution)/shard_map/dot_general | solution.py:120
  24.6 1.3 %fusion.125 = f32[128,1024]{1,0:T(8,128)S(1)} fusion(bf16[512,1024]{1,0:T(8,128)(2,1)S(1)} %copy-done.1, f32[128,1024]{1,0:T(8,128)S(1)} %get-tuple-element.8, f32[512]{0:T(512)S(1)} %multiply_add_fusion, f32[128]{0:T(128)S(1)} %multiply_multiply_fusion.7), kind=kOutput, calls=%fused_computation.173 | convolution fusion | flops 134545408 | bytes 2099712 | tf_op jit(solution)/shard_map/dot_general | solution.py:120
  25.9 1.8 %fusion.4 = bf16[1024,1024]{1,0:T(8,128)(2,1)S(1)} fusion(f32[128,1024]{1,0:T(8,128)S(1)} %fusion.125, bf16[512,1024]{1,0:T(8,128)(2,1)S(1)} %copy-done.2, f32[128,1024]{1,0:T(8,128)S(1)} %get-tuple-element.8, f32[512]{0:T(512)S(1)} %multiply_add_fusion, f32[128]{0:T(128)S(1)} %multiply_multiply_fusion.7), kind=kOutput, calls=%fused_computation.20 | convolution fusion | flops 134807552 | bytes 2361856 | tf_op jit(solution)/shard_map/dot_general | solution.py:120
  27.7 1.7 %fusion.6 = bf16[1024,1024]{1,0:T(8,128)(2,1)S(1)} fusion(bf16[1024,1024]{1,0:T(8,128)(2,1)S(1)} %fusion.4, f32[128,1024]{1,0:T(8,128)S(1)} %fusion.127, bf16[512,1024]{1,0:T(8,128)(2,1)S(1)} %copy-done.2, f32[128,1024]{1,0:T(8,128)S(1)} %get-tuple-element.16, f32[128]{0:T(128)S(1)} %get-tuple-element.20, f32[512]{0:T(512)S(1)} %multiply_add_fusion), kind=kOutput, calls=%fused_computation.22 | convolution fusion | flops 134807552 | bytes 2361856 | tf_op jit(solution)/shard_map/dot_general | solution.py:120
  29.4 1.3 %fusion.129 = f32[128,1024]{1,0:T(8,128)S(1)} fusion(bf16[512,1024]{1,0:T(8,128)(2,1)S(1)} %copy-done.1, f32[128,1024]{1,0:T(8,128)S(1)} %get-tuple-element.13, f32[128]{0:T(128)S(1)} %multiply_multiply_fusion.5, f32[512]{0:T(512)S(1)} %multiply_add_fusion), kind=kOutput, calls=%fused_computation.175 | convolution fusion | flops 134545408 | bytes 2099712 | tf_op jit(solution)/shard_map/dot_general | solution.py:120
  30.7 1.6 %fusion.8 = bf16[1024,1024]{1,0:T(8,128)(2,1)S(1)} fusion(bf16[1024,1024]{1,0:T(8,128)(2,1)S(1)} %fusion.6, f32[128,1024]{1,0:T(8,128)S(1)} %fusion.129, bf16[512,1024]{1,0:T(8,128)(2,1)S(1)} %copy-done.2, f32[128,1024]{1,0:T(8,128)S(1)} %get-tuple-element.13, f32[128]{0:T(128)S(1)} %multiply_multiply_fusion.5, f32[512]{0:T(512)S(1)} %multiply_add_fusion), kind=kOutput, calls=%fused_computation.24 | convolution fusion | flops 134807552 | bytes 2361856 | tf_op jit(solution)/shard_map/dot_general | solution.py:120
  32.3 1.6 %fusion.10 = bf16[1024,1024]{1,0:T(8,128)(2,1)S(1)} fusion(bf16[1024,1024]{1,0:T(8,128)(2,1)S(1)} %fusion.8, f32[128,1024]{1,0:T(8,128)S(1)} %fusion.131, bf16[512,1024]{1,0:T(8,128)(2,1)S(1)} %copy-done.2, f32[128,1024]{1,0:T(8,128)S(1)} %bitcast_convert_fusion, f32[128]{0:T(128)S(1)} %get-tuple-element.19, f32[512]{0:T(512)S(1)} %multiply_add_fusion), kind=kOutput, calls=%fused_computation.26 | convolution fusion | flops 134807552 | bytes 2361856 | tf_op jit(solution)/shard_map/dot_general | solution.py:120
  34.0 1.3 %fusion.133 = f32[128,1024]{1,0:T(8,128)S(1)} fusion(bf16[512,1024]{1,0:T(8,128)(2,1)S(1)} %copy-done.1, f32[128,1024]{1,0:T(8,128)S(1)} %get-tuple-element.14, f32[128]{0:T(128)S(1)} %get-tuple-element.18, f32[512]{0:T(512)S(1)} %multiply_add_fusion), kind=kOutput, calls=%fused_computation.177 | convolution fusion | flops 134545408 | bytes 2099712 | tf_op jit(solution)/shard_map/dot_general | solution.py:120
  35.2 1.6 %fusion.12 = bf16[1024,1024]{1,0:T(8,128)(2,1)S(1)} fusion(bf16[1024,1024]{1,0:T(8,128)(2,1)S(1)} %fusion.10, f32[128,1024]{1,0:T(8,128)S(1)} %fusion.133, bf16[512,1024]{1,0:T(8,128)(2,1)S(1)} %copy-done.2, f32[128,1024]{1,0:T(8,128)S(1)} %get-tuple-element.14, f32[128]{0:T(128)S(1)} %get-tuple-element.18, f32[512]{0:T(512)S(1)} %multiply_add_fusion), kind=kOutput, calls=%fused_computation.28 | convolution fusion | flops 134807552 | bytes 2361856 | tf_op jit(solution)/shard_map/dot_general | solution.py:120
  36.9 1.7 %fusion.14 = bf16[1024,1024]{1,0:T(8,128)(2,1)S(1)} fusion(bf16[1024,1024]{1,0:T(8,128)(2,1)S(1)} %fusion.12, f32[128,1024]{1,0:T(8,128)S(1)} %fusion.135, bf16[512,1024]{1,0:T(8,128)(2,1)S(1)} %copy-done.2, f32[128,1024]{1,0:T(8,128)S(1)} %get-tuple-element.15, f32[128]{0:T(128)S(1)} %get-tuple-element.17, f32[512]{0:T(512)S(1)} %multiply_add_fusion), kind=kOutput, calls=%fused_computation.30 | convolution fusion | flops 134807552 | bytes 2361856 | tf_op jit(solution)/shard_map/dot_general | solution.py:120
  38.5 1.3 %fusion.137 = f32[128,1024]{1,0:T(8,128)S(1)} fusion(bf16[512,1024]{1,0:T(8,128)(2,1)S(1)} %copy-done.1, f32[128,1024]{1,0:T(8,128)S(1)} %get-tuple-element.7, f32[128]{0:T(128)S(1)} %multiply_multiply_fusion.1, f32[512]{0:T(512)S(1)} %multiply_add_fusion), kind=kOutput, calls=%fused_computation.179 | convolution fusion | flops 134545408 | bytes 2099712 | tf_op jit(solution)/shard_map/dot_general | solution.py:120
  39.8 1.6 %fusion.16 = bf16[1024,1024]{1,0:T(8,128)(2,1)S(1)} fusion(bf16[1024,1024]{1,0:T(8,128)(2,1)S(1)} %fusion.14, f32[128,1024]{1,0:T(8,128)S(1)} %fusion.137, bf16[512,1024]{1,0:T(8,128)(2,1)S(1)} %copy-done.2, f32[128,1024]{1,0:T(8,128)S(1)} %get-tuple-element.7, f32[128]{0:T(128)S(1)} %multiply_multiply_fusion.1, f32[512]{0:T(512)S(1)} %multiply_add_fusion), kind=kOutput, calls=%fused_computation.32 | convolution fusion | flops 134807552 | bytes 2361856 | tf_op jit(solution)/shard_map/dot_general | solution.py:120
  41.5 1.7 %fusion.18 = bf16[1024,1024]{1,0:T(8,128)(2,1)S(1)} fusion(bf16[1024,1024]{1,0:T(8,128)(2,1)S(1)} %fusion.16, f32[128,1024]{1,0:T(8,128)S(1)} %fusion.139, bf16[512,1024]{1,0:T(8,128)(2,1)S(1)} %copy-done.2, f32[128,1024]{1,0:T(8,128)S(1)} %get-tuple-element.11, f32[128]{0:T(128)S(1)} %multiply_multiply_fusion, f32[512]{0:T(512)S(1)} %multiply_add_fusion), kind=kOutput, calls=%fused_computation.34 | convolution fusion | flops 134807552 | bytes 2361856 | tf_op jit(solution)/shard_map/dot_general | solution.py:120
  43.3 2.0 %copy-done.3 = bf16[2,2,512,1024]{3,2,1,0:T(8,128)(2,1)S(1)} copy-done((bf16[2,2,512,1024]{3,2,1,0:T(8,128)(2,1)S(1)}, bf16[2,2,512,1024]{3,2,1,0:T(8,128)(2,1)}, u32[]{:S(2)}) %copy-start.3) | copy-done | bytes 4194328
  48.4 12.6 %collective-permute-done.8 = bf16[256,1024]{1,0:T(8,128)(2,1)S(1)} collective-permute-done((bf16[256,1024]{1,0:T(8,128)(2,1)S(1)}, bf16[256,1024]{1,0:T(8,128)(2,1)S(1)}, u32[]{:S(2)}, u32[]{:S(2)}) %collective-permute-start.8) | collective-permute-done | bytes 524320 | tf_op jit(solution)/shard_map/ppermute | solution.py:135
  62.7 47.8 %all_to_all.5 = bf16[128,4,1152]{2,1,0:T(4,128)(2,1)S(1)} all-to-all(bf16[128,4,1152]{2,1,0:T(4,128)(2,1)S(1)} %reshape.128), channel_id=1, replica_groups=mesh['blk'=128,'map'=2] {'blk'}, dimensions={0} | all-to-all | bytes 2359296 | tf_op jit(solution)/shard_map/all_to_all | solution.py:158
  (51 shorter events, 14.0 us)
Async XLA Ops:
  0.0 110.9 %copy-start = (bf16[1,512,512]{2,1,0:T(8,128)(2,1)S(1)}, bf16[1,512,512]{2,1,0:T(8,128)(2,1)}, u32[]{:S(2)}) copy-start(bf16[1,512,512]{2,1,0:T(8,128)(2,1)} %param.10) | copy-start | bytes 1572868
  0.0 14.6 %copy-start.4 = (s32[1,1,256,1]{2,3,1,0:T(1,128)S(1)}, s32[1,1,256,1]{2,3,1,0:T(1,128)}, u32[]{:S(2)}) copy-start(s32[1,1,256,1]{2,3,1,0:T(1,128)} %param.11) | copy-start | bytes 3076
  0.0 14.9 %collective-permute-start = (bf16[128,1024]{1,0:T(8,128)(2,1)}, bf16[128,1024]{1,0:T(8,128)(2,1)}, u32[]{:S(2)}, u32[]{:S(2)}) collective-permute-start(bf16[128,1024]{1,0:T(8,128)(2,1)} %bitcast.49), channel_id=1, source_target_pairs={{0,8},{8,0},{16,24},{24,16},{32,40},{40,32},{48,56},{56,48},{64,72... | collective-permute-start | bytes 786440 | tf_op jit(solution)/shard_map/ppermute | solution.py:83
  1.6 13.3 %collective-permute-start.1 = (bf16[128,1024]{1,0:T(8,128)(2,1)}, bf16[128,1024]{1,0:T(8,128)(2,1)}, u32[]{:S(2)}, u32[]{:S(2)}) collective-permute-start(bf16[128,1024]{1,0:T(8,128)(2,1)} %bitcast.50), channel_id=1, source_target_pairs={{8,16},{16,8},{24,32},{32,24},{40,48},{48,40},{56,64},{64,56},{72,... | collective-permute-start | bytes 786440 | tf_op jit(solution)/shard_map/ppermute | solution.py:83
  3.3 14.0 %collective-permute-start.3 = (bf16[128,1024]{1,0:T(8,128)(2,1)}, bf16[128,1024]{1,0:T(8,128)(2,1)S(1)}, u32[]{:S(2)}, u32[]{:S(2)}) collective-permute-start(bf16[128,1024]{1,0:T(8,128)(2,1)} %bitcast.51), channel_id=1, source_target_pairs={{0,4},{4,0},{8,12},{12,8},{16,20},{20,16},{24,28},{28,24},{32,36},... | collective-permute-start | bytes 786440 | tf_op jit(solution)/shard_map/ppermute | solution.py:82
  6.3 13.5 %collective-permute-start.5 = (bf16[128,1024]{1,0:T(8,128)(2,1)}, bf16[128,1024]{1,0:T(8,128)(2,1)S(1)}, u32[]{:S(2)}, u32[]{:S(2)}) collective-permute-start(bf16[128,1024]{1,0:T(8,128)(2,1)} %bitcast.52), channel_id=1, source_target_pairs={{4,8},{8,4},{12,16},{16,12},{20,24},{24,20},{28,32},{32,28},{36,40... | collective-permute-start | bytes 786440 | tf_op jit(solution)/shard_map/ppermute | solution.py:82
  8.7 15.7 %collective-permute-start.7 = (bf16[128,1024]{1,0:T(8,128)(2,1)}, bf16[128,1024]{1,0:T(8,128)(2,1)S(1)}, u32[]{:S(2)}, u32[]{:S(2)}) collective-permute-start(bf16[128,1024]{1,0:T(8,128)(2,1)} %bitcast.53), channel_id=1, source_target_pairs={{0,2},{2,0},{4,6},{6,4},{8,10},{10,8},{12,14},{14,12},{16,18},{18,... | collective-permute-start | bytes 786440 | tf_op jit(solution)/shard_map/ppermute | solution.py:80
  12.0 7.9 %copy-start.1 = (bf16[512,1024]{1,0:T(8,128)(2,1)S(1)}, bf16[512,1024]{1,0:T(8,128)(2,1)}, u32[]{:S(2)}) copy-start(bf16[512,1024]{1,0:T(8,128)(2,1)} %constant.153) | copy-start | bytes 3145732
  16.0 8.4 %collective-permute-start.2 = (bf16[128,1024]{1,0:T(8,128)(2,1)S(1)}, bf16[128,1024]{1,0:T(8,128)(2,1)S(1)}, u32[]{:S(2)}, u32[]{:S(2)}) collective-permute-start(bf16[128,1024]{1,0:T(8,128)(2,1)S(1)} %get-tuple-element.12), channel_id=1, source_target_pairs={{0,2},{2,0},{4,6},{6,4},{8,10},{10,8},{12,14},{14,12},{16,18},{18,... | collective-permute-start | bytes 786440 | tf_op jit(solution)/shard_map/ppermute | solution.py:80
  22.5 1.9 %collective-permute-start.4 = (bf16[128,1024]{1,0:T(8,128)(2,1)S(1)}, bf16[128,1024]{1,0:T(8,128)(2,1)S(1)}, u32[]{:S(2)}, u32[]{:S(2)}) collective-permute-start(bf16[128,1024]{1,0:T(8,128)(2,1)S(1)} %collective-permute-done.3), channel_id=1, source_target_pairs={{0,2},{2,0},{4,6},{6,4},{8,10},{10,8},{12,14},{14,12},{16,18},{18,... | collective-permute-start | bytes 786440 | tf_op jit(solution)/shard_map/ppermute | solution.py:80
  22.6 1.9 %collective-permute-start.6 = (bf16[128,1024]{1,0:T(8,128)(2,1)S(1)}, bf16[128,1024]{1,0:T(8,128)(2,1)S(1)}, u32[]{:S(2)}, u32[]{:S(2)}) collective-permute-start(bf16[128,1024]{1,0:T(8,128)(2,1)S(1)} %collective-permute-done.5), channel_id=1, source_target_pairs={{0,2},{2,0},{4,6},{6,4},{8,10},{10,8},{12,14},{14,12},{16,18},{18,... | collective-permute-start | bytes 786440 | tf_op jit(solution)/shard_map/ppermute | solution.py:80
  24.4 1.5 %copy-start.2 = (bf16[512,1024]{1,0:T(8,128)(2,1)S(1)}, bf16[512,1024]{1,0:T(8,128)(2,1)}, u32[]{:S(2)}) copy-start(bf16[512,1024]{1,0:T(8,128)(2,1)} %constant.154) | copy-start | bytes 3145732
  43.1 2.2 %copy-start.3 = (bf16[2,2,512,1024]{3,2,1,0:T(8,128)(2,1)S(1)}, bf16[2,2,512,1024]{3,2,1,0:T(8,128)(2,1)}, u32[]{:S(2)}) copy-start(bf16[2,2,512,1024]{3,2,1,0:T(8,128)(2,1)} %constant.147.clone) | copy-start | bytes 12582916
  46.7 14.3 %collective-permute-start.8 = (bf16[256,1024]{1,0:T(8,128)(2,1)S(1)}, bf16[256,1024]{1,0:T(8,128)(2,1)S(1)}, u32[]{:S(2)}, u32[]{:S(2)}) collective-permute-start(bf16[256,1024]{1,0:T(8,128)(2,1)S(1)} %fusion.1), channel_id=1, source_target_pairs={{0,1},{1,0},{2,3},{3,2},{4,5},{5,4},{6,7},{7,6},{8,9},{9,8},{10,11... | collective-permute-start | bytes 1572872 | tf_op jit(solution)/shard_map/ppermute | solution.py:135

commit v2 on v1

v2 whole, which is shorter than its diff:
```python
import functools
import math

import jax
import jax.numpy as jnp
import ml_dtypes
import numpy as np
from jax import lax
from jax.experimental import pallas as pl
from jax.experimental.pallas import tpu as pltpu
from jax.sharding import PartitionSpec as P

STOPS = 8
MAPH = 256
SIDE = 128


def matching(count, distance, parity):
    seen, pairs = set(), []
    for start in range(count):
        cycle, at = [], start
        while at not in seen:
            seen.add(at)
            cycle.append(at)
            at = (at + distance) % count
        for place in range(parity, len(cycle) + parity, 2) if cycle else ():
            a, b = cycle[place % len(cycle)], cycle[(place + 1) % len(cycle)]
            pairs += [(a, b), (b, a)]
    return pairs


def range_table(freq_count):
    index = np.arange(freq_count, dtype=np.int64)
    angle = (index[:, None] * index[None, :] % freq_count).astype(np.float32) * np.float32(
        2.0 * math.pi / freq_count
    )
    factor = np.float32(1.0 / math.sqrt(freq_count))
    real_part, imag_part = np.cos(angle) * factor, -np.sin(angle) * factor
    table = np.block([[real_part, imag_part], [-imag_part, real_part]])
    return table.astype(ml_dtypes.bfloat16)


def stop_order(core):
    return [1, 2, 3, 4, 5, 6 - 6 * core, 6 * core, 7]


def cross_table(map_count, row_count, pulse_count):
    span = STOPS * map_count * pulse_count
    rows = np.arange(row_count, dtype=np.int64)[:, None]
    factor = np.float32(1.0 / math.sqrt(span))
    tables = []
    for m in range(map_count):
        for core in range(2):
            parts = []
            for k in stop_order(core):
                along = (k * map_count + m) * pulse_count + np.arange(pulse_count)
                angle = (rows * along[None, :] % span).astype(np.float32) * np.float32(
                    2.0 * math.pi / span
                )
                parts += [np.cos(angle) * factor, -np.sin(angle) * factor]
            tables.append(np.concatenate(parts, axis=1))
    return np.stack(tables).astype(ml_dtypes.bfloat16)


def call(kernel, outs, operands, scratch=(), flops=0, limit=24):
    specs = [pl.BlockSpec(memory_space=pltpu.SMEM)] + [
        pl.BlockSpec(memory_space=pltpu.VMEM) for _ in operands[1:]
    ]
    size = sum(math.prod(a.shape) * a.dtype.itemsize for a in [*operands, *outs])
    return pl.pallas_call(
        kernel,
        out_shape=outs,
        in_specs=specs,
        out_specs=[pl.BlockSpec(memory_space=pltpu.VMEM) for _ in outs],
        scratch_shapes=list(scratch),
        compiler_params=pltpu.CompilerParams(vmem_limit_bytes=limit * 2**20),
        cost_estimate=pl.CostEstimate(flops=flops, bytes_accessed=size, transcendentals=0),
    )(*operands)


def phase_kernel(map_count, span, facts, curvature, cos_early, sin_early, cos_late, sin_late):
    early, pulses, freqs = cos_early.shape
    width = freqs // 4
    pulse = lax.broadcasted_iota(jnp.int32, (pulses, width), 0)
    fine = lax.broadcasted_iota(jnp.int32, (pulses, width), 1).astype(jnp.float32) / freqs
    core, here_map = facts[0], facts[3]
    for place in range(STOPS):
        stop = {5: 6 - 6 * core, 6: 6 * core}.get(place, place if place == 7 else place + 1)
        along = ((stop * map_count + here_map) * pulses + pulse).astype(jnp.float32) / span - 0.5
        angle = curvature[0] * (along * along)
        low_c, low_s = jnp.cos(angle * fine), jnp.sin(angle * fine)
        step_c, step_s = jnp.cos(angle * 0.25), jnp.sin(angle * 0.25)
        now_c = step_c * low_c - step_s * low_s
        now_s = step_s * low_c + step_c * low_s
        for h in range(4):
            now_c, now_s = step_c * now_c - step_s * now_s, step_s * now_c + step_c * now_s
            columns = slice(h * width, (h + 1) * width)
            if place < early:
                cos_early[place, :, columns] = now_c
                sin_early[place, :, columns] = now_s
            else:
                cos_late[place - early, :, columns] = now_c
                sin_late[place - early, :, columns] = now_s


def transform(blocks, cosines, sines, ranges, phased, right_side):
    freqs = cosines.shape[2]
    pulses = cosines.shape[1]
    for place, block in enumerate(blocks):
        values = block().astype(jnp.float32)
        real_part, imag_part = values[:, :freqs], values[:, freqs:]
        cosine, sine = cosines[place], sines[place]
        rows = slice(place * pulses, (place + 1) * pulses)
        phased[rows, :freqs] = (real_part * cosine - imag_part * sine).astype(jnp.bfloat16)
        phased[rows, freqs:] = (real_part * sine + imag_part * cosine).astype(jnp.bfloat16)
    for half in range(2):
        columns = slice(half * freqs, (half + 1) * freqs)
        spectrum = jnp.dot(
            phased[...], ranges[:, columns], preferred_element_type=jnp.float32
        ).astype(jnp.bfloat16)
        for place in range(len(blocks)):
            piece = spectrum[place * pulses : (place + 1) * pulses]
            top = 2 * place * pulses
            right_side[top : top + pulses, columns] = piece
            other = slice((1 - half) * freqs, (2 - half) * freqs)
            right_side[top + pulses : top + 2 * pulses, other] = piece if half == 0 else -piece


def early_kernel(
    facts, own, near_a, near_b, twin, twin_a, twin_b, cosines, sines, ranges, cross, total,
    phased, right_side,
):
    core, chip_odd = facts[0] == 1, facts[1] == 1
    up = lambda: jnp.where(chip_odd, near_b[...], near_a[...])
    down = lambda: jnp.where(chip_odd, near_a[...], near_b[...])
    twin_up = lambda: jnp.where(chip_odd, twin_b[...], twin_a[...])
    twin_down = lambda: jnp.where(chip_odd, twin_a[...], twin_b[...])
    blocks = [
        down,
        lambda: jnp.where(core, twin[...], twin_down()),
        lambda: own[...],
        lambda: jnp.where(core, twin_up(), twin[...]),
        up,
        lambda: jnp.where(core, twin_down(), twin_up()),
    ]
    transform(blocks, cosines, sines, ranges, phased, right_side)
    total[...] = jnp.dot(cross[...], right_side[...], preferred_element_type=jnp.float32)


def late_kernel(
    facts, far_a, far_b, twin_far, cosines, sines, ranges, cross, total, sent, kept,
    phased, right_side,
):
    group_odd, here_map = facts[2] == 1, facts[3]
    blocks = [lambda: twin_far[...], lambda: jnp.where(group_odd, far_b[...], far_a[...])]
    transform(blocks, cosines, sines, ranges, phased, right_side)
    rows = sent.shape[0]
    for out, part in ((sent, 1 - here_map), (kept, here_map)):
        place = pl.ds(pl.multiple_of(part * rows, rows), rows)
        out[...] = (
            total[place, :]
            + jnp.dot(cross[place, :], right_side[...], preferred_element_type=jnp.float32)
        ).astype(out.dtype)


def pack_kernel(facts, kept, arrived, slot_hot, side, packed):
    width = kept.shape[1]
    image = (kept[...] + arrived[...].astype(jnp.float32)).astype(jnp.bfloat16)
    packed[:, :width] = jnp.dot(
        slot_hot[...], image, preferred_element_type=jnp.float32
    ).astype(packed.dtype)
    packed[:, width:] = jnp.dot(
        slot_hot[...], side[...], preferred_element_type=jnp.float32
    ).astype(packed.dtype)


def swap(block, count):
    return lax.ppermute(block, "blk", [(i, i ^ 1) for i in range(count)])


def body(ranges, crosses, phase_history, tile_curvature, interp_weights, strip_tiles, row_offsets, tile_owner):
    blk_count = lax.axis_size("blk")
    map_count = lax.axis_size("map")
    here_blk = lax.axis_index("blk")
    here_map = lax.axis_index("map")
    own_block = phase_history[0, 0]
    pulse_count = own_block.shape[0]
    freq_count = own_block.shape[1] // 2
    columns = interp_weights.shape[2]
    rows_here = strip_tiles.shape[2]

    core, chip_odd, group_odd = here_blk % 2, (here_blk // 2) % 2, (here_blk // 4) % 2
    facts = jnp.stack([core, chip_odd, group_odd, here_map]).astype(jnp.int32)

    near = [lax.ppermute(own_block, "blk", matching(blk_count, 2, p)) for p in (0, 1)]
    far = [lax.ppermute(own_block, "blk", matching(blk_count, 4, p)) for p in (0, 1)]
    twin = swap(own_block, blk_count)
    twin_near = [swap(block, blk_count) for block in near]
    twin_far = swap(jnp.where(core == group_odd, far[0], far[1]), blk_count)

    cross = lax.dynamic_index_in_dim(crosses, here_map * 2 + core, 0, keepdims=False)
    early, late = STOPS - 2, 2
    deep = 2 * pulse_count
    f32 = lambda *shape: jax.ShapeDtypeStruct(shape, jnp.float32)
    b16 = lambda *shape: jax.ShapeDtypeStruct(shape, jnp.bfloat16)
    curves = pl.pallas_call(
        functools.partial(phase_kernel, map_count, STOPS * map_count * pulse_count),
        out_shape=[f32(n, pulse_count, freq_count) for n in (early, early, late, late)],
        in_specs=[pl.BlockSpec(memory_space=pltpu.SMEM)] * 2,
        out_specs=[pl.BlockSpec(memory_space=pltpu.VMEM)] * 4,
        compiler_params=pltpu.CompilerParams(vmem_limit_bytes=16 * 2**20),
        cost_estimate=pl.CostEstimate(flops=2**22, bytes_accessed=2**22, transcendentals=2**19),
    )(facts, tile_curvature)
    work = lambda n: [
        pltpu.VMEM((n * pulse_count, 2 * freq_count), jnp.bfloat16),
        pltpu.VMEM((n * deep, 2 * columns), jnp.bfloat16),
    ]
    macs = lambda n: n * pulse_count * 4 * columns * (freq_count + map_count * rows_here)
    [total] = call(
        early_kernel,
        [f32(map_count * rows_here, 2 * columns)],
        [facts, own_block, *near, twin, *twin_near, *curves[:2], ranges, cross[:, : early * deep]],
        work(early),
        2 * macs(early),
    )
    sent, kept = call(
        late_kernel,
        [b16(rows_here, 2 * columns), f32(rows_here, 2 * columns)],
        [facts, *far, twin_far, *curves[2:], ranges, cross[:, early * deep :], total],
        work(late),
        2 * macs(late),
    )
    arrived = lax.ppermute(sent, "map", [(0, 1), (1, 0)])

    capacity = max(2, 2 * rows_here // blk_count)
    holder_index = jnp.arange(blk_count, dtype=jnp.int32)
    row_tiles = strip_tiles[0, 0, :, 0]
    own_offsets = row_offsets[0, 0]
    tile_match = row_tiles[:, None] == holder_index[None, :]
    destination = jnp.sum(jnp.where(tile_match, tile_owner[None, :], 0), axis=1)
    row_number = jnp.arange(rows_here, dtype=jnp.int32)
    same_before = (row_tiles[:, None] == row_tiles[None, :]) & (
        row_number[None, :] < row_number[:, None]
    )
    rank_within = jnp.sum(same_before.astype(jnp.int32), axis=1)
    slot_index = destination * capacity + rank_within
    slot_hot = (
        jnp.arange(blk_count * capacity, dtype=jnp.int32)[:, None] == slot_index[None, :]
    ).astype(jnp.bfloat16)
    side = jnp.broadcast_to(own_offsets.astype(jnp.bfloat16)[:, None], (rows_here, SIDE))
    [packed] = call(
        pack_kernel,
        [b16(blk_count * capacity, 2 * columns + SIDE)],
        [facts, kept, arrived, slot_hot, side],
        (),
        2 * blk_count * capacity * rows_here * (2 * columns + SIDE),
    )
    packed = packed.reshape(blk_count, capacity, 2 * columns + SIDE)
    got = lax.all_to_all(packed, "blk", split_axis=0, concat_axis=0, tiled=True)
    got = got.reshape(blk_count * capacity, 2 * columns + SIDE)

    weights = interp_weights[0]
    real_out = jnp.dot(got[:, :columns], weights, preferred_element_type=jnp.float32)
    imag_out = jnp.dot(got[:, columns : 2 * columns], weights, preferred_element_type=jnp.float32)
    power = real_out * real_out + imag_out * imag_out
    offsets = got[:, 2 * columns].astype(jnp.int32)
    place_hot = (jnp.arange(MAPH, dtype=jnp.int32)[:, None] == offsets[None, :]).astype(
        jnp.bfloat16
    )
    high = power.astype(jnp.bfloat16)
    rest = power - high.astype(jnp.float32)
    middle = rest.astype(jnp.bfloat16)
    low = (rest - middle.astype(jnp.float32)).astype(jnp.bfloat16)
    tile_map = sum(
        jnp.dot(place_hot, piece, preferred_element_type=jnp.float32)
        for piece in (low, middle, high)
    )
    return tile_map.reshape(1, 1, MAPH, columns)


def solution(mesh):
    in_specs = (
        P("blk", "map", None, None),
        P("blk"),
        P("blk", None, None),
        P("blk", "map", None, None),
        P("blk", "map", None),
        P(),
    )
    out_specs = P("blk", "map", None, None)

    def run(*args):
        map_count, pulse_count, width = args[0].shape[1:]
        ranges = jnp.asarray(range_table(width // 2))
        crosses = jnp.asarray(
            cross_table(map_count, map_count * args[3].shape[2], pulse_count)
        )
        held = lambda *here: body(ranges, crosses, *here)
        return jax.shard_map(
            held, mesh=mesh, in_specs=in_specs, out_specs=out_specs, check_vma=False
        )(*args)

    return run
```

time: 114 us -> 104 us (0.912)
  matrix products: 30.8 us -> 3.65 us
  Pallas kernels: 0 us -> 12 us
  local copies, waits for them, and re-layouts: 2.76 us -> 7.56 us
  waiting for transfers between devices: 16 us -> 20.7 us
  other arithmetic: 4.42 us -> 0.71 us
    dot_general x21 -> x0, matrix products: 28.2 us -> none  [the longest x16 24.8 us: body(): jnp.dot(p, ranges, preferred_element_type=jnp.float32).astype(jnp.bfloat16)]
    pallas_call x0 -> x4, Pallas kernels: none -> 12 us  [the longest x3 7.03 us: call(): pl.pallas_call(kernel, out_shape=outs, in_specs=specs, out_specs=[pl.Bloc...]
    ppermute x8, waiting for transfers between devices: 3.35 us -> 7.53 us  [the longest x2 7.52 us: body(): lax.ppermute(own_block, 'blk', matching(blk_count, 2, p))]
    squeeze x0 -> x1, local copies, waits for them, and re-layouts: none -> 3.22 us  [body(): lax.dynamic_index_in_dim(crosses, here_map * 2 + core, 0, keepdims=False)]
    slice x0 -> x2, local copies, waits for them, and re-layouts: none -> 2.74 us  [the longest x1 1.66 us: body(): cross[:, :early * deep]]
    convert_element_type x4 -> x1, other arithmetic: 2.32 us -> 0.07 us  [body(): slot_hot = (jnp.arange(blk_count * capacity, dtype=jnp.int32)[:, None] ==...]
    unnamed x10 -> x14, local copies, waits for them, and re-layouts: 2.06 us -> 0.9 us
  transfers between devices with their start and end apart: 9 -> 9, of which waited for: 4 -> 3; matrix products, arithmetic and copies ran while one was open for 10% -> 6% of each run, Pallas kernels for 0% -> 9%
where the time goes in v2:
time: 104 us; the launch traced here: 103 us
  blocking collectives  47.7 us (46%)
  waiting for transfers between devices  20.7 us (20%)
  Pallas kernels  12 us (12%)
  starting transfers between devices  10.1 us (10%)
  local copies, waits for them, and re-layouts  7.56 us (7%)
  matrix products  3.65 us (4%)
    all_to_all x1, blocking collectives, body(): got = lax.all_to_all(packed, 'blk', split_axis=0, concat_axis=0, tiled=True)  47.7 us
    ppermute x1, waiting for transfers between devices, body(): arrived = lax.ppermute(sent, 'map', [(0, 1), (1, 0)])  13.2 us
    ppermute x2, waiting for transfers between devices, body(): lax.ppermute(own_block, 'blk', matching(blk_count, 2, p))  7.52 us
    pallas_call x3, Pallas kernels, call(): pl.pallas_call(kernel, out_shape=outs, in_specs=specs, out_specs=[pl.Bloc...  7.03 us
    ppermute x2, starting transfers between devices, body(): lax.ppermute(own_block, 'blk', matching(blk_count, 2, p))  5.38 us
    pallas_call x1, Pallas kernels, body(): pl.pallas_call(functools.partial(phase_kernel, map_count, STOPS * map_cou...  5 us
    ppermute x2, starting transfers between devices, body(): lax.ppermute(own_block, 'blk', matching(blk_count, 4, p))  3.3 us
    squeeze x1, local copies, waits for them, and re-layouts, body(): lax.dynamic_index_in_dim(crosses, here_map * 2 + core, 0, keepdims=False)  3.22 us
  transfers between devices with their start and end apart: 9, of which 3 were waited for; matrix products, arithmetic and copies ran while one was open for 6% of the time, Pallas kernels for 9%

profile of v2, /device:TPU:32, one launch (start us, length us, event | category | flops | bytes accessed | tf_op | source)
XLA Modules:
  0.0 103.4 jit_solution(3468862935250343782)
XLA Ops:
  0.0 1.6 %collective-permute-start = (bf16[128,1024]{1,0:T(8,128)(2,1)}, bf16[128,1024]{1,0:T(8,128)(2,1)S(1)}, u32[]{:S(2)}, u32[]{:S(2)}) collective-permute-start(bf16[128,1024]{1,0:T(8,128)(2,1)} %bitcast.15), channel_id=1, source_target_pairs={{0,8},{8,0},{16,24},{24,16},{32,40},{40,32},{48,56},{56,48},{64,72... | collective-permute-start | bytes 786440 | tf_op jit(solution)/shard_map/ppermute | solution.py:196
  1.6 1.7 %collective-permute-start.1 = (bf16[128,1024]{1,0:T(8,128)(2,1)}, bf16[128,1024]{1,0:T(8,128)(2,1)S(1)}, u32[]{:S(2)}, u32[]{:S(2)}) collective-permute-start(bf16[128,1024]{1,0:T(8,128)(2,1)} %bitcast.16), channel_id=1, source_target_pairs={{8,16},{16,8},{24,32},{32,24},{40,48},{48,40},{56,64},{64,56},{72,... | collective-permute-start | bytes 786440 | tf_op jit(solution)/shard_map/ppermute | solution.py:196
  3.3 3.0 %collective-permute-start.3 = (bf16[128,1024]{1,0:T(8,128)(2,1)}, bf16[128,1024]{1,0:T(8,128)(2,1)S(1)}, u32[]{:S(2)}, u32[]{:S(2)}) collective-permute-start(bf16[128,1024]{1,0:T(8,128)(2,1)} %bitcast.17), channel_id=1, source_target_pairs={{0,4},{4,0},{8,12},{12,8},{16,20},{20,16},{24,28},{28,24},{32,36},... | collective-permute-start | bytes 786440 | tf_op jit(solution)/shard_map/ppermute | solution.py:195
  6.3 2.4 %collective-permute-start.4 = (bf16[128,1024]{1,0:T(8,128)(2,1)}, bf16[128,1024]{1,0:T(8,128)(2,1)S(1)}, u32[]{:S(2)}, u32[]{:S(2)}) collective-permute-start(bf16[128,1024]{1,0:T(8,128)(2,1)} %bitcast.18), channel_id=1, source_target_pairs={{4,8},{8,4},{12,16},{16,12},{20,24},{24,20},{28,32},{32,28},{36,40... | collective-permute-start | bytes 786440 | tf_op jit(solution)/shard_map/ppermute | solution.py:195
  8.7 3.2 %dynamic-slice_bitcast_fusion = bf16[512,2048]{1,0:T(8,128)(2,1)} fusion(bf16[4,512,2048]{2,1,0:T(8,128)(2,1)} %constant.61.clone, s32[]{:T(128)S(6)} %select_n.45), kind=kLoop, calls=%fused_computation | loop fusion | bytes 4194308 | tf_op jit(solution)/shard_map/jit(dynamic_index_in_dim)/squeeze | solution.py:201
  12.3 4.9 %collective-permute-done.3.near_a = bf16[128,1024]{1,0:T(8,128)(2,1)S(1)} collective-permute-done((bf16[128,1024]{1,0:T(8,128)(2,1)}, bf16[128,1024]{1,0:T(8,128)(2,1)S(1)}, u32[]{:S(2)}, u32[]{:S(2)}) %collective-permute-start.3) | collective-permute-done | bytes 262176 | tf_op jit(solution)/shard_map/ppermute | solution.py:195
  17.3 2.6 %collective-permute-done.4.near_b = bf16[128,1024]{1,0:T(8,128)(2,1)S(1)} collective-permute-done((bf16[128,1024]{1,0:T(8,128)(2,1)}, bf16[128,1024]{1,0:T(8,128)(2,1)S(1)}, u32[]{:S(2)}, u32[]{:S(2)}) %collective-permute-start.4) | collective-permute-done | bytes 262176 | tf_op jit(solution)/shard_map/ppermute | solution.py:195
  19.9 1.1 %slice.20.cross = bf16[512,512]{1,0:T(8,128)(2,1)S(1)} slice(bf16[512,2048]{1,0:T(8,128)(2,1)} %dynamic-slice_bitcast_fusion), slice={[0:512], [1536:2048]} | slice | bytes 1048576 | tf_op jit(solution)/shard_map/slice | solution.py:229
  21.0 1.7 %slice.21.cross = bf16[512,1536]{1,0:T(8,128)(2,1)S(1)} slice(bf16[512,2048]{1,0:T(8,128)(2,1)} %dynamic-slice_bitcast_fusion), slice={[0:512], [0:1536]} | slice | bytes 3145728 | tf_op jit(solution)/shard_map/slice | solution.py:222
  23.4 5.0 %shard_map.82 = (f32[6,128,512]{2,1,0:T(8,128)S(1)}, f32[6,128,512]{2,1,0:T(8,128)S(1)}, f32[2,128,512]{2,1,0:T(8,128)S(1)}, f32[2,128,512]{2,1,0:T(8,128)S(1)}) custom-call(s32[4]{0:T(128)S(1)} %pad_add_fusion.facts, f32[1]{0:T(128)S(6)} %copy.10.curvature), custom_call_target="tpu_custom_call" | custom-call | flops 4194304 | bytes 4194304 | tf_op jit(solution)/shard_map/pallas_call | solution.py:206
  28.4 0.8 collective-permute-start.2
  29.3 4.1 %shard_map.83.total = f32[512,1024]{1,0:T(8,128)S(1)} custom-call(s32[4]{0:T(128)S(1)} %pad_add_fusion.facts, bf16[128,1024]{1,0:T(8,128)(2,1)S(1)} %bitcast.20, bf16[128,1024]{1,0:T(8,128)(2,1)S(1)} %collective-permute-done.3.near_a, bf16[128,1024]{1,0:T(8,128)(2,1)S(1)} %collective-permute-done.4.near_b, ...), custom_call_target="tpu_custom_call" | custom-call | flops 3221225472 | bytes 10485776 | tf_op jit(solution)/shard_map/pallas_call | solution.py:70
  33.3 1.9 %shard_map.84 = (bf16[256,1024]{1,0:T(8,128)(2,1)S(1)}, f32[256,1024]{1,0:T(8,128)S(1)}) custom-call(s32[4]{0:T(128)S(1)} %pad_add_fusion.facts, bf16[128,1024]{1,0:T(8,128)(2,1)S(1)} %collective-permute-done.far_a, bf16[128,1024]{1,0:T(8,128)(2,1)S(1)} %collective-permute-done.1.far_b, bf16[128,1024]{1,0:T(8,128)(2,1)S(1)} %collective-permute-done.2.twin_far, ...), custom_call_target="tpu_custom_call" | custom-call | flops 1073741824 | bytes 8126480 | tf_op jit(solution)/shard_map/pallas_call | solution.py:70
  35.3 0.7 collective-permute-start.8
  36.0 13.2 %collective-permute-done.8.arrived = bf16[256,1024]{1,0:T(8,128)(2,1)S(1)} collective-permute-done((bf16[256,1024]{1,0:T(8,128)(2,1)S(1)}, bf16[256,1024]{1,0:T(8,128)(2,1)S(1)}, u32[]{:S(2)}, u32[]{:S(2)}) %collective-permute-start.8) | collective-permute-done | bytes 524320 | tf_op jit(solution)/shard_map/ppermute | solution.py:233
  49.3 1.1 %shard_map.85 = bf16[512,1152]{1,0:T(8,128)(2,1)S(1)} custom-call(s32[4]{0:T(128)S(1)} %pad_add_fusion.facts, f32[256,1024]{1,0:T(8,128)S(1)} %get-tuple-element.15.kept, bf16[256,1024]{1,0:T(8,128)(2,1)S(1)} %collective-permute-done.8.arrived, bf16[512,256]{1,0:T(8,128)(2,1)S(1)} %fusion.10.slot_hot, bf16[256,128]{1,0:T(8,128)(2,1)S(1)} %broadcast_in_dim.16.side), custom_call_target="tpu_custom_call" | custom-call | flops 301989888 | bytes 3080208 | tf_op jit(solution)/shard_map/pallas_call | solution.py:70
  50.4 0.3 reshape.31
  50.7 47.7 %all_to_all.5 = bf16[128,4,1152]{2,1,0:T(4,128)(2,1)S(1)} all-to-all(bf16[128,4,1152]{2,1,0:T(4,128)(2,1)S(1)} %reshape.31), channel_id=1, replica_groups=mesh['blk'=128,'map'=2] {'blk'}, dimensions={0} | all-to-all | bytes 2359296 | tf_op jit(solution)/shard_map/all_to_all | solution.py:259
  98.9 0.9 copy-done.3
  99.8 0.4 convolution_multiply_fusion
  100.2 1.5 %fusion = f32[512,512]{1,0:T(8,128)S(1)} fusion(f32[512,512]{1,0:T(8,128)S(1)} %convolution_multiply_fusion, bf16[512,1152]{1,0:T(8,128)(2,1)} %copy-done.3, bf16[1,512,512]{2,1,0:T(8,128)(2,1)S(1)} %copy-done), kind=kOutput, calls=%fused_computation.3 | convolution fusion | flops 268959744 | bytes 3145728 | tf_op jit(solution)/shard_map/dot_general | solution.py:263
  101.7 0.3 fusion.5
  102.0 0.3 convolution_add_fusion.1
  102.3 1.1 %fusion.1 = f32[1,1,256,512]{3,2,1,0:T(8,128)} fusion(f32[256,512]{1,0:T(8,128)S(1)} %convolution_add_fusion.1, f32[512,512]{1,0:T(8,128)S(1)} %fusion, s32[512]{0:T(512)S(1)} %convert_reduce_fusion), kind=kOutput, calls=%fused_computation.5 | convolution fusion | flops 134742016 | bytes 2099200 | tf_op jit(solution)/shard_map/dot_general | solution.py:275
  (32 shorter events, 1.1 us)
Async XLA Ops:
  0.0 99.8 %copy-start = (bf16[1,512,512]{2,1,0:T(8,128)(2,1)S(1)}, bf16[1,512,512]{2,1,0:T(8,128)(2,1)}, u32[]{:S(2)}) copy-start(bf16[1,512,512]{2,1,0:T(8,128)(2,1)} %param.10) | copy-start | bytes 1572868
  0.0 28.4 %collective-permute-start = (bf16[128,1024]{1,0:T(8,128)(2,1)}, bf16[128,1024]{1,0:T(8,128)(2,1)S(1)}, u32[]{:S(2)}, u32[]{:S(2)}) collective-permute-start(bf16[128,1024]{1,0:T(8,128)(2,1)} %bitcast.15), channel_id=1, source_target_pairs={{0,8},{8,0},{16,24},{24,16},{32,40},{40,32},{48,56},{56,48},{64,72... | collective-permute-start | bytes 786440 | tf_op jit(solution)/shard_map/ppermute | solution.py:196
  1.6 26.8 %collective-permute-start.1 = (bf16[128,1024]{1,0:T(8,128)(2,1)}, bf16[128,1024]{1,0:T(8,128)(2,1)S(1)}, u32[]{:S(2)}, u32[]{:S(2)}) collective-permute-start(bf16[128,1024]{1,0:T(8,128)(2,1)} %bitcast.16), channel_id=1, source_target_pairs={{8,16},{16,8},{24,32},{32,24},{40,48},{48,40},{56,64},{64,56},{72,... | collective-permute-start | bytes 786440 | tf_op jit(solution)/shard_map/ppermute | solution.py:196
  3.3 14.0 %collective-permute-start.3 = (bf16[128,1024]{1,0:T(8,128)(2,1)}, bf16[128,1024]{1,0:T(8,128)(2,1)S(1)}, u32[]{:S(2)}, u32[]{:S(2)}) collective-permute-start(bf16[128,1024]{1,0:T(8,128)(2,1)} %bitcast.17), channel_id=1, source_target_pairs={{0,4},{4,0},{8,12},{12,8},{16,20},{20,16},{24,28},{28,24},{32,36},... | collective-permute-start | bytes 786440 | tf_op jit(solution)/shard_map/ppermute | solution.py:195
  6.3 13.5 %collective-permute-start.4 = (bf16[128,1024]{1,0:T(8,128)(2,1)}, bf16[128,1024]{1,0:T(8,128)(2,1)S(1)}, u32[]{:S(2)}, u32[]{:S(2)}) collective-permute-start(bf16[128,1024]{1,0:T(8,128)(2,1)} %bitcast.18), channel_id=1, source_target_pairs={{4,8},{8,4},{12,16},{16,12},{20,24},{24,20},{28,32},{32,28},{36,40... | collective-permute-start | bytes 786440 | tf_op jit(solution)/shard_map/ppermute | solution.py:195
  8.7 20.5 %collective-permute-start.5 = (bf16[128,1024]{1,0:T(8,128)(2,1)}, bf16[128,1024]{1,0:T(8,128)(2,1)S(1)}, u32[]{:S(2)}, u32[]{:S(2)}) collective-permute-start(bf16[128,1024]{1,0:T(8,128)(2,1)} %bitcast.19), channel_id=1, source_target_pairs={{0,2},{2,0},{4,6},{6,4},{8,10},{10,8},{12,14},{14,12},{16,18},{18,... | collective-permute-start | bytes 786440 | tf_op jit(solution)/shard_map/ppermute | solution.py:178
  8.7 3.2 %copy-start.4 = (s32[1,1,256,1]{2,3,1,0:T(1,128)S(1)}, s32[1,1,256,1]{2,3,1,0:T(1,128)}, u32[]{:S(2)}) copy-start(s32[1,1,256,1]{2,3,1,0:T(1,128)} %param.11) | copy-start | bytes 3076
  8.7 3.2 %copy-start.5 = (s32[128]{0:T(128)S(1)}, s32[128]{0:T(128)}, u32[]{:S(2)}) copy-start(s32[128]{0:T(128)} %param.13) | copy-start | bytes 1540
  17.3 12.0 %collective-permute-start.6 = (bf16[128,1024]{1,0:T(8,128)(2,1)S(1)}, bf16[128,1024]{1,0:T(8,128)(2,1)S(1)}, u32[]{:S(2)}, u32[]{:S(2)}) collective-permute-start(bf16[128,1024]{1,0:T(8,128)(2,1)S(1)} %collective-permute-done.3.near_a), channel_id=1, source_target_pairs={{0,2},{2,0},{4,6},{6,4},{8,10},{10,8},{12,14},{14,12},{16,18},{18,... | collective-permute-start | bytes 786440 | tf_op jit(solution)/shard_map/ppermute | solution.py:178
  19.8 9.4 %collective-permute-start.7 = (bf16[128,1024]{1,0:T(8,128)(2,1)S(1)}, bf16[128,1024]{1,0:T(8,128)(2,1)S(1)}, u32[]{:S(2)}, u32[]{:S(2)}) collective-permute-start(bf16[128,1024]{1,0:T(8,128)(2,1)S(1)} %collective-permute-done.4.near_b), channel_id=1, source_target_pairs={{0,2},{2,0},{4,6},{6,4},{8,10},{10,8},{12,14},{14,12},{16,18},{18,... | collective-permute-start | bytes 786440 | tf_op jit(solution)/shard_map/ppermute | solution.py:178
  21.0 8.2 %copy-start.1 = (bf16[1024,1024]{1,0:T(8,128)(2,1)S(1)}, bf16[1024,1024]{1,0:T(8,128)(2,1)}, u32[]{:S(2)}) copy-start(bf16[1024,1024]{1,0:T(8,128)(2,1)} %constant.62.clone.ranges) | copy-start | bytes 6291460
  22.7 6.6 %copy-start.2 = (bf16[1,1,128,1024]{3,2,1,0:T(8,128)(2,1)S(1)}, bf16[1,1,128,1024]{3,2,1,0:T(8,128)(2,1)}, u32[]{:S(2)}) copy-start(bf16[1,1,128,1024]{3,2,1,0:T(8,128)(2,1)} %param.8) | copy-start | bytes 786436
  28.4 4.9 %collective-permute-start.2 = (bf16[128,1024]{1,0:T(8,128)(2,1)S(1)}, bf16[128,1024]{1,0:T(8,128)(2,1)S(1)}, u32[]{:S(2)}, u32[]{:S(2)}) collective-permute-start(bf16[128,1024]{1,0:T(8,128)(2,1)S(1)} %broadcast_select_fusion), channel_id=1, source_target_pairs={{0,2},{2,0},{4,6},{6,4},{8,10},{10,8},{12,14},{14,12},{16,18},{18,... | collective-permute-start | bytes 786440 | tf_op jit(solution)/shard_map/ppermute | solution.py:178
  33.3 2.6 %copy-start.6 = (s32[1,1,256]{2,1,0:T(1,128)S(1)}, s32[1,1,256]{2,1,0:T(1,128)}, u32[]{:S(2)}) copy-start(s32[1,1,256]{2,1,0:T(1,128)} %param.12) | copy-start | bytes 3076
  35.3 13.9 %collective-permute-start.8 = (bf16[256,1024]{1,0:T(8,128)(2,1)S(1)}, bf16[256,1024]{1,0:T(8,128)(2,1)S(1)}, u32[]{:S(2)}, u32[]{:S(2)}) collective-permute-start(bf16[256,1024]{1,0:T(8,128)(2,1)S(1)} %get-tuple-element.16), channel_id=1, source_target_pairs={{0,1},{1,0},{2,3},{3,2},{4,5},{5,4},{6,7},{7,6},{8,9},{9,8},{10,11... | collective-permute-start | bytes 1572872 | tf_op jit(solution)/shard_map/ppermute | solution.py:233
  98.7 1.0 copy-start.3

commit v3 on v2

v3 whole, which is shorter than its diff:
```python
import functools
import math

import jax
import jax.numpy as jnp
import ml_dtypes
import numpy as np
from jax import lax
from jax.experimental import pallas as pl
from jax.experimental.pallas import tpu as pltpu
from jax.sharding import PartitionSpec as P

STOPS = 8
MAPH = 256
SIDE = 128
GROUPS = (4, 2, 2)


def matching(count, distance, parity):
    seen, pairs = set(), []
    for start in range(count):
        cycle, at = [], start
        while at not in seen:
            seen.add(at)
            cycle.append(at)
            at = (at + distance) % count
        for place in range(parity, len(cycle) + parity, 2) if cycle else ():
            a, b = cycle[place % len(cycle)], cycle[(place + 1) % len(cycle)]
            pairs += [(a, b), (b, a)]
    return pairs


def range_table(freq_count):
    index = np.arange(freq_count, dtype=np.int64)
    angle = (index[:, None] * index[None, :] % freq_count).astype(np.float32) * np.float32(
        2.0 * math.pi / freq_count
    )
    factor = np.float32(1.0 / math.sqrt(freq_count))
    real_part, imag_part = np.cos(angle) * factor, -np.sin(angle) * factor
    table = np.block([[real_part, imag_part], [-imag_part, real_part]])
    return table.astype(ml_dtypes.bfloat16)


def stop_order(core):
    return [1, 4 - 2 * core, 3, 5, 2 - 2 * core, 6 - 2 * core, 6 * core, 7]


def cross_tables(map_count, row_count, pulse_count):
    span = STOPS * map_count * pulse_count
    rows = np.arange(row_count, dtype=np.int64)[:, None]
    factor = np.float32(1.0 / math.sqrt(span))
    tables, first = [], 0
    for size in GROUPS:
        table = []
        for m in range(map_count):
            for core in range(2):
                parts = []
                for k in stop_order(core)[first : first + size]:
                    along = (k * map_count + m) * pulse_count + np.arange(pulse_count)
                    angle = (rows * along[None, :] % span).astype(np.float32) * np.float32(
                        2.0 * math.pi / span
                    )
                    parts += [np.cos(angle) * factor, -np.sin(angle) * factor]
                table.append(np.concatenate(parts, axis=1))
        tables.append(np.stack(table).astype(ml_dtypes.bfloat16))
        first += size
    return tables


def call(kernel, outs, operands, scratch=(), flops=0, limit=24):
    specs = [pl.BlockSpec(memory_space=pltpu.SMEM)] + [
        pl.BlockSpec(memory_space=pltpu.VMEM) for _ in operands[1:]
    ]
    size = sum(math.prod(a.shape) * a.dtype.itemsize for a in [*operands, *outs])
    return pl.pallas_call(
        kernel,
        out_shape=outs,
        in_specs=specs,
        out_specs=[pl.BlockSpec(memory_space=pltpu.VMEM) for _ in outs],
        scratch_shapes=list(scratch),
        compiler_params=pltpu.CompilerParams(vmem_limit_bytes=limit * 2**20),
        cost_estimate=pl.CostEstimate(flops=flops, bytes_accessed=size, transcendentals=0),
    )(*operands)


def phase_kernel(map_count, span, facts, curvature, *curves):
    _, pulses, freqs = curves[0].shape
    width = freqs // 4
    core, here_map = facts[0], facts[3]
    outs = [
        (curves[2 * g], curves[2 * g + 1], p) for g, size in enumerate(GROUPS) for p in range(size)
    ]
    pulse = lax.broadcasted_iota(jnp.int32, (pulses, width), 0)
    fine = lax.broadcasted_iota(jnp.int32, (pulses, width), 1).astype(jnp.float32) / freqs
    pulse_on_lanes = lax.broadcasted_iota(jnp.int32, (STOPS, pulses), 1)
    stop_on_rows = lax.broadcasted_iota(jnp.int32, (STOPS, pulses), 0)

    def bend(stop, index):
        along = ((stop * map_count + here_map) * pulses + index).astype(jnp.float32) / span - 0.5
        return curvature[0] * (along * along)

    quarter = bend(stop_on_rows, pulse_on_lanes) * 0.25
    step = jnp.concatenate([jnp.cos(quarter), jnp.sin(quarter)] * (pulses // STOPS // 2), axis=0)
    turned = step.T
    stops = stop_order(core)
    for place in range(STOPS):
        cosines, sines, row = outs[place]
        options = sorted({stop_order(0)[place], stop_order(1)[place]})
        step_c, step_s = (
            turned[:, options[-1] + part : options[-1] + part + 1] for part in (0, STOPS)
        )
        if len(options) == 2:
            is_last = stops[place] == options[-1]
            step_c = jnp.where(is_last, step_c, turned[:, options[0] : options[0] + 1])
            step_s = jnp.where(
                is_last, step_s, turned[:, options[0] + STOPS : options[0] + STOPS + 1]
            )
        step_c = jnp.broadcast_to(step_c, (pulses, width))
        step_s = jnp.broadcast_to(step_s, (pulses, width))
        angle = bend(stops[place], pulse) * fine
        low_c, low_s = jnp.cos(angle), jnp.sin(angle)
        now_c = step_c * low_c - step_s * low_s
        now_s = step_s * low_c + step_c * low_s
        for h in range(4):
            now_c, now_s = step_c * now_c - step_s * now_s, step_s * now_c + step_c * now_s
            cosines[row, :, h * width : (h + 1) * width] = now_c
            sines[row, :, h * width : (h + 1) * width] = now_s


def transform(blocks, cosines, sines, ranges, phased, right_side):
    freqs = cosines.shape[2]
    pulses = cosines.shape[1]
    for place, block in enumerate(blocks):
        values = block().astype(jnp.float32)
        real_part, imag_part = values[:, :freqs], values[:, freqs:]
        cosine, sine = cosines[place], sines[place]
        rows = slice(place * pulses, (place + 1) * pulses)
        phased[rows, :freqs] = (real_part * cosine - imag_part * sine).astype(jnp.bfloat16)
        phased[rows, freqs:] = (real_part * sine + imag_part * cosine).astype(jnp.bfloat16)
    for half in range(2):
        columns = slice(half * freqs, (half + 1) * freqs)
        spectrum = jnp.dot(
            phased[...], ranges[:, columns], preferred_element_type=jnp.float32
        ).astype(jnp.bfloat16)
        for place in range(len(blocks)):
            piece = spectrum[place * pulses : (place + 1) * pulses]
            top = 2 * place * pulses
            right_side[top : top + pulses, columns] = piece
            other = slice((1 - half) * freqs, (2 - half) * freqs)
            right_side[top + pulses : top + 2 * pulses, other] = piece if half == 0 else -piece


def first_kernel(
    facts, own, near_a, near_b, twin, cosines, sines, ranges, cross, total, phased, right_side
):
    chip_odd = facts[1] == 1
    blocks = [
        lambda: jnp.where(chip_odd, near_a[...], near_b[...]),
        lambda: twin[...],
        lambda: own[...],
        lambda: jnp.where(chip_odd, near_b[...], near_a[...]),
    ]
    transform(blocks, cosines, sines, ranges, phased, right_side)
    total[...] = jnp.dot(cross[...], right_side[...], preferred_element_type=jnp.float32)


def second_kernel(
    facts, twin_a, twin_b, cosines, sines, ranges, cross, before, total, phased, right_side
):
    chip_odd = facts[1] == 1
    blocks = [
        lambda: jnp.where(chip_odd, twin_a[...], twin_b[...]),
        lambda: jnp.where(chip_odd, twin_b[...], twin_a[...]),
    ]
    transform(blocks, cosines, sines, ranges, phased, right_side)
    total[...] = before[...] + jnp.dot(
        cross[...], right_side[...], preferred_element_type=jnp.float32
    )


def last_kernel(
    facts, far_a, far_b, twin_far, cosines, sines, ranges, cross, total, sent, kept,
    phased, right_side,
):
    group_odd, here_map = facts[2] == 1, facts[3]
    blocks = [lambda: twin_far[...], lambda: jnp.where(group_odd, far_b[...], far_a[...])]
    transform(blocks, cosines, sines, ranges, phased, right_side)
    rows = sent.shape[0]
    for out, part in ((sent, 1 - here_map), (kept, here_map)):
        place = pl.ds(pl.multiple_of(part * rows, rows), rows)
        out[...] = (
            total[place, :]
            + jnp.dot(cross[place, :], right_side[...], preferred_element_type=jnp.float32)
        ).astype(out.dtype)


def pack_kernel(facts, kept, arrived, slot_hot, side, packed):
    width = kept.shape[1]
    image = (kept[...] + arrived[...].astype(jnp.float32)).astype(jnp.bfloat16)
    marks = 0.0
    for part in range(2):
        packed[:, part * width : (part + 1) * width] = jnp.dot(
            slot_hot[part], image, preferred_element_type=jnp.float32
        ).astype(packed.dtype)
        marks += jnp.dot(slot_hot[part], side[part], preferred_element_type=jnp.float32)
    packed[:, 2 * width :] = marks.astype(packed.dtype)


def map_kernel(facts, got, weights, out):
    columns = weights.shape[0]
    marks = got[:, 4 * columns :].astype(jnp.float32)
    total = 0.0
    for part in range(2):
        first = 2 * part * columns
        real_out = jnp.dot(
            got[:, first : first + columns], weights[...], preferred_element_type=jnp.float32
        )
        imag_out = jnp.dot(
            got[:, first + columns : first + 2 * columns],
            weights[...],
            preferred_element_type=jnp.float32,
        )
        power = real_out * real_out + imag_out * imag_out
        mark = marks[:, part * (SIDE // 2) : part * (SIDE // 2) + 1].astype(jnp.int32)
        spots = lax.broadcasted_iota(jnp.int32, (power.shape[0], MAPH), 1)
        hot = (mark == spots).astype(jnp.bfloat16)
        high = power.astype(jnp.bfloat16)
        low = (power - high.astype(jnp.float32)).astype(jnp.bfloat16)
        for piece in (low, high):
            total += lax.dot_general(
                hot, piece, (((0,), (0,)), ((), ())), preferred_element_type=jnp.float32
            )
    out[...] = total


def swap(block, count):
    return lax.ppermute(block, "blk", [(i, i ^ 1) for i in range(count)])


def slots(strip_tiles, row_offsets, tile_owner, blk_count):
    rows_here = strip_tiles.shape[2]
    capacity = max(2, 2 * rows_here // blk_count)
    row_tiles = strip_tiles[0, 0, :, 0]
    own_offsets = row_offsets[0, 0]
    tile_match = row_tiles[:, None] == jnp.arange(blk_count, dtype=jnp.int32)[None, :]
    destination = jnp.sum(jnp.where(tile_match, tile_owner[None, :], 0), axis=1)
    row_number = jnp.arange(rows_here, dtype=jnp.int32)
    same_before = (row_tiles[:, None] == row_tiles[None, :]) & (
        row_number[None, :] < row_number[:, None]
    )
    rank_within = jnp.sum(same_before.astype(jnp.int32), axis=1)
    slot_index = destination * capacity + rank_within
    numbers = jnp.arange(blk_count * capacity // 2, dtype=jnp.int32)[:, None] * 2
    slot_hot = jnp.stack([numbers + p == slot_index[None, :] for p in (0, 1)])
    lane_half = jnp.arange(SIDE, dtype=jnp.int32)[None, :] // (SIDE // 2)
    side = jnp.stack(
        [jnp.where(lane_half == p, own_offsets[:, None], 0).astype(jnp.bfloat16) for p in (0, 1)]
    )
    return slot_hot.astype(jnp.bfloat16), side


def body(ranges, crosses, phase_history, tile_curvature, interp_weights, strip_tiles, row_offsets, tile_owner):
    blk_count = lax.axis_size("blk")
    map_count = lax.axis_size("map")
    here_blk = lax.axis_index("blk")
    here_map = lax.axis_index("map")
    own_block = phase_history[0, 0]
    pulse_count = own_block.shape[0]
    freq_count = own_block.shape[1] // 2
    columns = interp_weights.shape[2]
    rows_here = strip_tiles.shape[2]

    core, chip_odd, group_odd = here_blk % 2, (here_blk // 2) % 2, (here_blk // 4) % 2
    facts = jnp.stack([core, chip_odd, group_odd, here_map]).astype(jnp.int32)
    slot_hot, side = slots(strip_tiles, row_offsets, tile_owner, blk_count)

    near = [lax.ppermute(own_block, "blk", matching(blk_count, 2, p)) for p in (0, 1)]
    far = [lax.ppermute(own_block, "blk", matching(blk_count, 4, p)) for p in (0, 1)]
    twin = swap(own_block, blk_count)

    f32 = lambda *shape: jax.ShapeDtypeStruct(shape, jnp.float32)
    b16 = lambda *shape: jax.ShapeDtypeStruct(shape, jnp.bfloat16)
    curves = pl.pallas_call(
        functools.partial(phase_kernel, map_count, STOPS * map_count * pulse_count),
        out_shape=[f32(n, pulse_count, freq_count) for n in GROUPS for _ in range(2)],
        in_specs=[pl.BlockSpec(memory_space=pltpu.SMEM)] * 2,
        out_specs=[pl.BlockSpec(memory_space=pltpu.VMEM)] * (2 * len(GROUPS)),
        compiler_params=pltpu.CompilerParams(vmem_limit_bytes=16 * 2**20),
        cost_estimate=pl.CostEstimate(flops=2**22, bytes_accessed=2**22, transcendentals=2**18),
    )(facts, tile_curvature)
    cross = [
        lax.dynamic_index_in_dim(table, here_map * 2 + core, 0, keepdims=False)
        for table in crosses
    ]
    near, twin, curves, cross, slot_hot, side = lax.optimization_barrier(
        (near, twin, curves, cross, slot_hot, side)
    )
    twin_near = [swap(block, blk_count) for block in near]

    deep = 2 * pulse_count
    work = lambda n: [
        pltpu.VMEM((n * pulse_count, 2 * freq_count), jnp.bfloat16),
        pltpu.VMEM((n * deep, 2 * columns), jnp.bfloat16),
    ]
    flops = lambda n: 2 * n * pulse_count * 4 * columns * (freq_count + map_count * rows_here)
    whole = f32(map_count * rows_here, 2 * columns)
    [total] = call(
        first_kernel,
        [whole],
        [facts, own_block, *near, twin, *curves[:2], ranges, cross[0]],
        work(GROUPS[0]),
        flops(GROUPS[0]),
    )
    far, total = lax.optimization_barrier((far, total))
    twin_far = swap(jnp.where(core == group_odd, far[0], far[1]), blk_count)
    [total] = call(
        second_kernel,
        [whole],
        [facts, *twin_near, *curves[2:4], ranges, cross[1], total],
        work(GROUPS[1]),
        flops(GROUPS[1]),
    )
    sent, kept = call(
        last_kernel,
        [b16(rows_here, 2 * columns), f32(rows_here, 2 * columns)],
        [facts, *far, twin_far, *curves[4:], ranges, cross[2], total],
        work(GROUPS[2]),
        flops(GROUPS[2]),
    )
    arrived = lax.ppermute(sent, "map", [(0, 1), (1, 0)])

    pairs = slot_hot.shape[1]
    wide = 4 * columns + SIDE
    [packed] = call(
        pack_kernel,
        [b16(pairs, wide)],
        [facts, kept, arrived, slot_hot, side],
        (),
        2 * pairs * rows_here * (wide + SIDE),
    )
    packed = packed.reshape(blk_count, pairs // blk_count, wide)
    got = lax.all_to_all(packed, "blk", split_axis=0, concat_axis=0, tiled=True)
    [tile_map] = call(
        map_kernel,
        [f32(MAPH, columns)],
        [facts, got.reshape(pairs, wide), interp_weights[0]],
        (),
        2 * pairs * 4 * columns * (columns + MAPH),
    )
    return tile_map.reshape(1, 1, MAPH, columns)


def solution(mesh):
    in_specs = (
        P("blk", "map", None, None),
        P("blk"),
        P("blk", None, None),
        P("blk", "map", None, None),
        P("blk", "map", None),
        P(),
    )
    out_specs = P("blk", "map", None, None)

    def run(*args):
        map_count, pulse_count, width = args[0].shape[1:]
        ranges = jnp.asarray(range_table(width // 2))
        crosses = [
            jnp.asarray(table)
            for table in cross_tables(map_count, map_count * args[3].shape[2], pulse_count)
        ]
        held = lambda *here: body(ranges, crosses, *here)
        return jax.shard_map(
            held, mesh=mesh, in_specs=in_specs, out_specs=out_specs, check_vma=False
        )(*args)

    return run
```

time: 104 us -> 94.5 us (0.909)
  local copies, waits for them, and re-layouts: 7.56 us -> 3.5 us
  waiting for transfers between devices: 20.7 us -> 17 us
  matrix products: 3.65 us -> 0 us
  Pallas kernels: 12 us -> 14.7 us
  other arithmetic: 0.71 us -> 3.18 us
  starting transfers between devices: 10.1 us -> 8.15 us
  blocking collectives: 47.7 us -> 46.6 us
    pallas_call x3 -> x5, Pallas kernels: 7.03 us -> 11.5 us  [call(): pl.pallas_call(kernel, out_shape=outs, in_specs=specs, out_specs=[pl.Bloc...]
    ppermute x2, waiting for transfers between devices: 7.52 us -> 3.2 us  [body(): lax.ppermute(own_block, 'blk', matching(blk_count, 2, p))]
    dot_general x5 -> x0, matrix products: 3.65 us -> none  [the longest x3 1.74 us: body(): jnp.dot(place_hot, piece, preferred_element_type=jnp.float32)]
    slice x2 -> x0, local copies, waits for them, and re-layouts: 2.74 us -> none  [the longest x1 1.66 us: body(): cross[:, :early * deep]]
    ppermute x2, starting transfers between devices: 3.3 us -> 1.19 us  [body(): lax.ppermute(own_block, 'blk', matching(blk_count, 4, p))]
    pallas_call x1, Pallas kernels: 5 us -> 3.19 us  [body(): pl.pallas_call(functools.partial(phase_kernel, map_count, STOPS * map_cou...]
    reduce_sum x2, other arithmetic: 0.35 us -> 1.81 us  [the longest x1 0.93 us: slots(): rank_within = jnp.sum(same_before.astype(jnp.int32), axis=1)]
    all_to_all x1, blocking collectives: 47.7 us -> 46.6 us  [body(): got = lax.all_to_all(packed, 'blk', split_axis=0, concat_axis=0, tiled=True)]
where the time goes in v3:
time: 94.5 us; the launch traced here: 94.2 us
  blocking collectives  46.6 us (49%)
  waiting for transfers between devices  17 us (18%)
  Pallas kernels  14.7 us (16%)
  starting transfers between devices  8.15 us (9%)
  local copies, waits for them, and re-layouts  3.5 us (4%)
  other arithmetic  3.18 us (3%)
  between operations  1.06 us (1%)
    all_to_all x1, blocking collectives, body(): got = lax.all_to_all(packed, 'blk', split_axis=0, concat_axis=0, tiled=True)  46.6 us
    ppermute x1, waiting for transfers between devices, body(): arrived = lax.ppermute(sent, 'map', [(0, 1), (1, 0)])  13.8 us
    pallas_call x5, Pallas kernels, call(): pl.pallas_call(kernel, out_shape=outs, in_specs=specs, out_specs=[pl.Bloc...  11.5 us
    ppermute x2, starting transfers between devices, body(): lax.ppermute(own_block, 'blk', matching(blk_count, 2, p))  5.53 us
    ppermute x2, waiting for transfers between devices, body(): lax.ppermute(own_block, 'blk', matching(blk_count, 2, p))  3.2 us
    pallas_call x1, Pallas kernels, body(): pl.pallas_call(functools.partial(phase_kernel, map_count, STOPS * map_cou...  3.19 us
    squeeze x2, local copies, waits for them, and re-layouts, body(): lax.dynamic_index_in_dim(table, here_map * 2 + core, 0, keepdims=False)  2.58 us
  transfers between devices with their start and end apart: 9, of which 3 were waited for; matrix products, arithmetic and copies ran while one was open for 6% of the time, Pallas kernels for 9%

profile of v3, /device:TPU:32, one launch (start us, length us, event | category | flops | bytes accessed | tf_op | source)
XLA Modules:
  0.0 94.2 jit_solution(82997602404876919)
XLA Ops:
  0.0 3.0 %collective-permute-start.2 = (bf16[128,1024]{1,0:T(8,128)(2,1)}, bf16[128,1024]{1,0:T(8,128)(2,1)}, u32[]{:S(2)}, u32[]{:S(2)}) collective-permute-start(bf16[128,1024]{1,0:T(8,128)(2,1)} %bitcast.15), channel_id=1, source_target_pairs={{0,4},{4,0},{8,12},{12,8},{16,20},{20,16},{24,28},{28,24},{32,36},... | collective-permute-start | bytes 786440 | tf_op jit(solution)/shard_map/ppermute | solution.py:277
  3.0 2.5 %collective-permute-start.3 = (bf16[128,1024]{1,0:T(8,128)(2,1)}, bf16[128,1024]{1,0:T(8,128)(2,1)}, u32[]{:S(2)}, u32[]{:S(2)}) collective-permute-start(bf16[128,1024]{1,0:T(8,128)(2,1)} %bitcast.16), channel_id=1, source_target_pairs={{4,8},{8,4},{12,16},{16,12},{20,24},{24,20},{28,32},{32,28},{36,40... | collective-permute-start | bytes 786440 | tf_op jit(solution)/shard_map/ppermute | solution.py:277
  5.5 1.2 %collective-permute-start.1 = (bf16[128,1024]{1,0:T(8,128)(2,1)}, bf16[128,1024]{1,0:T(8,128)(2,1)}, u32[]{:S(2)}, u32[]{:S(2)}) collective-permute-start(bf16[128,1024]{1,0:T(8,128)(2,1)} %bitcast.19), channel_id=1, source_target_pairs={{8,16},{16,8},{24,32},{32,24},{40,48},{48,40},{56,64},{64,56},{72,... | collective-permute-start | bytes 786440 | tf_op jit(solution)/shard_map/ppermute | solution.py:278
  6.7 0.9 convert_reduce_fusion
  7.7 0.9 select_reduce_fusion
  8.6 1.3 %dynamic-slice_bitcast_fusion.cross = bf16[512,1024]{1,0:T(8,128)(2,1)S(1)} fusion(bf16[4,512,1024]{2,1,0:T(8,128)(2,1)} %constant.92.clone, s32[]{:T(128)S(6)} %select_n.82), kind=kLoop, calls=%fused_computation | loop fusion | bytes 2097156 | tf_op jit(solution)/shard_map/jit(dynamic_index_in_dim)/squeeze | solution.py:292
  9.9 0.1 broadcast_compare_fusion.1
  10.1 0.1 select_convert_fusion.1
  11.1 3.2 %shard_map.100 = (f32[4,128,512]{2,1,0:T(8,128)S(1)}, f32[4,128,512]{2,1,0:T(8,128)S(1)}, f32[2,128,512]{2,1,0:T(8,128)S(1)}, f32[2,128,512]{2,1,0:T(8,128)S(1)}...) custom-call(s32[4]{0:T(128)S(1)} %pad_add_fusion.facts, f32[1]{0:T(128)S(6)} %copy.11.curvature), custom_call_target="tpu_custom_call" | custom-call | flops 4194304 | bytes 4194304 | tf_op jit(solution)/shard_map/pallas_call | solution.py:283
  14.3 1.3 %dynamic-slice_bitcast_fusion.1 = (bf16[512,512]{1,0:T(8,128)(2,1)S(1)}, bf16[512,512]{1,0:T(8,128)(2,1)S(1)}) fusion(bf16[4,512,512]{2,1,0:T(8,128)(2,1)} %constant.94.clone, s32[]{:T(128)S(6)} %select_n.82, bf16[4,512,512]{2,1,0:T(8,128)(2,1)} %constant.93.clone), kind=kLoop, calls=%fused_computation.1 | loop fusion | bytes 2097156 | tf_op jit(solution)/shard_map/jit(dynamic_index_in_dim)/squeeze | solution.py:292
  15.7 3.1 %collective-permute-done.3.near_b = bf16[128,1024]{1,0:T(8,128)(2,1)} collective-permute-done((bf16[128,1024]{1,0:T(8,128)(2,1)}, bf16[128,1024]{1,0:T(8,128)(2,1)}, u32[]{:S(2)}, u32[]{:S(2)}) %collective-permute-start.3) | collective-permute-done | bytes 262176 | tf_op jit(solution)/shard_map/ppermute | solution.py:277
  18.8 0.5 collective-permute-start.7
  19.4 3.5 %shard_map.101.before = f32[512,1024]{1,0:T(8,128)S(1)} custom-call(s32[4]{0:T(128)S(1)} %pad_add_fusion.facts, bf16[128,1024]{1,0:T(8,128)(2,1)S(1)} %bitcast.20, bf16[128,1024]{1,0:T(8,128)(2,1)} %collective-permute-done.2.near_a, bf16[128,1024]{1,0:T(8,128)(2,1)} %collective-permute-done.3.near_b, bf16[128,1024]{1,0:T(8,128)(2,1)} %collective-permute-done.4.twin, ...), custom_call_target="tpu_custom_call" | custom-call | flops 2147483648 | bytes 8388624 | tf_op jit(solution)/shard_map/pallas_call | solution.py:75
  22.9 1.0 %broadcast_select_fusion = bf16[128,1024]{1,0:T(8,128)(2,1)S(1)} fusion(bf16[128,1024]{1,0:T(8,128)(2,1)} %collective-permute-done.far_a, bf16[128,1024]{1,0:T(8,128)(2,1)} %collective-permute-done.1.far_b, pred[]{:T(512)S(6)} %eq.105), kind=kLoop, calls=%fused_computation.7 | loop fusion | flops 131072 | bytes 786433 | tf_op jit(solution)/shard_map/jit(_where)/select_n | solution.py:315
  23.9 0.1 collective-permute-start.5
  24.0 1.9 %shard_map.102.total = f32[512,1024]{1,0:T(8,128)S(1)} custom-call(s32[4]{0:T(128)S(1)} %pad_add_fusion.facts, bf16[128,1024]{1,0:T(8,128)(2,1)S(1)} %collective-permute-done.6.twin_a, bf16[128,1024]{1,0:T(8,128)(2,1)S(1)} %collective-permute-done.7.twin_b, f32[2,128,512]{2,1,0:T(8,128)S(1)} %get-tuple-element.47.cosines, ...), custom_call_target="tpu_custom_call" | custom-call | flops 1073741824 | bytes 8388624 | tf_op jit(solution)/shard_map/pallas_call | solution.py:75
  26.0 2.4 %shard_map.103 = (bf16[256,1024]{1,0:T(8,128)(2,1)S(1)}, f32[256,1024]{1,0:T(8,128)S(1)}) custom-call(s32[4]{0:T(128)S(1)} %pad_add_fusion.facts, bf16[128,1024]{1,0:T(8,128)(2,1)} %collective-permute-done.far_a, bf16[128,1024]{1,0:T(8,128)(2,1)} %collective-permute-done.1.far_b, bf16[128,1024]{1,0:T(8,128)(2,1)S(1)} %collective-permute-done.5.twin_far, ...), custom_call_target="tpu_custom_call" | custom-call | flops 1073741824 | bytes 8126480 | tf_op jit(solution)/shard_map/pallas_call | solution.py:75
  28.4 0.8 collective-permute-start.8
  29.2 13.8 %collective-permute-done.8.arrived = bf16[256,1024]{1,0:T(8,128)(2,1)S(1)} collective-permute-done((bf16[256,1024]{1,0:T(8,128)(2,1)S(1)}, bf16[256,1024]{1,0:T(8,128)(2,1)S(1)}, u32[]{:S(2)}, u32[]{:S(2)}) %collective-permute-start.8) | collective-permute-done | bytes 524320 | tf_op jit(solution)/shard_map/ppermute | solution.py:330
  42.9 1.1 %shard_map.104 = bf16[256,2176]{1,0:T(8,128)(2,1)S(1)} custom-call(s32[4]{0:T(128)S(1)} %pad_add_fusion.facts, f32[256,1024]{1,0:T(8,128)S(1)} %get-tuple-element.51.kept, bf16[256,1024]{1,0:T(8,128)(2,1)S(1)} %collective-permute-done.8.arrived, bf16[2,256,256]{2,1,0:T(8,128)(2,1)S(1)} %add_convert_fusion.slot_hot, bf16[2,256,128]{2,1,0:T(8,128)(2,1)S(1)} %pad_maximum_fusion.side), custom_call_target="tpu_custom_call" | custom-call | flops 301989888 | bytes 3080208 | tf_op jit(solution)/shard_map/pallas_call | solution.py:75
  44.0 0.5 reshape.265
  44.5 46.6 %all_to_all.5 = bf16[128,2,2176]{2,1,0:T(2,128)(2,1)S(1)} all-to-all(bf16[128,2,2176]{2,1,0:T(2,128)(2,1)S(1)} %reshape.265), channel_id=1, replica_groups=mesh['blk'=128,'map'=2] {'blk'}, dimensions={0} | all-to-all | bytes 2228224 | tf_op jit(solution)/shard_map/all_to_all | solution.py:342
  91.1 0.4 reshape.266.got
  91.6 2.6 %shard_map.105 = f32[256,512]{1,0:T(8,128)} custom-call(s32[4]{0:T(128)S(1)} %pad_add_fusion.facts, bf16[256,2176]{1,0:T(8,128)(2,1)S(1)} %reshape.266.got, bf16[512,512]{1,0:T(8,128)(2,1)S(1)} %bitcast.21), custom_call_target="tpu_custom_call" | custom-call | flops 805306368 | bytes 2162704 | tf_op jit(solution)/shard_map/pallas_call | solution.py:75
  (24 shorter events, 0.3 us)
Async XLA Ops:
  0.0 10.1 %copy-start.3 = (s32[1,1,256]{2,1,0:T(1,128)S(1)}, s32[1,1,256]{2,1,0:T(1,128)}, u32[]{:S(2)}) copy-start(s32[1,1,256]{2,1,0:T(1,128)} %param.14) | copy-start | bytes 3076
  0.0 15.7 %collective-permute-start.2 = (bf16[128,1024]{1,0:T(8,128)(2,1)}, bf16[128,1024]{1,0:T(8,128)(2,1)}, u32[]{:S(2)}, u32[]{:S(2)}) collective-permute-start(bf16[128,1024]{1,0:T(8,128)(2,1)} %bitcast.15), channel_id=1, source_target_pairs={{0,4},{4,0},{8,12},{12,8},{16,20},{20,16},{24,28},{28,24},{32,36},... | collective-permute-start | bytes 786440 | tf_op jit(solution)/shard_map/ppermute | solution.py:277
  3.0 15.8 %collective-permute-start.3 = (bf16[128,1024]{1,0:T(8,128)(2,1)}, bf16[128,1024]{1,0:T(8,128)(2,1)}, u32[]{:S(2)}, u32[]{:S(2)}) collective-permute-start(bf16[128,1024]{1,0:T(8,128)(2,1)} %bitcast.16), channel_id=1, source_target_pairs={{4,8},{8,4},{12,16},{16,12},{20,24},{24,20},{28,32},{32,28},{36,40... | collective-permute-start | bytes 786440 | tf_op jit(solution)/shard_map/ppermute | solution.py:277
  5.5 13.3 %collective-permute-start.4 = (bf16[128,1024]{1,0:T(8,128)(2,1)}, bf16[128,1024]{1,0:T(8,128)(2,1)}, u32[]{:S(2)}, u32[]{:S(2)}) collective-permute-start(bf16[128,1024]{1,0:T(8,128)(2,1)} %bitcast.17), channel_id=1, source_target_pairs={{0,2},{2,0},{4,6},{6,4},{8,10},{10,8},{12,14},{14,12},{16,18},{18,... | collective-permute-start | bytes 786440 | tf_op jit(solution)/shard_map/ppermute | solution.py:237
  5.5 17.4 %collective-permute-start = (bf16[128,1024]{1,0:T(8,128)(2,1)}, bf16[128,1024]{1,0:T(8,128)(2,1)}, u32[]{:S(2)}, u32[]{:S(2)}) collective-permute-start(bf16[128,1024]{1,0:T(8,128)(2,1)} %bitcast.18), channel_id=1, source_target_pairs={{0,8},{8,0},{16,24},{24,16},{32,40},{40,32},{48,56},{56,48},{64,72... | collective-permute-start | bytes 786440 | tf_op jit(solution)/shard_map/ppermute | solution.py:278
  5.5 17.4 %collective-permute-start.1 = (bf16[128,1024]{1,0:T(8,128)(2,1)}, bf16[128,1024]{1,0:T(8,128)(2,1)}, u32[]{:S(2)}, u32[]{:S(2)}) collective-permute-start(bf16[128,1024]{1,0:T(8,128)(2,1)} %bitcast.19), channel_id=1, source_target_pairs={{8,16},{16,8},{24,32},{32,24},{40,48},{48,40},{56,64},{64,56},{72,... | collective-permute-start | bytes 786440 | tf_op jit(solution)/shard_map/ppermute | solution.py:278
  9.9 9.5 %copy-start = (bf16[1024,1024]{1,0:T(8,128)(2,1)S(1)}, bf16[1024,1024]{1,0:T(8,128)(2,1)}, u32[]{:S(2)}) copy-start(bf16[1024,1024]{1,0:T(8,128)(2,1)} %constant.95.clone.ranges) | copy-start | bytes 6291460
  10.3 9.1 %copy-start.1 = (bf16[1,1,128,1024]{3,2,1,0:T(8,128)(2,1)S(1)}, bf16[1,1,128,1024]{3,2,1,0:T(8,128)(2,1)}, u32[]{:S(2)}) copy-start(bf16[1,1,128,1024]{3,2,1,0:T(8,128)(2,1)} %param.10) | copy-start | bytes 786436
  18.8 5.2 %collective-permute-start.6 = (bf16[128,1024]{1,0:T(8,128)(2,1)}, bf16[128,1024]{1,0:T(8,128)(2,1)S(1)}, u32[]{:S(2)}, u32[]{:S(2)}) collective-permute-start(bf16[128,1024]{1,0:T(8,128)(2,1)} %collective-permute-done.2.near_a), channel_id=1, source_target_pairs={{0,2},{2,0},{4,6},{6,4},{8,10},{10,8},{12,14},{14,12},{16,18},{18,... | collective-permute-start | bytes 786440 | tf_op jit(solution)/shard_map/ppermute | solution.py:237
  18.8 5.2 %collective-permute-start.7 = (bf16[128,1024]{1,0:T(8,128)(2,1)}, bf16[128,1024]{1,0:T(8,128)(2,1)S(1)}, u32[]{:S(2)}, u32[]{:S(2)}) collective-permute-start(bf16[128,1024]{1,0:T(8,128)(2,1)} %collective-permute-done.3.near_b), channel_id=1, source_target_pairs={{0,2},{2,0},{4,6},{6,4},{8,10},{10,8},{12,14},{14,12},{16,18},{18,... | collective-permute-start | bytes 786440 | tf_op jit(solution)/shard_map/ppermute | solution.py:237
  23.9 2.1 %collective-permute-start.5 = (bf16[128,1024]{1,0:T(8,128)(2,1)S(1)}, bf16[128,1024]{1,0:T(8,128)(2,1)S(1)}, u32[]{:S(2)}, u32[]{:S(2)}) collective-permute-start(bf16[128,1024]{1,0:T(8,128)(2,1)S(1)} %broadcast_select_fusion), channel_id=1, source_target_pairs={{0,2},{2,0},{4,6},{6,4},{8,10},{10,8},{12,14},{14,12},{16,18},{18,... | collective-permute-start | bytes 786440 | tf_op jit(solution)/shard_map/ppermute | solution.py:237
  28.4 14.6 %collective-permute-start.8 = (bf16[256,1024]{1,0:T(8,128)(2,1)S(1)}, bf16[256,1024]{1,0:T(8,128)(2,1)S(1)}, u32[]{:S(2)}, u32[]{:S(2)}) collective-permute-start(bf16[256,1024]{1,0:T(8,128)(2,1)S(1)} %get-tuple-element.52), channel_id=1, source_target_pairs={{0,1},{1,0},{2,3},{3,2},{4,5},{5,4},{6,7},{7,6},{8,9},{9,8},{10,11... | collective-permute-start | bytes 1572872 | tf_op jit(solution)/shard_map/ppermute | solution.py:330
  44.5 47.1 %copy-start.2 = (bf16[1,512,512]{2,1,0:T(8,128)(2,1)S(1)}, bf16[1,512,512]{2,1,0:T(8,128)(2,1)}, u32[]{:S(2)}) copy-start(bf16[1,512,512]{2,1,0:T(8,128)(2,1)} %param.12) | copy-start | bytes 1572868

commit v4 on v3

--- a/solution.py
+++ b/solution.py
@@ -13,7 +13,7 @@
 STOPS = 8
 MAPH = 256
 SIDE = 128
-GROUPS = (4, 2, 2)
+GROUPS = (2, 2, 4)
 
 
 def matching(count, distance, parity):
@@ -42,7 +42,7 @@
 
 
 def stop_order(core):
-    return [1, 4 - 2 * core, 3, 5, 2 - 2 * core, 6 - 2 * core, 6 * core, 7]
+    return [3, 4 - 2 * core, 1, 5, 2 - 2 * core, 6 - 2 * core, 6 * core, 7]
 
 
 def cross_tables(map_count, row_count, pulse_count):
@@ -67,11 +67,12 @@
     return tables
 
 
-def call(kernel, outs, operands, scratch=(), flops=0, limit=24):
+def call(kernel, outs, operands, scratch=(), flops=0, limit=24, far=()):
     specs = [pl.BlockSpec(memory_space=pltpu.SMEM)] + [
-        pl.BlockSpec(memory_space=pltpu.VMEM) for _ in operands[1:]
+        pl.BlockSpec(memory_space=pltpu.HBM if n in far else pltpu.VMEM)
+        for n in range(1, len(operands))
     ]
-    size = sum(math.prod(a.shape) * a.dtype.itemsize for a in [*operands, *outs])
+    size = sum(math.prod(a.shape) * a.dtype.itemsize for a in [*operands, *outs]) if flops else 0
     return pl.pallas_call(
         kernel,
         out_shape=outs,
@@ -150,60 +151,115 @@
             right_side[top + pulses : top + 2 * pulses, other] = piece if half == 0 else -piece
 
 
+def fetch(facts, tables, cross, arrival):
+    copy = pltpu.make_async_copy(tables.at[facts[4]], cross, arrival)
+    copy.start()
+    return copy
+
+
 def first_kernel(
-    facts, own, near_a, near_b, twin, cosines, sines, ranges, cross, total, phased, right_side
+    facts, own, twin, cosines, sines, ranges, tables, total, phased, right_side, cross, arrival
 ):
+    copy = fetch(facts, tables, cross, arrival)
+    transform([lambda: own[...], lambda: twin[...]], cosines, sines, ranges, phased, right_side)
+    copy.wait()
+    total[...] = jnp.dot(cross[...], right_side[...], preferred_element_type=jnp.float32)
+
+
+def second_kernel(
+    facts, near_a, near_b, cosines, sines, ranges, tables, before, total,
+    phased, right_side, cross, arrival,
+):
+    copy = fetch(facts, tables, cross, arrival)
     chip_odd = facts[1] == 1
     blocks = [
         lambda: jnp.where(chip_odd, near_a[...], near_b[...]),
-        lambda: twin[...],
-        lambda: own[...],
         lambda: jnp.where(chip_odd, near_b[...], near_a[...]),
     ]
     transform(blocks, cosines, sines, ranges, phased, right_side)
-    total[...] = jnp.dot(cross[...], right_side[...], preferred_element_type=jnp.float32)
-
-
-def second_kernel(
-    facts, twin_a, twin_b, cosines, sines, ranges, cross, before, total, phased, right_side
+    copy.wait()
+    total[...] = before[...] + jnp.dot(
+        cross[...], right_side[...], preferred_element_type=jnp.float32
+    )
+
+
+def part_rows(ref, part):
+    rows = ref.shape[0] // 2
+    return ref[pl.ds(pl.multiple_of(part * rows, rows), rows), :]
+
+
+def last_kernel(
+    facts, twin_near_a, twin_near_b, far_a, far_b, twin_far_a, twin_far_b,
+    cosines, sines, ranges, tables, before, sent, right_side, phased, cross, arrival,
 ):
-    chip_odd = facts[1] == 1
+    copy = fetch(facts, tables, cross, arrival)
+    chip_odd, group_odd = facts[1] == 1, facts[2] == 1
+    from_a = facts[0] != facts[2]
     blocks = [
-        lambda: jnp.where(chip_odd, twin_a[...], twin_b[...]),
-        lambda: jnp.where(chip_odd, twin_b[...], twin_a[...]),
+        lambda: jnp.where(chip_odd, twin_near_a[...], twin_near_b[...]),
+        lambda: jnp.where(chip_odd, twin_near_b[...], twin_near_a[...]),
+        lambda: jnp.where(from_a, twin_far_a[...], twin_far_b[...]),
+        lambda: jnp.where(group_odd, far_b[...], far_a[...]),
     ]
     transform(blocks, cosines, sines, ranges, phased, right_side)
-    total[...] = before[...] + jnp.dot(
-        cross[...], right_side[...], preferred_element_type=jnp.float32
-    )
-
-
-def last_kernel(
-    facts, far_a, far_b, twin_far, cosines, sines, ranges, cross, total, sent, kept,
-    phased, right_side,
-):
-    group_odd, here_map = facts[2] == 1, facts[3]
-    blocks = [lambda: twin_far[...], lambda: jnp.where(group_odd, far_b[...], far_a[...])]
-    transform(blocks, cosines, sines, ranges, phased, right_side)
-    rows = sent.shape[0]
-    for out, part in ((sent, 1 - here_map), (kept, here_map)):
-        place = pl.ds(pl.multiple_of(part * rows, rows), rows)
-        out[...] = (
-            total[place, :]
-            + jnp.dot(cross[place, :], right_side[...], preferred_element_type=jnp.float32)
-        ).astype(out.dtype)
-
-
-def pack_kernel(facts, kept, arrived, slot_hot, side, packed):
+    copy.wait()
+    other = 1 - facts[3]
+    sent[...] = (
+        part_rows(before, other)
+        + jnp.dot(
+            part_rows(cross, other), right_side[...], preferred_element_type=jnp.float32
+        )
+    ).astype(sent.dtype)
+
+
+def kept_kernel(facts, right_side, tables, before, kept, cross, arrival):
+    copy = fetch(facts, tables, cross, arrival)
+    copy.wait()
+    kept[...] = part_rows(before, facts[3]) + jnp.dot(
+        part_rows(cross, facts[3]), right_side[...], preferred_element_type=jnp.float32
+    )
+
+
+def slot_kernel(facts, tiles, offsets, owner, slot_hot, marks):
+    count, rows = owner.shape[1], tiles.shape[1]
+    _, pairs, _ = slot_hot.shape
+    capacity = 2 * pairs // count
+    tile_hot = (lax.broadcasted_iota(jnp.int32, (count, rows), 0) == tiles[...]).astype(
+        jnp.bfloat16
+    )
+    owners = jnp.broadcast_to(owner[...].astype(jnp.float32), (8, count)).astype(jnp.bfloat16)
+    holder = jnp.dot(owners, tile_hot, preferred_element_type=jnp.float32)[0:1]
+    same = lax.dot_general(
+        tile_hot, tile_hot, (((0,), (0,)), ((), ())), preferred_element_type=jnp.float32
+    )
+    earlier = lax.broadcasted_iota(jnp.int32, (rows, rows), 0) < lax.broadcasted_iota(
+        jnp.int32, (rows, rows), 1
+    )
+    rank = jnp.sum(jnp.where(earlier, same, 0.0), axis=0, keepdims=True)
+    slot = (holder * capacity + rank).astype(jnp.int32)
+    numbers = 2 * lax.broadcasted_iota(jnp.int32, (pairs, rows), 0)
+    half = marks.shape[1] // 2
+    for part in range(2):
+        hot = numbers + part == slot
+        slot_hot[part] = hot.astype(jnp.float32).astype(jnp.bfloat16)
+        mark = jnp.sum(
+            jnp.where(hot, offsets[...].astype(jnp.float32), 0.0), axis=1, keepdims=True
+        )
+        spread = jnp.broadcast_to(mark, (pairs, half))
+        sides = [spread, jnp.zeros_like(spread)]
+        both = jnp.concatenate(sides if part == 0 else sides[::-1], axis=1)
+        total = both if part == 0 else total + both
+    marks[...] = total.astype(jnp.bfloat16)
+
+
+def pack_kernel(facts, kept, arrived, slot_hot, marks, packed):
     width = kept.shape[1]
     image = (kept[...] + arrived[...].astype(jnp.float32)).astype(jnp.bfloat16)
-    marks = 0.0
     for part in range(2):
         packed[:, part * width : (part + 1) * width] = jnp.dot(
             slot_hot[part], image, preferred_element_type=jnp.float32
         ).astype(packed.dtype)
-        marks += jnp.dot(slot_hot[part], side[part], preferred_element_type=jnp.float32)
-    packed[:, 2 * width :] = marks.astype(packed.dtype)
+    packed[:, 2 * width :] = marks[...]
 
 
 def map_kernel(facts, got, weights, out):
@@ -237,28 +293,6 @@
     return lax.ppermute(block, "blk", [(i, i ^ 1) for i in range(count)])
 
 
-def slots(strip_tiles, row_offsets, tile_owner, blk_count):
-    rows_here = strip_tiles.shape[2]
-    capacity = max(2, 2 * rows_here // blk_count)
-    row_tiles = strip_tiles[0, 0, :, 0]
-    own_offsets = row_offsets[0, 0]
-    tile_match = row_tiles[:, None] == jnp.arange(blk_count, dtype=jnp.int32)[None, :]
-    destination = jnp.sum(jnp.where(tile_match, tile_owner[None, :], 0), axis=1)
-    row_number = jnp.arange(rows_here, dtype=jnp.int32)
-    same_before = (row_tiles[:, None] == row_tiles[None, :]) & (
-        row_number[None, :] < row_number[:, None]
-    )
-    rank_within = jnp.sum(same_before.astype(jnp.int32), axis=1)
-    slot_index = destination * capacity + rank_within
-    numbers = jnp.arange(blk_count * capacity // 2, dtype=jnp.int32)[:, None] * 2
-    slot_hot = jnp.stack([numbers + p == slot_index[None, :] for p in (0, 1)])
-    lane_half = jnp.arange(SIDE, dtype=jnp.int32)[None, :] // (SIDE // 2)
-    side = jnp.stack(
-        [jnp.where(lane_half == p, own_offsets[:, None], 0).astype(jnp.bfloat16) for p in (0, 1)]
-    )
-    return slot_hot.astype(jnp.bfloat16), side
-
-
 def body(ranges, crosses, phase_history, tile_curvature, interp_weights, strip_tiles, row_offsets, tile_owner):
     blk_count = lax.axis_size("blk")
     map_count = lax.axis_size("map")
@@ -271,8 +305,7 @@
     rows_here = strip_tiles.shape[2]
 
     core, chip_odd, group_odd = here_blk % 2, (here_blk // 2) % 2, (here_blk // 4) % 2
-    facts = jnp.stack([core, chip_odd, group_odd, here_map]).astype(jnp.int32)
-    slot_hot, side = slots(strip_tiles, row_offsets, tile_owner, blk_count)
+    facts = jnp.stack([core, chip_odd, group_odd, here_map, here_map * 2 + core]).astype(jnp.int32)
 
     near = [lax.ppermute(own_block, "blk", matching(blk_count, 2, p)) for p in (0, 1)]
     far = [lax.ppermute(own_block, "blk", matching(blk_count, 4, p)) for p in (0, 1)]
@@ -288,55 +321,77 @@
         compiler_params=pltpu.CompilerParams(vmem_limit_bytes=16 * 2**20),
         cost_estimate=pl.CostEstimate(flops=2**22, bytes_accessed=2**22, transcendentals=2**18),
     )(facts, tile_curvature)
-    cross = [
-        lax.dynamic_index_in_dim(table, here_map * 2 + core, 0, keepdims=False)
-        for table in crosses
-    ]
-    near, twin, curves, cross, slot_hot, side = lax.optimization_barrier(
-        (near, twin, curves, cross, slot_hot, side)
-    )
-    twin_near = [swap(block, blk_count) for block in near]
-
     deep = 2 * pulse_count
-    work = lambda n: [
-        pltpu.VMEM((n * pulse_count, 2 * freq_count), jnp.bfloat16),
-        pltpu.VMEM((n * deep, 2 * columns), jnp.bfloat16),
+    image_shape = (map_count * rows_here, 2 * columns)
+    half_shape = (rows_here, 2 * columns)
+    right = lambda n: pltpu.VMEM((n * deep, 2 * columns), jnp.bfloat16)
+    spread = lambda n: pltpu.VMEM((n * pulse_count, 2 * freq_count), jnp.bfloat16)
+    table = lambda n: [
+        pltpu.VMEM((map_count * rows_here, n * deep), jnp.bfloat16),
+        pltpu.SemaphoreType.DMA,
     ]
     flops = lambda n: 2 * n * pulse_count * 4 * columns * (freq_count + map_count * rows_here)
-    whole = f32(map_count * rows_here, 2 * columns)
+    n = GROUPS[0]
     [total] = call(
         first_kernel,
-        [whole],
-        [facts, own_block, *near, twin, *curves[:2], ranges, cross[0]],
-        work(GROUPS[0]),
-        flops(GROUPS[0]),
-    )
-    far, total = lax.optimization_barrier((far, total))
-    twin_far = swap(jnp.where(core == group_odd, far[0], far[1]), blk_count)
+        [f32(*image_shape)],
+        [facts, own_block, twin, *curves[:2], ranges, crosses[0]],
+        [spread(n), right(n), *table(n)],
+        flops(n),
+        far=(6,),
+    )
+    near, far, total = lax.optimization_barrier((near, far, total))
+    twin_near = [swap(block, blk_count) for block in near]
+    twin_far = [swap(block, blk_count) for block in far]
+    n = GROUPS[1]
     [total] = call(
         second_kernel,
-        [whole],
-        [facts, *twin_near, *curves[2:4], ranges, cross[1], total],
-        work(GROUPS[1]),
-        flops(GROUPS[1]),
-    )
-    sent, kept = call(
+        [f32(*image_shape)],
+        [facts, *near, *curves[2:4], ranges, crosses[1], total],
+        [spread(n), right(n), *table(n)],
+        flops(n),
+        far=(6,),
+    )
+    twin_near, twin_far, total = lax.optimization_barrier((twin_near, twin_far, total))
+    n = GROUPS[2]
+    sent, right_side = call(
         last_kernel,
-        [b16(rows_here, 2 * columns), f32(rows_here, 2 * columns)],
-        [facts, *far, twin_far, *curves[4:], ranges, cross[2], total],
-        work(GROUPS[2]),
-        flops(GROUPS[2]),
+        [b16(*half_shape), b16(n * deep, 2 * columns)],
+        [facts, *twin_near, *far, *twin_far, *curves[4:], ranges, crosses[2], total],
+        [spread(n), *table(n)],
+        flops(n),
+        far=(10,),
+    )
+    sent, right_side, strip_tiles, row_offsets = lax.optimization_barrier(
+        (sent, right_side, strip_tiles, row_offsets)
     )
     arrived = lax.ppermute(sent, "map", [(0, 1), (1, 0)])
-
-    pairs = slot_hot.shape[1]
+    pairs = max(2, 2 * rows_here // blk_count) * blk_count // 2
+    slot_hot, marks = call(
+        slot_kernel,
+        [b16(2, pairs, rows_here), b16(pairs, SIDE)],
+        [
+            facts,
+            strip_tiles.reshape(1, rows_here),
+            row_offsets.reshape(1, rows_here),
+            tile_owner.reshape(1, blk_count),
+        ],
+    )
+    [kept] = call(
+        kept_kernel,
+        [f32(*half_shape)],
+        [facts, right_side, crosses[2], total],
+        table(n),
+        far=(2,),
+    )
+
     wide = 4 * columns + SIDE
     [packed] = call(
         pack_kernel,
         [b16(pairs, wide)],
-        [facts, kept, arrived, slot_hot, side],
+        [facts, kept, arrived, slot_hot, marks],
         (),
-        2 * pairs * rows_here * (wide + SIDE),
+        2 * pairs * rows_here * wide,
     )
     packed = packed.reshape(blk_count, pairs // blk_count, wide)
     got = lax.all_to_all(packed, "blk", split_axis=0, concat_axis=0, tiled=True)

time: 94.5 us -> 93.4 us (0.988)
  waiting for transfers between devices: 17 us -> 11.9 us
  other arithmetic: 3.18 us -> 0 us
  local copies, waits for them, and re-layouts: 3.5 us -> 6.31 us
  starting transfers between devices: 8.15 us -> 10.3 us
  blocking collectives: 46.6 us -> 47.9 us
  Pallas kernels: 14.7 us -> 15.8 us
    unnamed x8 -> x20, local copies, waits for them, and re-layouts: 0.02 us -> 4.26 us
    ppermute x1, waiting for transfers between devices: 13.8 us -> 10 us  [body(): arrived = lax.ppermute(sent, 'map', [(0, 1), (1, 0)])]
    squeeze x2 -> x0, local copies, waits for them, and re-layouts: 2.58 us -> none  [body(): lax.dynamic_index_in_dim(table, here_map * 2 + core, 0, keepdims=False)]
    ppermute x2, starting transfers between devices: 1.19 us -> 3.15 us  [body(): lax.ppermute(own_block, 'blk', matching(blk_count, 4, p))]
    reduce_sum x2 -> x0, other arithmetic: 1.81 us -> none  [the longest x1 0.93 us: slots(): rank_within = jnp.sum(same_before.astype(jnp.int32), axis=1)]
    ppermute x2, waiting for transfers between devices: 3.2 us -> 1.86 us  [body(): lax.ppermute(own_block, 'blk', matching(blk_count, 2, p))]
    all_to_all x1, blocking collectives: 46.6 us -> 47.9 us  [body(): got = lax.all_to_all(packed, 'blk', split_axis=0, concat_axis=0, tiled=True)]
    ppermute x2, starting transfers between devices: 5.53 us -> 4.4 us  [body(): lax.ppermute(own_block, 'blk', matching(blk_count, 2, p))]
  transfers between devices with their start and end apart: 9 -> 10, of which waited for: 3 -> 3; matrix products, arithmetic and copies ran while one was open for 6% -> 0% of each run, Pallas kernels for 9% -> 10%
where the time goes in v4:
time: 93.4 us; the launch traced here: 93.1 us
  blocking collectives  47.9 us (51%)
  Pallas kernels  15.8 us (17%)
  waiting for transfers between devices  11.9 us (13%)
  starting transfers between devices  10.3 us (11%)
  local copies, waits for them, and re-layouts  6.31 us (7%)
    all_to_all x1, blocking collectives, body(): got = lax.all_to_all(packed, 'blk', split_axis=0, concat_axis=0, tiled=True)  47.9 us
    pallas_call x7, Pallas kernels, call(): pl.pallas_call(kernel, out_shape=outs, in_specs=specs, out_specs=[pl.Bloc...  12.6 us
    ppermute x1, waiting for transfers between devices, body(): arrived = lax.ppermute(sent, 'map', [(0, 1), (1, 0)])  10 us
    ppermute x2, starting transfers between devices, body(): lax.ppermute(own_block, 'blk', matching(blk_count, 2, p))  4.4 us
    unnamed x20, local copies, waits for them, and re-layouts  4.26 us
    pallas_call x1, Pallas kernels, body(): pl.pallas_call(functools.partial(phase_kernel, map_count, STOPS * map_cou...  3.19 us
    ppermute x2, starting transfers between devices, body(): lax.ppermute(own_block, 'blk', matching(blk_count, 4, p))  3.15 us
  transfers between devices with their start and end apart: 10, of which 3 were waited for; matrix products, arithmetic and copies ran while one was open for 0% of the time, Pallas kernels for 10%

profile of v4, /device:TPU:32, one launch (start us, length us, event | category | flops | bytes accessed | tf_op | source)
XLA Modules:
  0.0 93.1 jit_solution(7765314826843428881)
XLA Ops:
  0.0 2.6 %collective-permute-start.3 = (bf16[128,1024]{1,0:T(8,128)(2,1)}, bf16[128,1024]{1,0:T(8,128)(2,1)S(1)}, u32[]{:S(2)}, u32[]{:S(2)}) collective-permute-start(bf16[128,1024]{1,0:T(8,128)(2,1)} %bitcast.12), channel_id=1, source_target_pairs={{8,16},{16,8},{24,32},{32,24},{40,48},{48,40},{56,64},{64,56},{72,... | collective-permute-start | bytes 786440 | tf_op jit(solution)/shard_map/ppermute | solution.py:311
  2.6 0.6 collective-permute-start.2
  3.2 3.4 %collective-permute-start.1 = (bf16[128,1024]{1,0:T(8,128)(2,1)}, bf16[128,1024]{1,0:T(8,128)(2,1)S(1)}, u32[]{:S(2)}, u32[]{:S(2)}) collective-permute-start(bf16[128,1024]{1,0:T(8,128)(2,1)} %bitcast.14), channel_id=1, source_target_pairs={{4,8},{8,4},{12,16},{16,12},{20,24},{24,20},{28,32},{32,28},{36,40... | collective-permute-start | bytes 786440 | tf_op jit(solution)/shard_map/ppermute | solution.py:310
  6.6 1.0 %collective-permute-start = (bf16[128,1024]{1,0:T(8,128)(2,1)}, bf16[128,1024]{1,0:T(8,128)(2,1)S(1)}, u32[]{:S(2)}, u32[]{:S(2)}) collective-permute-start(bf16[128,1024]{1,0:T(8,128)(2,1)} %bitcast.15), channel_id=1, source_target_pairs={{0,4},{4,0},{8,12},{12,8},{16,20},{20,16},{24,28},{28,24},{32,36},... | collective-permute-start | bytes 786440 | tf_op jit(solution)/shard_map/ppermute | solution.py:310
  8.3 3.2 %shard_map.100 = (f32[2,128,512]{2,1,0:T(8,128)S(1)}, f32[2,128,512]{2,1,0:T(8,128)S(1)}, f32[2,128,512]{2,1,0:T(8,128)S(1)}, f32[2,128,512]{2,1,0:T(8,128)S(1)}...) custom-call(s32[5]{0:T(128)S(1)} %stack.23.facts, f32[1]{0:T(128)S(6)} %copy.11.curvature), custom_call_target="tpu_custom_call" | custom-call | flops 4194304 | bytes 4194304 | tf_op jit(solution)/shard_map/pallas_call | solution.py:316
  11.5 1.6 %copy-done = bf16[1024,1024]{1,0:T(8,128)(2,1)S(1)} copy-done((bf16[1024,1024]{1,0:T(8,128)(2,1)S(1)}, bf16[1024,1024]{1,0:T(8,128)(2,1)}, u32[]{:S(2)}) %copy-start) | copy-done | bytes 2097176
  13.1 1.6 %copy-done.4 = bf16[4,512,512]{2,1,0:T(8,128)(2,1)S(1)} copy-done((bf16[4,512,512]{2,1,0:T(8,128)(2,1)S(1)}, bf16[4,512,512]{2,1,0:T(8,128)(2,1)}, u32[]{:S(2)}) %copy-start.4) | copy-done | bytes 2097176
  14.7 0.9 %copy-done.5 = bf16[1,1,128,1024]{3,2,1,0:T(8,128)(2,1)S(1)} copy-done((bf16[1,1,128,1024]{3,2,1,0:T(8,128)(2,1)S(1)}, bf16[1,1,128,1024]{3,2,1,0:T(8,128)(2,1)}, u32[]{:S(2)}) %copy-start.5) | copy-done | bytes 262168
  15.7 2.0 %shard_map.101.before = f32[512,1024]{1,0:T(8,128)S(1)} custom-call(s32[5]{0:T(128)S(1)} %stack.23.facts, bf16[128,1024]{1,0:T(8,128)(2,1)S(1)} %bitcast.16, bf16[128,1024]{1,0:T(8,128)(2,1)S(1)} %collective-permute-done.4.twin, f32[2,128,512]{2,1,0:T(8,128)S(1)} %get-tuple-element.29.cosines, f32[2,128,512]{2,1,0:T(8,128)S(1)} %get-tuple-element.30.sines, ...), custom_call_target="tpu_custom_call" | custom-call | flops 1073741824 | bytes 7864340 | tf_op jit(solution)/shard_map/pallas_call | solution.py:76
  17.7 1.5 %collective-permute-done.1.near_b = bf16[128,1024]{1,0:T(8,128)(2,1)S(1)} collective-permute-done((bf16[128,1024]{1,0:T(8,128)(2,1)}, bf16[128,1024]{1,0:T(8,128)(2,1)S(1)}, u32[]{:S(2)}, u32[]{:S(2)}) %collective-permute-start.1) | collective-permute-done | bytes 262176 | tf_op jit(solution)/shard_map/ppermute | solution.py:310
  19.2 0.3 collective-permute-done.near_a
  19.6 0.5 collective-permute-start.6
  20.1 0.5 collective-permute-start.8
  20.6 2.0 %shard_map.102.before = f32[512,1024]{1,0:T(8,128)S(1)} custom-call(s32[5]{0:T(128)S(1)} %stack.23.facts, bf16[128,1024]{1,0:T(8,128)(2,1)S(1)} %collective-permute-done.near_a, bf16[128,1024]{1,0:T(8,128)(2,1)S(1)} %collective-permute-done.1.near_b, f32[2,128,512]{2,1,0:T(8,128)S(1)} %get-tuple-element.35.cosines, ...), custom_call_target="tpu_custom_call" | custom-call | flops 1073741824 | bytes 9961492 | tf_op jit(solution)/shard_map/pallas_call | solution.py:76
  22.8 2.6 %shard_map.103 = (bf16[256,1024]{1,0:T(8,128)(2,1)S(1)}, bf16[1024,1024]{1,0:T(8,128)(2,1)S(1)}) custom-call(s32[5]{0:T(128)S(1)} %stack.23.facts, bf16[128,1024]{1,0:T(8,128)(2,1)S(1)} %collective-permute-done.5.twin_near_a, bf16[128,1024]{1,0:T(8,128)(2,1)S(1)} %collective-permute-done.6.twin_near_b, bf16[128,1024]{1,0:T(8,128)(2,1)S(1)} %collective-permute-done.2.far_a, ...), custom_call_target="tpu_custom_call" | custom-call | flops 2147483648 | bytes 14680084 | tf_op jit(solution)/shard_map/pallas_call | solution.py:76
  25.4 1.8 %collective-permute-start.9 = (bf16[256,1024]{1,0:T(8,128)(2,1)S(1)}, bf16[256,1024]{1,0:T(8,128)(2,1)S(1)}, u32[]{:S(2)}, u32[]{:S(2)}) collective-permute-start(bf16[256,1024]{1,0:T(8,128)(2,1)S(1)} %get-tuple-element.48), channel_id=1, source_target_pairs={{0,1},{1,0},{2,3},{3,2},{4,5},{5,4},{6,7},{7,6},{8,9},{9,8},{10,11... | collective-permute-start | bytes 1572872 | tf_op jit(solution)/shard_map/ppermute | solution.py:368
  27.2 1.3 %shard_map.104.kept = f32[256,1024]{1,0:T(8,128)S(1)} custom-call(s32[5]{0:T(128)S(1)} %stack.23.facts, bf16[1024,1024]{1,0:T(8,128)(2,1)S(1)} %get-tuple-element.47.right_side, bf16[4,512,1024]{2,1,0:T(8,128)(2,1)S(1)} %copy-done.2, f32[512,1024]{1,0:T(8,128)S(1)} %shard_map.102.before), custom_call_target="tpu_custom_call" | custom-call | tf_op jit(solution)/shard_map/pallas_call | solution.py:76
  28.6 0.9 %shard_map.105 = (bf16[2,256,256]{2,1,0:T(8,128)(2,1)S(1)}, bf16[256,128]{1,0:T(8,128)(2,1)S(1)}) custom-call(s32[5]{0:T(128)S(1)} %stack.23.facts, s32[1,256]{1,0:T(1,128)S(1)} %bitcast.17, s32[1,256]{1,0:T(1,128)S(1)} %bitcast.18, s32[1,128]{1,0:T(1,128)S(1)} %bitcast.19), custom_call_target="tpu_custom_call" | custom-call | tf_op jit(solution)/shard_map/pallas_call | solution.py:76
  29.5 10.0 %collective-permute-done.9.arrived = bf16[256,1024]{1,0:T(8,128)(2,1)S(1)} collective-permute-done((bf16[256,1024]{1,0:T(8,128)(2,1)S(1)}, bf16[256,1024]{1,0:T(8,128)(2,1)S(1)}, u32[]{:S(2)}, u32[]{:S(2)}) %collective-permute-start.9) | collective-permute-done | bytes 524320 | tf_op jit(solution)/shard_map/ppermute | solution.py:368
  39.5 1.0 %shard_map.106 = bf16[256,2176]{1,0:T(8,128)(2,1)S(1)} custom-call(s32[5]{0:T(128)S(1)} %stack.23.facts, f32[256,1024]{1,0:T(8,128)S(1)} %shard_map.104.kept, bf16[256,1024]{1,0:T(8,128)(2,1)S(1)} %collective-permute-done.9.arrived, bf16[2,256,256]{2,1,0:T(8,128)(2,1)S(1)} %get-tuple-element.51.slot_hot, bf16[256,128]{1,0:T(8,128)(2,1)S(1)} %get-tuple-element.52.marks), custom_call_target="tpu_custom_call" | custom-call | flops 285212672 | bytes 3014676 | tf_op jit(solution)/shard_map/pallas_call | solution.py:76
  40.5 0.5 reshape.21
  41.0 47.9 %all_to_all.5 = bf16[128,2,2176]{2,1,0:T(2,128)(2,1)} all-to-all(bf16[128,2,2176]{2,1,0:T(2,128)(2,1)S(1)} %reshape.21), channel_id=1, replica_groups=mesh['blk'=128,'map'=2] {'blk'}, dimensions={0} | all-to-all | bytes 2228224 | tf_op jit(solution)/shard_map/all_to_all | solution.py:397
  89.0 1.5 %reshape.22.got = bf16[256,2176]{1,0:T(8,128)(2,1)S(1)} reshape(bf16[128,2,2176]{2,1,0:T(2,128)(2,1)} %all_to_all.5) | data formatting | bytes 2228224 | tf_op jit(solution)/shard_map/reshape | solution.py:401
  90.5 2.6 %shard_map.107 = f32[256,512]{1,0:T(8,128)} custom-call(s32[5]{0:T(128)S(1)} %stack.23.facts, bf16[256,2176]{1,0:T(8,128)(2,1)S(1)} %reshape.22.got, bf16[512,512]{1,0:T(8,128)(2,1)S(1)} %bitcast.20), custom_call_target="tpu_custom_call" | custom-call | flops 805306368 | bytes 2162708 | tf_op jit(solution)/shard_map/pallas_call | solution.py:76
  (28 shorter events, 0.3 us)
Async XLA Ops:
  0.0 11.5 %collective-permute-start.4 = (bf16[128,1024]{1,0:T(8,128)(2,1)}, bf16[128,1024]{1,0:T(8,128)(2,1)S(1)}, u32[]{:S(2)}, u32[]{:S(2)}) collective-permute-start(bf16[128,1024]{1,0:T(8,128)(2,1)} %bitcast.11), channel_id=1, source_target_pairs={{0,2},{2,0},{4,6},{6,4},{8,10},{10,8},{12,14},{14,12},{16,18},{18,... | collective-permute-start | bytes 786440 | tf_op jit(solution)/shard_map/ppermute | solution.py:293
  0.0 17.7 %collective-permute-start.3 = (bf16[128,1024]{1,0:T(8,128)(2,1)}, bf16[128,1024]{1,0:T(8,128)(2,1)S(1)}, u32[]{:S(2)}, u32[]{:S(2)}) collective-permute-start(bf16[128,1024]{1,0:T(8,128)(2,1)} %bitcast.12), channel_id=1, source_target_pairs={{8,16},{16,8},{24,32},{32,24},{40,48},{48,40},{56,64},{64,56},{72,... | collective-permute-start | bytes 786440 | tf_op jit(solution)/shard_map/ppermute | solution.py:311
  2.6 15.1 %collective-permute-start.2 = (bf16[128,1024]{1,0:T(8,128)(2,1)}, bf16[128,1024]{1,0:T(8,128)(2,1)S(1)}, u32[]{:S(2)}, u32[]{:S(2)}) collective-permute-start(bf16[128,1024]{1,0:T(8,128)(2,1)} %bitcast.13), channel_id=1, source_target_pairs={{0,8},{8,0},{16,24},{24,16},{32,40},{40,32},{48,56},{56,48},{64,72... | collective-permute-start | bytes 786440 | tf_op jit(solution)/shard_map/ppermute | solution.py:311
  3.2 16.1 %collective-permute-start.1 = (bf16[128,1024]{1,0:T(8,128)(2,1)}, bf16[128,1024]{1,0:T(8,128)(2,1)S(1)}, u32[]{:S(2)}, u32[]{:S(2)}) collective-permute-start(bf16[128,1024]{1,0:T(8,128)(2,1)} %bitcast.14), channel_id=1, source_target_pairs={{4,8},{8,4},{12,16},{16,12},{20,24},{24,20},{28,32},{32,28},{36,40... | collective-permute-start | bytes 786440 | tf_op jit(solution)/shard_map/ppermute | solution.py:310
  6.6 13.0 %collective-permute-start = (bf16[128,1024]{1,0:T(8,128)(2,1)}, bf16[128,1024]{1,0:T(8,128)(2,1)S(1)}, u32[]{:S(2)}, u32[]{:S(2)}) collective-permute-start(bf16[128,1024]{1,0:T(8,128)(2,1)} %bitcast.15), channel_id=1, source_target_pairs={{0,4},{4,0},{8,12},{12,8},{16,20},{20,16},{24,28},{28,24},{32,36},... | collective-permute-start | bytes 786440 | tf_op jit(solution)/shard_map/ppermute | solution.py:310
  11.5 1.6 %copy-start = (bf16[1024,1024]{1,0:T(8,128)(2,1)S(1)}, bf16[1024,1024]{1,0:T(8,128)(2,1)}, u32[]{:S(2)}) copy-start(bf16[1024,1024]{1,0:T(8,128)(2,1)} %constant.58.clone.ranges) | copy-start | bytes 6291460
  13.1 1.6 %copy-start.4 = (bf16[4,512,512]{2,1,0:T(8,128)(2,1)S(1)}, bf16[4,512,512]{2,1,0:T(8,128)(2,1)}, u32[]{:S(2)}) copy-start(bf16[4,512,512]{2,1,0:T(8,128)(2,1)} %constant.59.clone.tables) | copy-start | bytes 6291460
  14.7 0.9 %copy-start.5 = (bf16[1,1,128,1024]{3,2,1,0:T(8,128)(2,1)S(1)}, bf16[1,1,128,1024]{3,2,1,0:T(8,128)(2,1)}, u32[]{:S(2)}) copy-start(bf16[1,1,128,1024]{3,2,1,0:T(8,128)(2,1)} %param.10) | copy-start | bytes 786436
  15.6 4.9 %copy-start.1 = (bf16[1024,1024]{1,0:T(8,128)(2,1)S(1)}, bf16[1024,1024]{1,0:T(8,128)(2,1)}, u32[]{:S(2)}) copy-start(bf16[1024,1024]{1,0:T(8,128)(2,1)} %constant.58.clone.ranges) | copy-start | bytes 6291460
  15.7 4.9 %copy-start.3 = (bf16[4,512,512]{2,1,0:T(8,128)(2,1)S(1)}, bf16[4,512,512]{2,1,0:T(8,128)(2,1)}, u32[]{:S(2)}) copy-start(bf16[4,512,512]{2,1,0:T(8,128)(2,1)} %constant.60.clone.tables) | copy-start | bytes 6291460
  19.6 3.1 %collective-permute-start.5 = (bf16[128,1024]{1,0:T(8,128)(2,1)S(1)}, bf16[128,1024]{1,0:T(8,128)(2,1)S(1)}, u32[]{:S(2)}, u32[]{:S(2)}) collective-permute-start(bf16[128,1024]{1,0:T(8,128)(2,1)S(1)} %collective-permute-done.near_a), channel_id=1, source_target_pairs={{0,2},{2,0},{4,6},{6,4},{8,10},{10,8},{12,14},{14,12},{16,18},{18,... | collective-permute-start | bytes 786440 | tf_op jit(solution)/shard_map/ppermute | solution.py:293
  19.6 3.1 %collective-permute-start.6 = (bf16[128,1024]{1,0:T(8,128)(2,1)S(1)}, bf16[128,1024]{1,0:T(8,128)(2,1)S(1)}, u32[]{:S(2)}, u32[]{:S(2)}) collective-permute-start(bf16[128,1024]{1,0:T(8,128)(2,1)S(1)} %collective-permute-done.1.near_b), channel_id=1, source_target_pairs={{0,2},{2,0},{4,6},{6,4},{8,10},{10,8},{12,14},{14,12},{16,18},{18,... | collective-permute-start | bytes 786440 | tf_op jit(solution)/shard_map/ppermute | solution.py:293
  20.1 2.6 %collective-permute-start.7 = (bf16[128,1024]{1,0:T(8,128)(2,1)S(1)}, bf16[128,1024]{1,0:T(8,128)(2,1)S(1)}, u32[]{:S(2)}, u32[]{:S(2)}) collective-permute-start(bf16[128,1024]{1,0:T(8,128)(2,1)S(1)} %collective-permute-done.2.far_a), channel_id=1, source_target_pairs={{0,2},{2,0},{4,6},{6,4},{8,10},{10,8},{12,14},{14,12},{16,18},{18,... | collective-permute-start | bytes 786440 | tf_op jit(solution)/shard_map/ppermute | solution.py:293
  20.1 2.6 %collective-permute-start.8 = (bf16[128,1024]{1,0:T(8,128)(2,1)S(1)}, bf16[128,1024]{1,0:T(8,128)(2,1)S(1)}, u32[]{:S(2)}, u32[]{:S(2)}) collective-permute-start(bf16[128,1024]{1,0:T(8,128)(2,1)S(1)} %collective-permute-done.3.far_b), channel_id=1, source_target_pairs={{0,2},{2,0},{4,6},{6,4},{8,10},{10,8},{12,14},{14,12},{16,18},{18,... | collective-permute-start | bytes 786440 | tf_op jit(solution)/shard_map/ppermute | solution.py:293
  20.6 2.2 %copy-start.2 = (bf16[4,512,1024]{2,1,0:T(8,128)(2,1)S(1)}, bf16[4,512,1024]{2,1,0:T(8,128)(2,1)}, u32[]{:S(2)}) copy-start(bf16[4,512,1024]{2,1,0:T(8,128)(2,1)} %constant.61.clone.tables) | copy-start | bytes 12582916
  25.4 3.1 %copy-start.6 = (s32[1,1,256,1]{2,3,1,0:T(1,128)S(1)}, s32[1,1,256,1]{2,3,1,0:T(1,128)}, u32[]{:S(2)}) copy-start(s32[1,1,256,1]{2,3,1,0:T(1,128)} %param.13) | copy-start | bytes 3076
  25.4 3.1 %copy-start.7 = (s32[1,1,256]{2,1,0:T(1,128)S(1)}, s32[1,1,256]{2,1,0:T(1,128)}, u32[]{:S(2)}) copy-start(s32[1,1,256]{2,1,0:T(1,128)} %param.14) | copy-start | bytes 3076
  25.4 3.1 %copy-start.8 = (s32[128]{0:T(128)S(1)}, s32[128]{0:T(128)}, u32[]{:S(2)}) copy-start(s32[128]{0:T(128)} %param.15) | copy-start | bytes 1540
  25.4 14.1 %collective-permute-start.9 = (bf16[256,1024]{1,0:T(8,128)(2,1)S(1)}, bf16[256,1024]{1,0:T(8,128)(2,1)S(1)}, u32[]{:S(2)}, u32[]{:S(2)}) collective-permute-start(bf16[256,1024]{1,0:T(8,128)(2,1)S(1)} %get-tuple-element.48), channel_id=1, source_target_pairs={{0,1},{1,0},{2,3},{3,2},{4,5},{5,4},{6,7},{7,6},{8,9},{9,8},{10,11... | collective-permute-start | bytes 1572872 | tf_op jit(solution)/shard_map/ppermute | solution.py:368
  41.0 49.4 %copy-start.9 = (bf16[1,512,512]{2,1,0:T(8,128)(2,1)S(1)}, bf16[1,512,512]{2,1,0:T(8,128)(2,1)}, u32[]{:S(2)}) copy-start(bf16[1,512,512]{2,1,0:T(8,128)(2,1)} %param.12) | copy-start | bytes 1572868

commit v5 on v4

--- a/solution.py
+++ b/solution.py
@@ -84,7 +84,7 @@
     )(*operands)
 
 
-def phase_kernel(map_count, span, facts, curvature, *curves):
+def phase_factors(map_count, span, facts, curvature, curves):
     _, pulses, freqs = curves[0].shape
     width = freqs // 4
     core, here_map = facts[0], facts[3]
@@ -158,11 +158,25 @@
 
 
 def first_kernel(
-    facts, own, twin, cosines, sines, ranges, tables, total, phased, right_side, cross, arrival
+    map_count, span, facts, curvature, own_far, twin, tables, total, *rest
 ):
-    copy = fetch(facts, tables, cross, arrival)
+    later = 2 * len(GROUPS) - 2
+    cosines, sines, phased, right_side, cross, own, ranges, arrival, own_here, ranges_here = rest[
+        later:
+    ]
+    copies = [
+        pltpu.make_async_copy(own_far, own, own_here),
+        pltpu.make_async_copy(tables.at[facts[4], : ranges.shape[0]], ranges, ranges_here),
+        pltpu.make_async_copy(
+            tables.at[facts[4], ranges.shape[0] :, : cross.shape[1]], cross, arrival
+        ),
+    ]
+    for copy in copies:
+        copy.start()
+    phase_factors(map_count, span, facts, curvature, (cosines, sines, *rest[:later]))
+    for copy in copies:
+        copy.wait()
     transform([lambda: own[...], lambda: twin[...]], cosines, sines, ranges, phased, right_side)
-    copy.wait()
     total[...] = jnp.dot(cross[...], right_side[...], preferred_element_type=jnp.float32)
 
 
@@ -264,29 +278,29 @@
 
 def map_kernel(facts, got, weights, out):
     columns = weights.shape[0]
-    marks = got[:, 4 * columns :].astype(jnp.float32)
-    total = 0.0
+    pairs = got.shape[0]
+    parts = [got[:, n * columns : (n + 1) * columns] for n in range(4)]
+    mapped = jnp.dot(
+        jnp.concatenate(parts, axis=0), weights[...], preferred_element_type=jnp.float32
+    )
+    squared = mapped * mapped
+    marks = got[:, 4 * columns :].astype(jnp.float32).T
+    spots = lax.broadcasted_iota(jnp.int32, (MAPH, pairs), 0)
+    hots, pieces = [], []
     for part in range(2):
-        first = 2 * part * columns
-        real_out = jnp.dot(
-            got[:, first : first + columns], weights[...], preferred_element_type=jnp.float32
-        )
-        imag_out = jnp.dot(
-            got[:, first + columns : first + 2 * columns],
-            weights[...],
-            preferred_element_type=jnp.float32,
-        )
-        power = real_out * real_out + imag_out * imag_out
-        mark = marks[:, part * (SIDE // 2) : part * (SIDE // 2) + 1].astype(jnp.int32)
-        spots = lax.broadcasted_iota(jnp.int32, (power.shape[0], MAPH), 1)
-        hot = (mark == spots).astype(jnp.bfloat16)
+        real_out = squared[2 * part * pairs : (2 * part + 1) * pairs]
+        power = real_out + squared[(2 * part + 1) * pairs : (2 * part + 2) * pairs]
+        mark = marks[part * (SIDE // 2) : part * (SIDE // 2) + 1].astype(jnp.int32)
+        hot = (mark == spots).astype(jnp.float32).astype(jnp.bfloat16)
         high = power.astype(jnp.bfloat16)
         low = (power - high.astype(jnp.float32)).astype(jnp.bfloat16)
-        for piece in (low, high):
-            total += lax.dot_general(
-                hot, piece, (((0,), (0,)), ((), ())), preferred_element_type=jnp.float32
-            )
-    out[...] = total
+        hots += [hot, hot]
+        pieces += [low, high]
+    out[...] = jnp.dot(
+        jnp.concatenate(hots, axis=1),
+        jnp.concatenate(pieces, axis=0),
+        preferred_element_type=jnp.float32,
+    )
 
 
 def swap(block, count):
@@ -313,14 +327,6 @@
 
     f32 = lambda *shape: jax.ShapeDtypeStruct(shape, jnp.float32)
     b16 = lambda *shape: jax.ShapeDtypeStruct(shape, jnp.bfloat16)
-    curves = pl.pallas_call(
-        functools.partial(phase_kernel, map_count, STOPS * map_count * pulse_count),
-        out_shape=[f32(n, pulse_count, freq_count) for n in GROUPS for _ in range(2)],
-        in_specs=[pl.BlockSpec(memory_space=pltpu.SMEM)] * 2,
-        out_specs=[pl.BlockSpec(memory_space=pltpu.VMEM)] * (2 * len(GROUPS)),
-        compiler_params=pltpu.CompilerParams(vmem_limit_bytes=16 * 2**20),
-        cost_estimate=pl.CostEstimate(flops=2**22, bytes_accessed=2**22, transcendentals=2**18),
-    )(facts, tile_curvature)
     deep = 2 * pulse_count
     image_shape = (map_count * rows_here, 2 * columns)
     half_shape = (rows_here, 2 * columns)
@@ -332,22 +338,35 @@
     ]
     flops = lambda n: 2 * n * pulse_count * 4 * columns * (freq_count + map_count * rows_here)
     n = GROUPS[0]
-    [total] = call(
-        first_kernel,
-        [f32(*image_shape)],
-        [facts, own_block, twin, *curves[:2], ranges, crosses[0]],
-        [spread(n), right(n), *table(n)],
-        flops(n),
-        far=(6,),
-    )
-    near, far, total = lax.optimization_barrier((near, far, total))
+    smem, vmem, hbm = (
+        pl.BlockSpec(memory_space=kind) for kind in (pltpu.SMEM, pltpu.VMEM, pltpu.HBM)
+    )
+    total, *curves = pl.pallas_call(
+        functools.partial(first_kernel, map_count, STOPS * map_count * pulse_count),
+        out_shape=[f32(*image_shape)]
+        + [f32(size, pulse_count, freq_count) for size in GROUPS[1:] for _ in range(2)],
+        in_specs=[smem, smem, hbm, vmem, hbm],
+        out_specs=[vmem] * (2 * len(GROUPS) - 1),
+        scratch_shapes=[pltpu.VMEM((n, pulse_count, freq_count), jnp.float32)] * 2
+        + [
+            spread(n),
+            right(n),
+            table(n)[0],
+            pltpu.VMEM(own_block.shape, jnp.bfloat16),
+            pltpu.VMEM(ranges.shape, jnp.bfloat16),
+        ]
+        + [pltpu.SemaphoreType.DMA] * 3,
+        compiler_params=pltpu.CompilerParams(vmem_limit_bytes=44 * 2**20),
+        cost_estimate=pl.CostEstimate(flops=flops(n), bytes_accessed=0, transcendentals=2**18),
+    )(facts, tile_curvature, own_block, twin, crosses[0])
+    far, near, total = lax.optimization_barrier((far, near, total))
     twin_near = [swap(block, blk_count) for block in near]
     twin_far = [swap(block, blk_count) for block in far]
     n = GROUPS[1]
     [total] = call(
         second_kernel,
         [f32(*image_shape)],
-        [facts, *near, *curves[2:4], ranges, crosses[1], total],
+        [facts, *near, *curves[:2], ranges, crosses[1], total],
         [spread(n), right(n), *table(n)],
         flops(n),
         far=(6,),
@@ -357,7 +376,7 @@
     sent, right_side = call(
         last_kernel,
         [b16(*half_shape), b16(n * deep, 2 * columns)],
-        [facts, *twin_near, *far, *twin_far, *curves[4:], ranges, crosses[2], total],
+        [facts, *twin_near, *far, *twin_far, *curves[2:], ranges, crosses[2], total],
         [spread(n), *table(n)],
         flops(n),
         far=(10,),
@@ -419,10 +438,11 @@
     def run(*args):
         map_count, pulse_count, width = args[0].shape[1:]
         ranges = jnp.asarray(range_table(width // 2))
-        crosses = [
-            jnp.asarray(table)
-            for table in cross_tables(map_count, map_count * args[3].shape[2], pulse_count)
-        ]
+        crosses = cross_tables(map_count, map_count * args[3].shape[2], pulse_count)
+        first = np.zeros((len(crosses[0]), width + crosses[0].shape[1], width), crosses[0].dtype)
+        first[:, : width] = range_table(width // 2)
+        first[:, width : , : crosses[0].shape[2]] = crosses[0]
+        crosses = [jnp.asarray(table) for table in (first, *crosses[1:])]
         held = lambda *here: body(ranges, crosses, *here)
         return jax.shard_map(
             held, mesh=mesh, in_specs=in_specs, out_specs=out_specs, check_vma=False

time: 93.4 us -> 93.3 us (level)
  waiting for transfers between devices: 11.9 us -> 16.7 us
  local copies, waits for them, and re-layouts: 6.31 us -> 3.28 us
  starting transfers between devices: 10.3 us -> 9.07 us
    ppermute x2, waiting for transfers between devices: 1.86 us -> 5.46 us  [body(): lax.ppermute(own_block, 'blk', matching(blk_count, 2, p))]
    unnamed x20 -> x16, local copies, waits for them, and re-layouts: 4.26 us -> 1.23 us
    pallas_call x7 -> x6, Pallas kernels: 12.6 us -> 10.3 us  [call(): pl.pallas_call(kernel, out_shape=outs, in_specs=specs, out_specs=[pl.Bloc...]
    pallas_call x1, Pallas kernels: 3.19 us -> 5.44 us  [body(): pl.pallas_call(functools.partial(first_kernel, map_count, STOPS * map_cou...]
    ppermute x1, waiting for transfers between devices: 10 us -> 11.2 us  [body(): arrived = lax.ppermute(sent, 'map', [(0, 1), (1, 0)])]
    ppermute x1, starting transfers between devices: 1.76 us -> 0.65 us  [body(): arrived = lax.ppermute(sent, 'map', [(0, 1), (1, 0)])]
where the time goes in v5:
time: 93.3 us; the launch traced here: 93.1 us
  blocking collectives  47.5 us (51%)
  waiting for transfers between devices  16.7 us (18%)
  Pallas kernels  15.7 us (17%)
  starting transfers between devices  9.07 us (10%)
  local copies, waits for them, and re-layouts  3.28 us (4%)
    all_to_all x1, blocking collectives, body(): got = lax.all_to_all(packed, 'blk', split_axis=0, concat_axis=0, tiled=True)  47.5 us
    ppermute x1, waiting for transfers between devices, body(): arrived = lax.ppermute(sent, 'map', [(0, 1), (1, 0)])  11.2 us
    pallas_call x6, Pallas kernels, call(): pl.pallas_call(kernel, out_shape=outs, in_specs=specs, out_specs=[pl.Bloc...  10.3 us
    ppermute x2, waiting for transfers between devices, body(): lax.ppermute(own_block, 'blk', matching(blk_count, 2, p))  5.46 us
    pallas_call x1, Pallas kernels, body(): pl.pallas_call(functools.partial(first_kernel, map_count, STOPS * map_cou...  5.44 us
    ppermute x2, starting transfers between devices, body(): lax.ppermute(own_block, 'blk', matching(blk_count, 2, p))  5.02 us
    ppermute x2, starting transfers between devices, body(): lax.ppermute(own_block, 'blk', matching(blk_count, 4, p))  2.38 us
  transfers between devices with their start and end apart: 10, of which 3 were waited for; matrix products, arithmetic and copies ran while one was open for 0% of the time, Pallas kernels for 10%

profile of v5, /device:TPU:32, one launch (start us, length us, event | category | flops | bytes accessed | tf_op | source)
XLA Modules:
  0.0 93.1 jit_solution(14994374313800038446)
XLA Ops:
  0.0 5.0 %collective-permute-start.3 = (bf16[128,1024]{1,0:T(8,128)(2,1)}, bf16[128,1024]{1,0:T(8,128)(2,1)S(1)}, u32[]{:S(2)}, u32[]{:S(2)}) collective-permute-start(bf16[128,1024]{1,0:T(8,128)(2,1)} %bitcast.12), channel_id=1, source_target_pairs={{4,8},{8,4},{12,16},{16,12},{20,24},{24,20},{28,32},{32,28},{36,40... | collective-permute-start | bytes 786440 | tf_op jit(solution)/shard_map/ppermute | solution.py:324
  5.0 2.1 %collective-permute-start.1 = (bf16[128,1024]{1,0:T(8,128)(2,1)}, bf16[128,1024]{1,0:T(8,128)(2,1)S(1)}, u32[]{:S(2)}, u32[]{:S(2)}) collective-permute-start(bf16[128,1024]{1,0:T(8,128)(2,1)} %bitcast.14), channel_id=1, source_target_pairs={{8,16},{16,8},{24,32},{32,24},{40,48},{48,40},{56,64},{64,56},{72,... | collective-permute-start | bytes 786440 | tf_op jit(solution)/shard_map/ppermute | solution.py:325
  7.1 0.3 collective-permute-start
  8.1 0.1 stack.23.facts
  8.2 1.1 %copy-done.3 = bf16[1,1,128,1024]{3,2,1,0:T(8,128)(2,1)S(1)} copy-done((bf16[1,1,128,1024]{3,2,1,0:T(8,128)(2,1)S(1)}, bf16[1,1,128,1024]{3,2,1,0:T(8,128)(2,1)}, u32[]{:S(2)}) %copy-start.3) | copy-done | bytes 262168
  9.3 5.4 %shard_map.100 = (f32[512,1024]{1,0:T(8,128)S(1)}, f32[2,128,512]{2,1,0:T(8,128)S(1)}, f32[2,128,512]{2,1,0:T(8,128)S(1)}, f32[4,128,512]{2,1,0:T(8,128)S(1)}, f32[4,128,512]{2,1,0:T(8,128)S(1)}) custom-call(s32[5]{0:T(128)S(1)} %stack.23.facts, f32[1]{0:T(128)S(6)} %copy.11.curvature, bf16[128,1024]{1,0:T(8,128)(2,1)S(1)} %bitcast.16, ...), custom_call_target="tpu_custom_call" | custom-call | flops 1073741824 | tf_op jit(solution)/shard_map/pallas_call | solution.py:344
  14.7 1.1 %collective-permute-done.3.near_b = bf16[128,1024]{1,0:T(8,128)(2,1)S(1)} collective-permute-done((bf16[128,1024]{1,0:T(8,128)(2,1)}, bf16[128,1024]{1,0:T(8,128)(2,1)S(1)}, u32[]{:S(2)}, u32[]{:S(2)}) %collective-permute-start.3) | collective-permute-done | bytes 262176 | tf_op jit(solution)/shard_map/ppermute | solution.py:324
  15.8 4.4 %collective-permute-done.2.near_a = bf16[128,1024]{1,0:T(8,128)(2,1)S(1)} collective-permute-done((bf16[128,1024]{1,0:T(8,128)(2,1)}, bf16[128,1024]{1,0:T(8,128)(2,1)S(1)}, u32[]{:S(2)}, u32[]{:S(2)}) %collective-permute-start.2) | collective-permute-done | bytes 262176 | tf_op jit(solution)/shard_map/ppermute | solution.py:324
  20.2 0.5 collective-permute-start.6
  20.7 0.1 collective-permute-start.7
  20.8 0.4 collective-permute-start.8
  21.2 2.0 %shard_map.101.before = f32[512,1024]{1,0:T(8,128)S(1)} custom-call(s32[5]{0:T(128)S(1)} %stack.23.facts, bf16[128,1024]{1,0:T(8,128)(2,1)S(1)} %collective-permute-done.2.near_a, bf16[128,1024]{1,0:T(8,128)(2,1)S(1)} %collective-permute-done.3.near_b, f32[2,128,512]{2,1,0:T(8,128)S(1)} %get-tuple-element.33.cosines, ...), custom_call_target="tpu_custom_call" | custom-call | flops 1073741824 | bytes 9961492 | tf_op jit(solution)/shard_map/pallas_call | solution.py:76
  23.3 0.1 copy-done
  23.4 2.6 %shard_map.102 = (bf16[256,1024]{1,0:T(8,128)(2,1)S(1)}, bf16[1024,1024]{1,0:T(8,128)(2,1)S(1)}) custom-call(s32[5]{0:T(128)S(1)} %stack.23.facts, bf16[128,1024]{1,0:T(8,128)(2,1)S(1)} %collective-permute-done.5.twin_near_a, bf16[128,1024]{1,0:T(8,128)(2,1)S(1)} %collective-permute-done.6.twin_near_b, bf16[128,1024]{1,0:T(8,128)(2,1)S(1)} %collective-permute-done.far_a, ...), custom_call_target="tpu_custom_call" | custom-call | flops 2147483648 | bytes 14680084 | tf_op jit(solution)/shard_map/pallas_call | solution.py:76
  26.0 0.0 copy-start.4
  26.1 0.6 collective-permute-start.9
  26.7 1.3 %shard_map.103.kept = f32[256,1024]{1,0:T(8,128)S(1)} custom-call(s32[5]{0:T(128)S(1)} %stack.23.facts, bf16[1024,1024]{1,0:T(8,128)(2,1)S(1)} %get-tuple-element.45.right_side, bf16[4,512,1024]{2,1,0:T(8,128)(2,1)S(1)} %copy-done, f32[512,1024]{1,0:T(8,128)S(1)} %shard_map.101.before), custom_call_target="tpu_custom_call" | custom-call | tf_op jit(solution)/shard_map/pallas_call | solution.py:76
  28.1 0.9 %shard_map.104 = (bf16[2,256,256]{2,1,0:T(8,128)(2,1)S(1)}, bf16[256,128]{1,0:T(8,128)(2,1)S(1)}) custom-call(s32[5]{0:T(128)S(1)} %stack.23.facts, s32[1,256]{1,0:T(1,128)S(1)} %bitcast.17, s32[1,256]{1,0:T(1,128)S(1)} %bitcast.18, s32[1,128]{1,0:T(1,128)S(1)} %bitcast.19), custom_call_target="tpu_custom_call" | custom-call | tf_op jit(solution)/shard_map/pallas_call | solution.py:76
  29.0 11.2 %collective-permute-done.9.arrived = bf16[256,1024]{1,0:T(8,128)(2,1)S(1)} collective-permute-done((bf16[256,1024]{1,0:T(8,128)(2,1)S(1)}, bf16[256,1024]{1,0:T(8,128)(2,1)S(1)}, u32[]{:S(2)}, u32[]{:S(2)}) %collective-permute-start.9) | collective-permute-done | bytes 524320 | tf_op jit(solution)/shard_map/ppermute | solution.py:387
  40.2 1.0 %shard_map.105 = bf16[256,2176]{1,0:T(8,128)(2,1)S(1)} custom-call(s32[5]{0:T(128)S(1)} %stack.23.facts, f32[256,1024]{1,0:T(8,128)S(1)} %shard_map.103.kept, bf16[256,1024]{1,0:T(8,128)(2,1)S(1)} %collective-permute-done.9.arrived, bf16[2,256,256]{2,1,0:T(8,128)(2,1)S(1)} %get-tuple-element.49.slot_hot, bf16[256,128]{1,0:T(8,128)(2,1)S(1)} %get-tuple-element.50.marks), custom_call_target="tpu_custom_call" | custom-call | flops 285212672 | bytes 3014676 | tf_op jit(solution)/shard_map/pallas_call | solution.py:76
  41.2 0.5 reshape.21
  41.7 47.5 %all_to_all.5 = bf16[128,2,2176]{2,1,0:T(2,128)(2,1)} all-to-all(bf16[128,2,2176]{2,1,0:T(2,128)(2,1)S(1)} %reshape.21), channel_id=1, replica_groups=mesh['blk'=128,'map'=2] {'blk'}, dimensions={0} | all-to-all | bytes 2228224 | tf_op jit(solution)/shard_map/all_to_all | solution.py:416
  89.2 1.5 %reshape.22.got = bf16[256,2176]{1,0:T(8,128)(2,1)S(1)} reshape(bf16[128,2,2176]{2,1,0:T(2,128)(2,1)} %all_to_all.5) | data formatting | bytes 2228224 | tf_op jit(solution)/shard_map/reshape | solution.py:420
  90.7 2.4 %shard_map.106 = f32[256,512]{1,0:T(8,128)} custom-call(s32[5]{0:T(128)S(1)} %stack.23.facts, bf16[256,2176]{1,0:T(8,128)(2,1)S(1)} %reshape.22.got, bf16[512,512]{1,0:T(8,128)(2,1)S(1)} %bitcast.20), custom_call_target="tpu_custom_call" | custom-call | flops 805306368 | bytes 2162708 | tf_op jit(solution)/shard_map/pallas_call | solution.py:76
  (23 shorter events, 0.1 us)
Async XLA Ops:
  0.0 8.2 %collective-permute-start.4 = (bf16[128,1024]{1,0:T(8,128)(2,1)}, bf16[128,1024]{1,0:T(8,128)(2,1)S(1)}, u32[]{:S(2)}, u32[]{:S(2)}) collective-permute-start(bf16[128,1024]{1,0:T(8,128)(2,1)} %bitcast.11), channel_id=1, source_target_pairs={{0,2},{2,0},{4,6},{6,4},{8,10},{10,8},{12,14},{14,12},{16,18},{18,... | collective-permute-start | bytes 786440 | tf_op jit(solution)/shard_map/ppermute | solution.py:307
  0.0 15.8 %collective-permute-start.3 = (bf16[128,1024]{1,0:T(8,128)(2,1)}, bf16[128,1024]{1,0:T(8,128)(2,1)S(1)}, u32[]{:S(2)}, u32[]{:S(2)}) collective-permute-start(bf16[128,1024]{1,0:T(8,128)(2,1)} %bitcast.12), channel_id=1, source_target_pairs={{4,8},{8,4},{12,16},{16,12},{20,24},{24,20},{28,32},{32,28},{36,40... | collective-permute-start | bytes 786440 | tf_op jit(solution)/shard_map/ppermute | solution.py:324
  5.0 15.2 %collective-permute-start.2 = (bf16[128,1024]{1,0:T(8,128)(2,1)}, bf16[128,1024]{1,0:T(8,128)(2,1)S(1)}, u32[]{:S(2)}, u32[]{:S(2)}) collective-permute-start(bf16[128,1024]{1,0:T(8,128)(2,1)} %bitcast.13), channel_id=1, source_target_pairs={{0,4},{4,0},{8,12},{12,8},{16,20},{20,16},{24,28},{28,24},{32,36},... | collective-permute-start | bytes 786440 | tf_op jit(solution)/shard_map/ppermute | solution.py:324
  5.0 15.2 %collective-permute-start.1 = (bf16[128,1024]{1,0:T(8,128)(2,1)}, bf16[128,1024]{1,0:T(8,128)(2,1)S(1)}, u32[]{:S(2)}, u32[]{:S(2)}) collective-permute-start(bf16[128,1024]{1,0:T(8,128)(2,1)} %bitcast.14), channel_id=1, source_target_pairs={{8,16},{16,8},{24,32},{32,24},{40,48},{48,40},{56,64},{64,56},{72,... | collective-permute-start | bytes 786440 | tf_op jit(solution)/shard_map/ppermute | solution.py:325
  7.1 13.1 %collective-permute-start = (bf16[128,1024]{1,0:T(8,128)(2,1)}, bf16[128,1024]{1,0:T(8,128)(2,1)S(1)}, u32[]{:S(2)}, u32[]{:S(2)}) collective-permute-start(bf16[128,1024]{1,0:T(8,128)(2,1)} %bitcast.15), channel_id=1, source_target_pairs={{0,8},{8,0},{16,24},{24,16},{32,40},{40,32},{48,56},{56,48},{64,72... | collective-permute-start | bytes 786440 | tf_op jit(solution)/shard_map/ppermute | solution.py:325
  8.2 13.1 %copy-start.1 = (bf16[1024,1024]{1,0:T(8,128)(2,1)S(1)}, bf16[1024,1024]{1,0:T(8,128)(2,1)}, u32[]{:S(2)}) copy-start(bf16[1024,1024]{1,0:T(8,128)(2,1)} %constant.59.clone.ranges) | copy-start | bytes 6291460
  8.2 13.1 %copy-start.2 = (bf16[4,512,512]{2,1,0:T(8,128)(2,1)S(1)}, bf16[4,512,512]{2,1,0:T(8,128)(2,1)}, u32[]{:S(2)}) copy-start(bf16[4,512,512]{2,1,0:T(8,128)(2,1)} %constant.60.clone.tables) | copy-start | bytes 6291460
  8.2 1.1 %copy-start.3 = (bf16[1,1,128,1024]{3,2,1,0:T(8,128)(2,1)S(1)}, bf16[1,1,128,1024]{3,2,1,0:T(8,128)(2,1)}, u32[]{:S(2)}) copy-start(bf16[1,1,128,1024]{3,2,1,0:T(8,128)(2,1)} %param.10) | copy-start | bytes 786436
  20.2 3.1 %collective-permute-start.5 = (bf16[128,1024]{1,0:T(8,128)(2,1)S(1)}, bf16[128,1024]{1,0:T(8,128)(2,1)S(1)}, u32[]{:S(2)}, u32[]{:S(2)}) collective-permute-start(bf16[128,1024]{1,0:T(8,128)(2,1)S(1)} %collective-permute-done.2.near_a), channel_id=1, source_target_pairs={{0,2},{2,0},{4,6},{6,4},{8,10},{10,8},{12,14},{14,12},{16,18},{18,... | collective-permute-start | bytes 786440 | tf_op jit(solution)/shard_map/ppermute | solution.py:307
  20.2 3.1 %collective-permute-start.6 = (bf16[128,1024]{1,0:T(8,128)(2,1)S(1)}, bf16[128,1024]{1,0:T(8,128)(2,1)S(1)}, u32[]{:S(2)}, u32[]{:S(2)}) collective-permute-start(bf16[128,1024]{1,0:T(8,128)(2,1)S(1)} %collective-permute-done.3.near_b), channel_id=1, source_target_pairs={{0,2},{2,0},{4,6},{6,4},{8,10},{10,8},{12,14},{14,12},{16,18},{18,... | collective-permute-start | bytes 786440 | tf_op jit(solution)/shard_map/ppermute | solution.py:307
  20.7 2.6 %collective-permute-start.7 = (bf16[128,1024]{1,0:T(8,128)(2,1)S(1)}, bf16[128,1024]{1,0:T(8,128)(2,1)S(1)}, u32[]{:S(2)}, u32[]{:S(2)}) collective-permute-start(bf16[128,1024]{1,0:T(8,128)(2,1)S(1)} %collective-permute-done.far_a), channel_id=1, source_target_pairs={{0,2},{2,0},{4,6},{6,4},{8,10},{10,8},{12,14},{14,12},{16,18},{18,... | collective-permute-start | bytes 786440 | tf_op jit(solution)/shard_map/ppermute | solution.py:307
  20.8 2.5 %collective-permute-start.8 = (bf16[128,1024]{1,0:T(8,128)(2,1)S(1)}, bf16[128,1024]{1,0:T(8,128)(2,1)S(1)}, u32[]{:S(2)}, u32[]{:S(2)}) collective-permute-start(bf16[128,1024]{1,0:T(8,128)(2,1)S(1)} %collective-permute-done.1.far_b), channel_id=1, source_target_pairs={{0,2},{2,0},{4,6},{6,4},{8,10},{10,8},{12,14},{14,12},{16,18},{18,... | collective-permute-start | bytes 786440 | tf_op jit(solution)/shard_map/ppermute | solution.py:307
  21.2 2.2 %copy-start = (bf16[4,512,1024]{2,1,0:T(8,128)(2,1)S(1)}, bf16[4,512,1024]{2,1,0:T(8,128)(2,1)}, u32[]{:S(2)}) copy-start(bf16[4,512,1024]{2,1,0:T(8,128)(2,1)} %constant.61.clone.tables) | copy-start | bytes 12582916
  26.0 2.0 %copy-start.4 = (s32[1,1,256,1]{2,3,1,0:T(1,128)S(1)}, s32[1,1,256,1]{2,3,1,0:T(1,128)}, u32[]{:S(2)}) copy-start(s32[1,1,256,1]{2,3,1,0:T(1,128)} %param.13) | copy-start | bytes 3076
  26.0 2.0 %copy-start.5 = (s32[1,1,256]{2,1,0:T(1,128)S(1)}, s32[1,1,256]{2,1,0:T(1,128)}, u32[]{:S(2)}) copy-start(s32[1,1,256]{2,1,0:T(1,128)} %param.14) | copy-start | bytes 3076
  26.0 2.0 %copy-start.6 = (s32[128]{0:T(128)S(1)}, s32[128]{0:T(128)}, u32[]{:S(2)}) copy-start(s32[128]{0:T(128)} %param.15) | copy-start | bytes 1540
  26.1 14.2 %collective-permute-start.9 = (bf16[256,1024]{1,0:T(8,128)(2,1)S(1)}, bf16[256,1024]{1,0:T(8,128)(2,1)S(1)}, u32[]{:S(2)}, u32[]{:S(2)}) collective-permute-start(bf16[256,1024]{1,0:T(8,128)(2,1)S(1)} %get-tuple-element.46), channel_id=1, source_target_pairs={{0,1},{1,0},{2,3},{3,2},{4,5},{5,4},{6,7},{7,6},{8,9},{9,8},{10,11... | collective-permute-start | bytes 1572872 | tf_op jit(solution)/shard_map/ppermute | solution.py:387
  41.7 49.0 %copy-start.7 = (bf16[1,512,512]{2,1,0:T(8,128)(2,1)S(1)}, bf16[1,512,512]{2,1,0:T(8,128)(2,1)}, u32[]{:S(2)}) copy-start(bf16[1,512,512]{2,1,0:T(8,128)(2,1)} %param.12) | copy-start | bytes 1572868

commit v6 on v5

--- a/solution.py
+++ b/solution.py
@@ -30,15 +30,18 @@
     return pairs
 
 
-def range_table(freq_count):
+def range_tables(freq_count):
     index = np.arange(freq_count, dtype=np.int64)
-    angle = (index[:, None] * index[None, :] % freq_count).astype(np.float32) * np.float32(
-        2.0 * math.pi / freq_count
-    )
+    angle = (index[: freq_count // 2, None] * index[None, :] % freq_count).astype(
+        np.float32
+    ) * np.float32(2.0 * math.pi / freq_count)
     factor = np.float32(1.0 / math.sqrt(freq_count))
     real_part, imag_part = np.cos(angle) * factor, -np.sin(angle) * factor
-    table = np.block([[real_part, imag_part], [-imag_part, real_part]])
-    return table.astype(ml_dtypes.bfloat16)
+    tables = [
+        np.block([[real_part[:, p::2], imag_part[:, p::2]], [-imag_part[:, p::2], real_part[:, p::2]]])
+        for p in (0, 1)
+    ]
+    return np.concatenate(tables).astype(ml_dtypes.bfloat16)
 
 
 def stop_order(core):
@@ -68,9 +71,9 @@
 
 
 def call(kernel, outs, operands, scratch=(), flops=0, limit=24, far=()):
-    specs = [pl.BlockSpec(memory_space=pltpu.SMEM)] + [
+    specs = [
         pl.BlockSpec(memory_space=pltpu.HBM if n in far else pltpu.VMEM)
-        for n in range(1, len(operands))
+        for n in range(len(operands))
     ]
     size = sum(math.prod(a.shape) * a.dtype.itemsize for a in [*operands, *outs]) if flops else 0
     return pl.pallas_call(
@@ -84,10 +87,16 @@
     )(*operands)
 
 
-def phase_factors(map_count, span, facts, curvature, curves):
+def whereabouts():
+    here, here_map = lax.axis_index("blk"), lax.axis_index("map")
+    core = here % 2
+    return core, here // 2 % 2, here // 4 % 2, here_map, here_map * 2 + core
+
+
+def phase_factors(map_count, span, curvature, curves):
     _, pulses, freqs = curves[0].shape
     width = freqs // 4
-    core, here_map = facts[0], facts[3]
+    core, _, _, here_map, _ = whereabouts()
     outs = [
         (curves[2 * g], curves[2 * g + 1], p) for g, size in enumerate(GROUPS) for p in range(size)
     ]
@@ -131,49 +140,63 @@
 def transform(blocks, cosines, sines, ranges, phased, right_side):
     freqs = cosines.shape[2]
     pulses = cosines.shape[1]
+    half = freqs // 2
     for place, block in enumerate(blocks):
         values = block().astype(jnp.float32)
         real_part, imag_part = values[:, :freqs], values[:, freqs:]
         cosine, sine = cosines[place], sines[place]
         rows = slice(place * pulses, (place + 1) * pulses)
-        phased[rows, :freqs] = (real_part * cosine - imag_part * sine).astype(jnp.bfloat16)
-        phased[rows, freqs:] = (real_part * sine + imag_part * cosine).astype(jnp.bfloat16)
-    for half in range(2):
-        columns = slice(half * freqs, (half + 1) * freqs)
+        turned = (real_part * cosine - imag_part * sine, real_part * sine + imag_part * cosine)
+        for n, part in enumerate(turned):
+            columns = slice(n * half, (n + 1) * half)
+            low, high = part[:, :half], part[:, half:]
+            phased[0, rows, columns] = (low + high).astype(jnp.bfloat16)
+            phased[1, rows, columns] = (low - high).astype(jnp.bfloat16)
+    for parity in range(2):
         spectrum = jnp.dot(
-            phased[...], ranges[:, columns], preferred_element_type=jnp.float32
+            phased[parity],
+            ranges[parity * freqs : (parity + 1) * freqs],
+            preferred_element_type=jnp.float32,
         ).astype(jnp.bfloat16)
+        first = slice(parity * half, (parity + 1) * half)
+        second = slice(freqs + parity * half, freqs + (parity + 1) * half)
         for place in range(len(blocks)):
             piece = spectrum[place * pulses : (place + 1) * pulses]
-            top = 2 * place * pulses
-            right_side[top : top + pulses, columns] = piece
-            other = slice((1 - half) * freqs, (2 - half) * freqs)
-            right_side[top + pulses : top + 2 * pulses, other] = piece if half == 0 else -piece
-
-
-def fetch(facts, tables, cross, arrival):
-    copy = pltpu.make_async_copy(tables.at[facts[4]], cross, arrival)
+            real_part, imag_part = piece[:, :half], piece[:, half:]
+            top = slice(2 * place * pulses, (2 * place + 1) * pulses)
+            below = slice((2 * place + 1) * pulses, (2 * place + 2) * pulses)
+            right_side[top, first] = real_part
+            right_side[top, second] = imag_part
+            right_side[below, first] = -imag_part
+            right_side[below, second] = real_part
+
+
+def fetch(tables, cross, arrival):
+    copy = pltpu.make_async_copy(tables.at[whereabouts()[4]], cross, arrival)
     copy.start()
     return copy
 
 
 def first_kernel(
-    map_count, span, facts, curvature, own_far, twin, tables, total, *rest
+    map_count, span, curvature, own_far, twin, tables, total, *rest
 ):
     later = 2 * len(GROUPS) - 2
     cosines, sines, phased, right_side, cross, own, ranges, arrival, own_here, ranges_here = rest[
         later:
     ]
+    index = whereabouts()[4]
     copies = [
         pltpu.make_async_copy(own_far, own, own_here),
-        pltpu.make_async_copy(tables.at[facts[4], : ranges.shape[0]], ranges, ranges_here),
         pltpu.make_async_copy(
-            tables.at[facts[4], ranges.shape[0] :, : cross.shape[1]], cross, arrival
+            tables.at[index, : ranges.shape[0], : ranges.shape[1]], ranges, ranges_here
+        ),
+        pltpu.make_async_copy(
+            tables.at[index, ranges.shape[0] :, : cross.shape[1]], cross, arrival
         ),
     ]
     for copy in copies:
         copy.start()
-    phase_factors(map_count, span, facts, curvature, (cosines, sines, *rest[:later]))
+    phase_factors(map_count, span, curvature, (cosines, sines, *rest[:later]))
     for copy in copies:
         copy.wait()
     transform([lambda: own[...], lambda: twin[...]], cosines, sines, ranges, phased, right_side)
@@ -181,11 +204,11 @@
 
 
 def second_kernel(
-    facts, near_a, near_b, cosines, sines, ranges, tables, before, total,
+    near_a, near_b, cosines, sines, ranges, tables, before, total,
     phased, right_side, cross, arrival,
 ):
-    copy = fetch(facts, tables, cross, arrival)
-    chip_odd = facts[1] == 1
+    copy = fetch(tables, cross, arrival)
+    chip_odd = whereabouts()[1] == 1
     blocks = [
         lambda: jnp.where(chip_odd, near_a[...], near_b[...]),
         lambda: jnp.where(chip_odd, near_b[...], near_a[...]),
@@ -203,12 +226,12 @@
 
 
 def last_kernel(
-    facts, twin_near_a, twin_near_b, far_a, far_b, twin_far_a, twin_far_b,
+    twin_near_a, twin_near_b, far_a, far_b, twin_far_a, twin_far_b,
     cosines, sines, ranges, tables, before, sent, right_side, phased, cross, arrival,
 ):
-    copy = fetch(facts, tables, cross, arrival)
-    chip_odd, group_odd = facts[1] == 1, facts[2] == 1
-    from_a = facts[0] != facts[2]
+    copy = fetch(tables, cross, arrival)
+    core, chip, group, here_map, _ = whereabouts()
+    chip_odd, group_odd, from_a = chip == 1, group == 1, core != group
     blocks = [
         lambda: jnp.where(chip_odd, twin_near_a[...], twin_near_b[...]),
         lambda: jnp.where(chip_odd, twin_near_b[...], twin_near_a[...]),
@@ -217,7 +240,7 @@
     ]
     transform(blocks, cosines, sines, ranges, phased, right_side)
     copy.wait()
-    other = 1 - facts[3]
+    other = 1 - here_map
     sent[...] = (
         part_rows(before, other)
         + jnp.dot(
@@ -226,15 +249,25 @@
     ).astype(sent.dtype)
 
 
-def kept_kernel(facts, right_side, tables, before, kept, cross, arrival):
-    copy = fetch(facts, tables, cross, arrival)
+def kept_kernel(right_side, tables, before, kept, cross, arrival):
+    copy = fetch(tables, cross, arrival)
     copy.wait()
-    kept[...] = part_rows(before, facts[3]) + jnp.dot(
-        part_rows(cross, facts[3]), right_side[...], preferred_element_type=jnp.float32
-    )
-
-
-def slot_kernel(facts, tiles, offsets, owner, slot_hot, marks):
+    here_map = whereabouts()[3]
+    kept[...] = part_rows(before, here_map) + jnp.dot(
+        part_rows(cross, here_map), right_side[...], preferred_element_type=jnp.float32
+    )
+
+
+def slot_kernel(tiles, offsets, owner, weights, slot_hot, marks, ordered):
+    columns = weights.shape[0]
+    place = lax.broadcasted_iota(jnp.int32, weights.shape, 0)
+    source = jnp.where(place < columns // 2, 2 * place, 2 * place - columns + 1)
+    order = source == lax.broadcasted_iota(jnp.int32, weights.shape, 1)
+    ordered[...] = jnp.dot(
+        order.astype(jnp.float32).astype(jnp.bfloat16),
+        weights[...],
+        preferred_element_type=jnp.float32,
+    ).astype(jnp.bfloat16)
     count, rows = owner.shape[1], tiles.shape[1]
     _, pairs, _ = slot_hot.shape
     capacity = 2 * pairs // count
@@ -266,7 +299,7 @@
     marks[...] = total.astype(jnp.bfloat16)
 
 
-def pack_kernel(facts, kept, arrived, slot_hot, marks, packed):
+def pack_kernel(kept, arrived, slot_hot, marks, packed):
     width = kept.shape[1]
     image = (kept[...] + arrived[...].astype(jnp.float32)).astype(jnp.bfloat16)
     for part in range(2):
@@ -276,7 +309,7 @@
     packed[:, 2 * width :] = marks[...]
 
 
-def map_kernel(facts, got, weights, out):
+def map_kernel(got, weights, out):
     columns = weights.shape[0]
     pairs = got.shape[0]
     parts = [got[:, n * columns : (n + 1) * columns] for n in range(4)]
@@ -310,16 +343,11 @@
 def body(ranges, crosses, phase_history, tile_curvature, interp_weights, strip_tiles, row_offsets, tile_owner):
     blk_count = lax.axis_size("blk")
     map_count = lax.axis_size("map")
-    here_blk = lax.axis_index("blk")
-    here_map = lax.axis_index("map")
     own_block = phase_history[0, 0]
     pulse_count = own_block.shape[0]
     freq_count = own_block.shape[1] // 2
     columns = interp_weights.shape[2]
     rows_here = strip_tiles.shape[2]
-
-    core, chip_odd, group_odd = here_blk % 2, (here_blk // 2) % 2, (here_blk // 4) % 2
-    facts = jnp.stack([core, chip_odd, group_odd, here_map, here_map * 2 + core]).astype(jnp.int32)
 
     near = [lax.ppermute(own_block, "blk", matching(blk_count, 2, p)) for p in (0, 1)]
     far = [lax.ppermute(own_block, "blk", matching(blk_count, 4, p)) for p in (0, 1)]
@@ -331,7 +359,7 @@
     image_shape = (map_count * rows_here, 2 * columns)
     half_shape = (rows_here, 2 * columns)
     right = lambda n: pltpu.VMEM((n * deep, 2 * columns), jnp.bfloat16)
-    spread = lambda n: pltpu.VMEM((n * pulse_count, 2 * freq_count), jnp.bfloat16)
+    spread = lambda n: pltpu.VMEM((2, n * pulse_count, freq_count), jnp.bfloat16)
     table = lambda n: [
         pltpu.VMEM((map_count * rows_here, n * deep), jnp.bfloat16),
         pltpu.SemaphoreType.DMA,
@@ -345,7 +373,7 @@
         functools.partial(first_kernel, map_count, STOPS * map_count * pulse_count),
         out_shape=[f32(*image_shape)]
         + [f32(size, pulse_count, freq_count) for size in GROUPS[1:] for _ in range(2)],
-        in_specs=[smem, smem, hbm, vmem, hbm],
+        in_specs=[smem, hbm, vmem, hbm],
         out_specs=[vmem] * (2 * len(GROUPS) - 1),
         scratch_shapes=[pltpu.VMEM((n, pulse_count, freq_count), jnp.float32)] * 2
         + [
@@ -358,7 +386,7 @@
         + [pltpu.SemaphoreType.DMA] * 3,
         compiler_params=pltpu.CompilerParams(vmem_limit_bytes=44 * 2**20),
         cost_estimate=pl.CostEstimate(flops=flops(n), bytes_accessed=0, transcendentals=2**18),
-    )(facts, tile_curvature, own_block, twin, crosses[0])
+    )(tile_curvature, own_block, twin, crosses[0])
     far, near, total = lax.optimization_barrier((far, near, total))
     twin_near = [swap(block, blk_count) for block in near]
     twin_far = [swap(block, blk_count) for block in far]
@@ -366,49 +394,49 @@
     [total] = call(
         second_kernel,
         [f32(*image_shape)],
-        [facts, *near, *curves[:2], ranges, crosses[1], total],
+        [*near, *curves[:2], ranges, crosses[1], total],
         [spread(n), right(n), *table(n)],
         flops(n),
-        far=(6,),
+        far=(5,),
     )
     twin_near, twin_far, total = lax.optimization_barrier((twin_near, twin_far, total))
     n = GROUPS[2]
     sent, right_side = call(
         last_kernel,
         [b16(*half_shape), b16(n * deep, 2 * columns)],
-        [facts, *twin_near, *far, *twin_far, *curves[2:], ranges, crosses[2], total],
+        [*twin_near, *far, *twin_far, *curves[2:], ranges, crosses[2], total],
         [spread(n), *table(n)],
         flops(n),
-        far=(10,),
-    )
-    sent, right_side, strip_tiles, row_offsets = lax.optimization_barrier(
-        (sent, right_side, strip_tiles, row_offsets)
+        far=(9,),
+    )
+    sent, right_side, strip_tiles, row_offsets, interp_weights = lax.optimization_barrier(
+        (sent, right_side, strip_tiles, row_offsets, interp_weights)
     )
     arrived = lax.ppermute(sent, "map", [(0, 1), (1, 0)])
     pairs = max(2, 2 * rows_here // blk_count) * blk_count // 2
-    slot_hot, marks = call(
+    slot_hot, marks, ordered = call(
         slot_kernel,
-        [b16(2, pairs, rows_here), b16(pairs, SIDE)],
+        [b16(2, pairs, rows_here), b16(pairs, SIDE), b16(columns, columns)],
         [
-            facts,
             strip_tiles.reshape(1, rows_here),
             row_offsets.reshape(1, rows_here),
             tile_owner.reshape(1, blk_count),
+            interp_weights[0],
         ],
     )
     [kept] = call(
         kept_kernel,
         [f32(*half_shape)],
-        [facts, right_side, crosses[2], total],
+        [right_side, crosses[2], total],
         table(n),
-        far=(2,),
+        far=(1,),
     )
 
     wide = 4 * columns + SIDE
     [packed] = call(
         pack_kernel,
         [b16(pairs, wide)],
-        [facts, kept, arrived, slot_hot, marks],
+        [kept, arrived, slot_hot, marks],
         (),
         2 * pairs * rows_here * wide,
     )
@@ -417,7 +445,7 @@
     [tile_map] = call(
         map_kernel,
         [f32(MAPH, columns)],
-        [facts, got.reshape(pairs, wide), interp_weights[0]],
+        [got.reshape(pairs, wide), ordered],
         (),
         2 * pairs * 4 * columns * (columns + MAPH),
     )
@@ -437,10 +465,10 @@
 
     def run(*args):
         map_count, pulse_count, width = args[0].shape[1:]
-        ranges = jnp.asarray(range_table(width // 2))
+        ranges = jnp.asarray(range_tables(width // 2))
         crosses = cross_tables(map_count, map_count * args[3].shape[2], pulse_count)
         first = np.zeros((len(crosses[0]), width + crosses[0].shape[1], width), crosses[0].dtype)
-        first[:, : width] = range_table(width // 2)
+        first[:, :width, : width // 2] = range_tables(width // 2)
         first[:, width : , : crosses[0].shape[2]] = crosses[0]
         crosses = [jnp.asarray(table) for table in (first, *crosses[1:])]
         held = lambda *here: body(ranges, crosses, *here)

time: 93.3 us -> 91.2 us (0.977)
  Pallas kernels: 15.7 us -> 11.2 us
  waiting for transfers between devices: 16.7 us -> 18.9 us
    pallas_call x6, Pallas kernels: 10.3 us -> 6.73 us  [call(): pl.pallas_call(kernel, out_shape=outs, in_specs=specs, out_specs=[pl.Bloc...]
    ppermute x2, waiting for transfers between devices: 5.46 us -> 6.53 us  [body(): lax.ppermute(own_block, 'blk', matching(blk_count, 2, p))]
    pallas_call x1, Pallas kernels: 5.44 us -> 4.44 us  [body(): pl.pallas_call(functools.partial(first_kernel, map_count, STOPS * map_cou...]
  transfers between devices with their start and end apart: 10 -> 10, of which waited for: 3 -> 4; matrix products, arithmetic and copies ran while one was open for 0% -> 0% of each run, Pallas kernels for 10% -> 8%
where the time goes in v6:
time: 91.2 us; the launch traced here: 91 us
  blocking collectives  47.3 us (52%)
  waiting for transfers between devices  18.9 us (21%)
  Pallas kernels  11.2 us (12%)
  starting transfers between devices  9.07 us (10%)
  local copies, waits for them, and re-layouts  3.65 us (4%)
    all_to_all x1, blocking collectives, body(): got = lax.all_to_all(packed, 'blk', split_axis=0, concat_axis=0, tiled=True)  47.3 us
    ppermute x1, waiting for transfers between devices, body(): arrived = lax.ppermute(sent, 'map', [(0, 1), (1, 0)])  12 us
    pallas_call x6, Pallas kernels, call(): pl.pallas_call(kernel, out_shape=outs, in_specs=specs, out_specs=[pl.Bloc...  6.73 us
    ppermute x2, waiting for transfers between devices, body(): lax.ppermute(own_block, 'blk', matching(blk_count, 2, p))  6.53 us
    ppermute x2, starting transfers between devices, body(): lax.ppermute(own_block, 'blk', matching(blk_count, 2, p))  5.02 us
    pallas_call x1, Pallas kernels, body(): pl.pallas_call(functools.partial(first_kernel, map_count, STOPS * map_cou...  4.44 us
    ppermute x2, starting transfers between devices, body(): lax.ppermute(own_block, 'blk', matching(blk_count, 4, p))  2.38 us
  transfers between devices with their start and end apart: 10, of which 4 were waited for; matrix products, arithmetic and copies ran while one was open for 0% of the time, Pallas kernels for 8%

profile of v6, /device:TPU:32, one launch (start us, length us, event | category | flops | bytes accessed | tf_op | source)
XLA Modules:
  0.0 91.0 jit_solution(1530301418858937265)
XLA Ops:
  0.0 5.0 %collective-permute-start.3 = (bf16[128,1024]{1,0:T(8,128)(2,1)}, bf16[128,1024]{1,0:T(8,128)(2,1)S(1)}, u32[]{:S(2)}, u32[]{:S(2)}) collective-permute-start(bf16[128,1024]{1,0:T(8,128)(2,1)} %bitcast.8), channel_id=1, source_target_pairs={{4,8},{8,4},{12,16},{16,12},{20,24},{24,20},{28,32},{32,28},{36,40... | collective-permute-start | bytes 786440 | tf_op jit(solution)/shard_map/ppermute | solution.py:352
  5.0 2.1 %collective-permute-start.1 = (bf16[128,1024]{1,0:T(8,128)(2,1)}, bf16[128,1024]{1,0:T(8,128)(2,1)S(1)}, u32[]{:S(2)}, u32[]{:S(2)}) collective-permute-start(bf16[128,1024]{1,0:T(8,128)(2,1)} %bitcast.10), channel_id=1, source_target_pairs={{8,16},{16,8},{24,32},{32,24},{40,48},{48,40},{56,64},{64,56},{72,... | collective-permute-start | bytes 786440 | tf_op jit(solution)/shard_map/ppermute | solution.py:353
  7.1 0.3 collective-permute-start
  8.1 0.0 copy-start.1
  8.1 1.1 %copy-done.4 = bf16[1,1,128,1024]{3,2,1,0:T(8,128)(2,1)S(1)} copy-done((bf16[1,1,128,1024]{3,2,1,0:T(8,128)(2,1)S(1)}, bf16[1,1,128,1024]{3,2,1,0:T(8,128)(2,1)}, u32[]{:S(2)}) %copy-start.4) | copy-done | bytes 262168
  9.2 4.4 %shard_map.100 = (f32[512,1024]{1,0:T(8,128)S(1)}, f32[2,128,512]{2,1,0:T(8,128)S(1)}, f32[2,128,512]{2,1,0:T(8,128)S(1)}, f32[4,128,512]{2,1,0:T(8,128)S(1)}, f32[4,128,512]{2,1,0:T(8,128)S(1)}) custom-call(f32[1]{0:T(128)S(6)} %copy.11.curvature, bf16[128,1024]{1,0:T(8,128)(2,1)S(1)} %bitcast.12, bf16[128,1024]{1,0:T(8,128)(2,1)S(1)} %collective-permute-done.4.twin, ...), custom_call_target="tpu_custom_call" | custom-call | flops 1073741824 | tf_op jit(solution)/shard_map/pallas_call | solution.py:372
  13.6 2.2 %collective-permute-done.3.near_b = bf16[128,1024]{1,0:T(8,128)(2,1)S(1)} collective-permute-done((bf16[128,1024]{1,0:T(8,128)(2,1)}, bf16[128,1024]{1,0:T(8,128)(2,1)S(1)}, u32[]{:S(2)}, u32[]{:S(2)}) %collective-permute-start.3) | collective-permute-done | bytes 262176 | tf_op jit(solution)/shard_map/ppermute | solution.py:352
  15.8 4.4 %collective-permute-done.2.near_a = bf16[128,1024]{1,0:T(8,128)(2,1)S(1)} collective-permute-done((bf16[128,1024]{1,0:T(8,128)(2,1)}, bf16[128,1024]{1,0:T(8,128)(2,1)S(1)}, u32[]{:S(2)}, u32[]{:S(2)}) %collective-permute-start.2) | collective-permute-done | bytes 262176 | tf_op jit(solution)/shard_map/ppermute | solution.py:352
  20.2 0.5 collective-permute-start.6
  20.7 0.1 collective-permute-start.7
  20.8 0.4 collective-permute-start.8
  21.2 1.3 %shard_map.101.before = f32[512,1024]{1,0:T(8,128)S(1)} custom-call(bf16[128,1024]{1,0:T(8,128)(2,1)S(1)} %collective-permute-done.2.near_a, bf16[128,1024]{1,0:T(8,128)(2,1)S(1)} %collective-permute-done.3.near_b, f32[2,128,512]{2,1,0:T(8,128)S(1)} %get-tuple-element.35.cosines, f32[2,128,512]{2,1,0:T(8,128)S(1)} %get-tuple-element.36.sines, ...), custom_call_target="tpu_custom_call" | custom-call | flops 1073741824 | bytes 8912896 | tf_op jit(solution)/shard_map/pallas_call | solution.py:79
  22.5 0.3 collective-permute-done.8.twin_far_b
  22.8 0.6 copy-done
  23.4 1.7 %shard_map.102 = (bf16[256,1024]{1,0:T(8,128)(2,1)S(1)}, bf16[1024,1024]{1,0:T(8,128)(2,1)S(1)}) custom-call(bf16[128,1024]{1,0:T(8,128)(2,1)S(1)} %collective-permute-done.5.twin_near_a, bf16[128,1024]{1,0:T(8,128)(2,1)S(1)} %collective-permute-done.6.twin_near_b, bf16[128,1024]{1,0:T(8,128)(2,1)S(1)} %collective-permute-done.far_a, ...), custom_call_target="tpu_custom_call" | custom-call | flops 2147483648 | bytes 13631488 | tf_op jit(solution)/shard_map/pallas_call | solution.py:79
  25.2 0.6 collective-permute-start.9
  25.8 0.8 shard_map.103.kept
  26.7 0.7 shard_map.104
  27.3 12.0 %collective-permute-done.9.arrived = bf16[256,1024]{1,0:T(8,128)(2,1)S(1)} collective-permute-done((bf16[256,1024]{1,0:T(8,128)(2,1)S(1)}, bf16[256,1024]{1,0:T(8,128)(2,1)S(1)}, u32[]{:S(2)}, u32[]{:S(2)}) %collective-permute-start.9) | collective-permute-done | bytes 524320 | tf_op jit(solution)/shard_map/ppermute | solution.py:415
  39.4 0.5 shard_map.105
  39.8 0.5 reshape.21
  40.3 47.3 %all_to_all.5 = bf16[128,2,2176]{2,1,0:T(2,128)(2,1)} all-to-all(bf16[128,2,2176]{2,1,0:T(2,128)(2,1)S(1)} %reshape.21), channel_id=1, replica_groups=mesh['blk'=128,'map'=2] {'blk'}, dimensions={0} | all-to-all | bytes 2228224 | tf_op jit(solution)/shard_map/all_to_all | solution.py:444
  87.6 1.5 %reshape.22.got = bf16[256,2176]{1,0:T(8,128)(2,1)S(1)} reshape(bf16[128,2,2176]{2,1,0:T(2,128)(2,1)} %all_to_all.5) | data formatting | bytes 2228224 | tf_op jit(solution)/shard_map/reshape | solution.py:448
  89.2 1.8 %shard_map.106 = f32[256,512]{1,0:T(8,128)} custom-call(bf16[256,2176]{1,0:T(8,128)(2,1)S(1)} %reshape.22.got, bf16[512,512]{1,0:T(8,128)(2,1)S(1)} %get-tuple-element.54.weights), custom_call_target="tpu_custom_call" | custom-call | flops 805306368 | bytes 2162688 | tf_op jit(solution)/shard_map/pallas_call | solution.py:79
  (22 shorter events, 0.1 us)
Async XLA Ops:
  0.0 8.1 %collective-permute-start.4 = (bf16[128,1024]{1,0:T(8,128)(2,1)}, bf16[128,1024]{1,0:T(8,128)(2,1)S(1)}, u32[]{:S(2)}, u32[]{:S(2)}) collective-permute-start(bf16[128,1024]{1,0:T(8,128)(2,1)} %bitcast.7), channel_id=1, source_target_pairs={{0,2},{2,0},{4,6},{6,4},{8,10},{10,8},{12,14},{14,12},{16,18},{18,... | collective-permute-start | bytes 786440 | tf_op jit(solution)/shard_map/ppermute | solution.py:340
  0.0 15.8 %collective-permute-start.3 = (bf16[128,1024]{1,0:T(8,128)(2,1)}, bf16[128,1024]{1,0:T(8,128)(2,1)S(1)}, u32[]{:S(2)}, u32[]{:S(2)}) collective-permute-start(bf16[128,1024]{1,0:T(8,128)(2,1)} %bitcast.8), channel_id=1, source_target_pairs={{4,8},{8,4},{12,16},{16,12},{20,24},{24,20},{28,32},{32,28},{36,40... | collective-permute-start | bytes 786440 | tf_op jit(solution)/shard_map/ppermute | solution.py:352
  5.0 15.2 %collective-permute-start.2 = (bf16[128,1024]{1,0:T(8,128)(2,1)}, bf16[128,1024]{1,0:T(8,128)(2,1)S(1)}, u32[]{:S(2)}, u32[]{:S(2)}) collective-permute-start(bf16[128,1024]{1,0:T(8,128)(2,1)} %bitcast.9), channel_id=1, source_target_pairs={{0,4},{4,0},{8,12},{12,8},{16,20},{20,16},{24,28},{28,24},{32,36},... | collective-permute-start | bytes 786440 | tf_op jit(solution)/shard_map/ppermute | solution.py:352
  5.0 15.2 %collective-permute-start.1 = (bf16[128,1024]{1,0:T(8,128)(2,1)}, bf16[128,1024]{1,0:T(8,128)(2,1)S(1)}, u32[]{:S(2)}, u32[]{:S(2)}) collective-permute-start(bf16[128,1024]{1,0:T(8,128)(2,1)} %bitcast.10), channel_id=1, source_target_pairs={{8,16},{16,8},{24,32},{32,24},{40,48},{48,40},{56,64},{64,56},{72,... | collective-permute-start | bytes 786440 | tf_op jit(solution)/shard_map/ppermute | solution.py:353
  7.1 13.1 %collective-permute-start = (bf16[128,1024]{1,0:T(8,128)(2,1)}, bf16[128,1024]{1,0:T(8,128)(2,1)S(1)}, u32[]{:S(2)}, u32[]{:S(2)}) collective-permute-start(bf16[128,1024]{1,0:T(8,128)(2,1)} %bitcast.11), channel_id=1, source_target_pairs={{0,8},{8,0},{16,24},{24,16},{32,40},{40,32},{48,56},{56,48},{64,72... | collective-permute-start | bytes 786440 | tf_op jit(solution)/shard_map/ppermute | solution.py:353
  8.1 13.1 %copy-start.1 = (bf16[1024,512]{1,0:T(8,128)(2,1)S(1)}, bf16[1024,512]{1,0:T(8,128)(2,1)}, u32[]{:S(2)}) copy-start(bf16[1024,512]{1,0:T(8,128)(2,1)} %constant.9.clone.ranges) | copy-start | bytes 3145732
  8.1 13.1 %copy-start.2 = (bf16[4,512,512]{2,1,0:T(8,128)(2,1)S(1)}, bf16[4,512,512]{2,1,0:T(8,128)(2,1)}, u32[]{:S(2)}) copy-start(bf16[4,512,512]{2,1,0:T(8,128)(2,1)} %constant.10.clone.tables) | copy-start | bytes 6291460
  8.1 1.1 %copy-start.4 = (bf16[1,1,128,1024]{3,2,1,0:T(8,128)(2,1)S(1)}, bf16[1,1,128,1024]{3,2,1,0:T(8,128)(2,1)}, u32[]{:S(2)}) copy-start(bf16[1,1,128,1024]{3,2,1,0:T(8,128)(2,1)} %param.10) | copy-start | bytes 786436
  20.2 2.3 %collective-permute-start.5 = (bf16[128,1024]{1,0:T(8,128)(2,1)S(1)}, bf16[128,1024]{1,0:T(8,128)(2,1)S(1)}, u32[]{:S(2)}, u32[]{:S(2)}) collective-permute-start(bf16[128,1024]{1,0:T(8,128)(2,1)S(1)} %collective-permute-done.2.near_a), channel_id=1, source_target_pairs={{0,2},{2,0},{4,6},{6,4},{8,10},{10,8},{12,14},{14,12},{16,18},{18,... | collective-permute-start | bytes 786440 | tf_op jit(solution)/shard_map/ppermute | solution.py:340
  20.2 2.3 %collective-permute-start.6 = (bf16[128,1024]{1,0:T(8,128)(2,1)S(1)}, bf16[128,1024]{1,0:T(8,128)(2,1)S(1)}, u32[]{:S(2)}, u32[]{:S(2)}) collective-permute-start(bf16[128,1024]{1,0:T(8,128)(2,1)S(1)} %collective-permute-done.3.near_b), channel_id=1, source_target_pairs={{0,2},{2,0},{4,6},{6,4},{8,10},{10,8},{12,14},{14,12},{16,18},{18,... | collective-permute-start | bytes 786440 | tf_op jit(solution)/shard_map/ppermute | solution.py:340
  20.7 1.8 %collective-permute-start.7 = (bf16[128,1024]{1,0:T(8,128)(2,1)S(1)}, bf16[128,1024]{1,0:T(8,128)(2,1)S(1)}, u32[]{:S(2)}, u32[]{:S(2)}) collective-permute-start(bf16[128,1024]{1,0:T(8,128)(2,1)S(1)} %collective-permute-done.far_a), channel_id=1, source_target_pairs={{0,2},{2,0},{4,6},{6,4},{8,10},{10,8},{12,14},{14,12},{16,18},{18,... | collective-permute-start | bytes 786440 | tf_op jit(solution)/shard_map/ppermute | solution.py:340
  20.8 2.1 %collective-permute-start.8 = (bf16[128,1024]{1,0:T(8,128)(2,1)S(1)}, bf16[128,1024]{1,0:T(8,128)(2,1)S(1)}, u32[]{:S(2)}, u32[]{:S(2)}) collective-permute-start(bf16[128,1024]{1,0:T(8,128)(2,1)S(1)} %collective-permute-done.1.far_b), channel_id=1, source_target_pairs={{0,2},{2,0},{4,6},{6,4},{8,10},{10,8},{12,14},{14,12},{16,18},{18,... | collective-permute-start | bytes 786440 | tf_op jit(solution)/shard_map/ppermute | solution.py:340
  21.2 2.2 %copy-start = (bf16[4,512,1024]{2,1,0:T(8,128)(2,1)S(1)}, bf16[4,512,1024]{2,1,0:T(8,128)(2,1)}, u32[]{:S(2)}) copy-start(bf16[4,512,1024]{2,1,0:T(8,128)(2,1)} %constant.11.clone.tables) | copy-start | bytes 12582916
  25.1 1.5 %copy-start.3 = (bf16[1,512,512]{2,1,0:T(8,128)(2,1)S(1)}, bf16[1,512,512]{2,1,0:T(8,128)(2,1)}, u32[]{:S(2)}) copy-start(bf16[1,512,512]{2,1,0:T(8,128)(2,1)} %param.12) | copy-start | bytes 1572868
  25.2 1.5 %copy-start.5 = (s32[1,1,256,1]{2,3,1,0:T(1,128)S(1)}, s32[1,1,256,1]{2,3,1,0:T(1,128)}, u32[]{:S(2)}) copy-start(s32[1,1,256,1]{2,3,1,0:T(1,128)} %param.13) | copy-start | bytes 3076
  25.2 1.5 %copy-start.6 = (s32[1,1,256]{2,1,0:T(1,128)S(1)}, s32[1,1,256]{2,1,0:T(1,128)}, u32[]{:S(2)}) copy-start(s32[1,1,256]{2,1,0:T(1,128)} %param.14) | copy-start | bytes 3076
  25.2 1.5 %copy-start.7 = (s32[128]{0:T(128)S(1)}, s32[128]{0:T(128)}, u32[]{:S(2)}) copy-start(s32[128]{0:T(128)} %param.15) | copy-start | bytes 1540
  25.2 14.2 %collective-permute-start.9 = (bf16[256,1024]{1,0:T(8,128)(2,1)S(1)}, bf16[256,1024]{1,0:T(8,128)(2,1)S(1)}, u32[]{:S(2)}, u32[]{:S(2)}) collective-permute-start(bf16[256,1024]{1,0:T(8,128)(2,1)S(1)} %get-tuple-element.48), channel_id=1, source_target_pairs={{0,1},{1,0},{2,3},{3,2},{4,5},{5,4},{6,7},{7,6},{8,9},{9,8},{10,11... | collective-permute-start | bytes 1572872 | tf_op jit(solution)/shard_map/ppermute | solution.py:415

commit v7 on v6

--- a/solution.py
+++ b/solution.py
@@ -301,23 +301,27 @@
 
 def pack_kernel(kept, arrived, slot_hot, marks, packed):
     width = kept.shape[1]
+    count, group, _ = packed.shape
     image = (kept[...] + arrived[...].astype(jnp.float32)).astype(jnp.bfloat16)
     for part in range(2):
-        packed[:, part * width : (part + 1) * width] = jnp.dot(
-            slot_hot[part], image, preferred_element_type=jnp.float32
-        ).astype(packed.dtype)
-    packed[:, 2 * width :] = marks[...]
+        packed[:, :, part * width : (part + 1) * width] = (
+            jnp.dot(slot_hot[part], image, preferred_element_type=jnp.float32)
+            .astype(packed.dtype)
+            .reshape(count, group, width)
+        )
+    packed[:, :, 2 * width :] = marks[...].reshape(count, group, marks.shape[1])
 
 
 def map_kernel(got, weights, out):
     columns = weights.shape[0]
-    pairs = got.shape[0]
-    parts = [got[:, n * columns : (n + 1) * columns] for n in range(4)]
+    pairs = got.shape[0] * got.shape[1]
+    flat = got[...].reshape(pairs, got.shape[2])
+    parts = [flat[:, n * columns : (n + 1) * columns] for n in range(4)]
     mapped = jnp.dot(
         jnp.concatenate(parts, axis=0), weights[...], preferred_element_type=jnp.float32
     )
     squared = mapped * mapped
-    marks = got[:, 4 * columns :].astype(jnp.float32).T
+    marks = flat[:, 4 * columns :].astype(jnp.float32).T
     spots = lax.broadcasted_iota(jnp.int32, (MAPH, pairs), 0)
     hots, pieces = [], []
     for part in range(2):
@@ -435,17 +439,16 @@
     wide = 4 * columns + SIDE
     [packed] = call(
         pack_kernel,
-        [b16(pairs, wide)],
+        [b16(blk_count, pairs // blk_count, wide)],
         [kept, arrived, slot_hot, marks],
         (),
         2 * pairs * rows_here * wide,
     )
-    packed = packed.reshape(blk_count, pairs // blk_count, wide)
     got = lax.all_to_all(packed, "blk", split_axis=0, concat_axis=0, tiled=True)
     [tile_map] = call(
         map_kernel,
         [f32(MAPH, columns)],
-        [got.reshape(pairs, wide), ordered],
+        [got, ordered],
         (),
         2 * pairs * 4 * columns * (columns + MAPH),
     )

time: 91.2 us -> 89.1 us (0.977)
  local copies, waits for them, and re-layouts: 3.65 us -> 1.69 us
    reshape x2 -> x0, local copies, waits for them, and re-layouts: 1.96 us -> none  [the longest x1 1.5 us: body(): got.reshape(pairs, wide)]
where the time goes in v7:
time: 89.1 us; the launch traced here: 89 us
  blocking collectives  47.2 us (53%)
  waiting for transfers between devices  18.9 us (21%)
  Pallas kernels  11.3 us (13%)
  starting transfers between devices  9.07 us (10%)
  local copies, waits for them, and re-layouts  1.69 us (2%)
    all_to_all x1, blocking collectives, body(): got = lax.all_to_all(packed, 'blk', split_axis=0, concat_axis=0, tiled=True)  47.2 us
    ppermute x1, waiting for transfers between devices, body(): arrived = lax.ppermute(sent, 'map', [(0, 1), (1, 0)])  12 us
    pallas_call x6, Pallas kernels, call(): pl.pallas_call(kernel, out_shape=outs, in_specs=specs, out_specs=[pl.Bloc...  6.82 us
    ppermute x2, waiting for transfers between devices, body(): lax.ppermute(own_block, 'blk', matching(blk_count, 2, p))  6.53 us
    ppermute x2, starting transfers between devices, body(): lax.ppermute(own_block, 'blk', matching(blk_count, 2, p))  5.02 us
    pallas_call x1, Pallas kernels, body(): pl.pallas_call(functools.partial(first_kernel, map_count, STOPS * map_cou...  4.44 us
    ppermute x2, starting transfers between devices, body(): lax.ppermute(own_block, 'blk', matching(blk_count, 4, p))  2.38 us
  transfers between devices with their start and end apart: 10, of which 4 were waited for; matrix products, arithmetic and copies ran while one was open for 0% of the time, Pallas kernels for 8%

profile of v7, /device:TPU:32, one launch (start us, length us, event | category | flops | bytes accessed | tf_op | source)
XLA Modules:
  0.0 89.0 jit_solution(15268758116240015204)
XLA Ops:
  0.0 5.0 %collective-permute-start.3 = (bf16[128,1024]{1,0:T(8,128)(2,1)}, bf16[128,1024]{1,0:T(8,128)(2,1)S(1)}, u32[]{:S(2)}, u32[]{:S(2)}) collective-permute-start(bf16[128,1024]{1,0:T(8,128)(2,1)} %bitcast.8), channel_id=1, source_target_pairs={{4,8},{8,4},{12,16},{16,12},{20,24},{24,20},{28,32},{32,28},{36,40... | collective-permute-start | bytes 786440 | tf_op jit(solution)/shard_map/ppermute | solution.py:356
  5.0 2.1 %collective-permute-start.1 = (bf16[128,1024]{1,0:T(8,128)(2,1)}, bf16[128,1024]{1,0:T(8,128)(2,1)S(1)}, u32[]{:S(2)}, u32[]{:S(2)}) collective-permute-start(bf16[128,1024]{1,0:T(8,128)(2,1)} %bitcast.10), channel_id=1, source_target_pairs={{8,16},{16,8},{24,32},{32,24},{40,48},{48,40},{56,64},{64,56},{72,... | collective-permute-start | bytes 786440 | tf_op jit(solution)/shard_map/ppermute | solution.py:357
  7.1 0.3 collective-permute-start
  8.1 0.0 copy-start.1
  8.1 0.0 copy-start.2
  8.1 1.1 %copy-done.4 = bf16[1,1,128,1024]{3,2,1,0:T(8,128)(2,1)S(1)} copy-done((bf16[1,1,128,1024]{3,2,1,0:T(8,128)(2,1)S(1)}, bf16[1,1,128,1024]{3,2,1,0:T(8,128)(2,1)}, u32[]{:S(2)}) %copy-start.4) | copy-done | bytes 262168
  9.2 4.4 %shard_map.100 = (f32[512,1024]{1,0:T(8,128)S(1)}, f32[2,128,512]{2,1,0:T(8,128)S(1)}, f32[2,128,512]{2,1,0:T(8,128)S(1)}, f32[4,128,512]{2,1,0:T(8,128)S(1)}, f32[4,128,512]{2,1,0:T(8,128)S(1)}) custom-call(f32[1]{0:T(128)S(6)} %copy.11.curvature, bf16[128,1024]{1,0:T(8,128)(2,1)S(1)} %bitcast.12, bf16[128,1024]{1,0:T(8,128)(2,1)S(1)} %collective-permute-done.4.twin, ...), custom_call_target="tpu_custom_call" | custom-call | flops 1073741824 | tf_op jit(solution)/shard_map/pallas_call | solution.py:376
  13.6 2.2 %collective-permute-done.3.near_b = bf16[128,1024]{1,0:T(8,128)(2,1)S(1)} collective-permute-done((bf16[128,1024]{1,0:T(8,128)(2,1)}, bf16[128,1024]{1,0:T(8,128)(2,1)S(1)}, u32[]{:S(2)}, u32[]{:S(2)}) %collective-permute-start.3) | collective-permute-done | bytes 262176 | tf_op jit(solution)/shard_map/ppermute | solution.py:356
  15.8 4.4 %collective-permute-done.2.near_a = bf16[128,1024]{1,0:T(8,128)(2,1)S(1)} collective-permute-done((bf16[128,1024]{1,0:T(8,128)(2,1)}, bf16[128,1024]{1,0:T(8,128)(2,1)S(1)}, u32[]{:S(2)}, u32[]{:S(2)}) %collective-permute-start.2) | collective-permute-done | bytes 262176 | tf_op jit(solution)/shard_map/ppermute | solution.py:356
  20.2 0.5 collective-permute-start.6
  20.7 0.1 collective-permute-start.7
  20.8 0.4 collective-permute-start.8
  21.2 1.3 %shard_map.101.before = f32[512,1024]{1,0:T(8,128)S(1)} custom-call(bf16[128,1024]{1,0:T(8,128)(2,1)S(1)} %collective-permute-done.2.near_a, bf16[128,1024]{1,0:T(8,128)(2,1)S(1)} %collective-permute-done.3.near_b, f32[2,128,512]{2,1,0:T(8,128)S(1)} %get-tuple-element.35.cosines, f32[2,128,512]{2,1,0:T(8,128)S(1)} %get-tuple-element.36.sines, ...), custom_call_target="tpu_custom_call" | custom-call | flops 1073741824 | bytes 8912896 | tf_op jit(solution)/shard_map/pallas_call | solution.py:79
  22.5 0.3 collective-permute-done.8.twin_far_b
  22.8 0.6 copy-done
  23.4 1.7 %shard_map.102 = (bf16[256,1024]{1,0:T(8,128)(2,1)S(1)}, bf16[1024,1024]{1,0:T(8,128)(2,1)S(1)}) custom-call(bf16[128,1024]{1,0:T(8,128)(2,1)S(1)} %collective-permute-done.5.twin_near_a, bf16[128,1024]{1,0:T(8,128)(2,1)S(1)} %collective-permute-done.6.twin_near_b, bf16[128,1024]{1,0:T(8,128)(2,1)S(1)} %collective-permute-done.far_a, ...), custom_call_target="tpu_custom_call" | custom-call | flops 2147483648 | bytes 13631488 | tf_op jit(solution)/shard_map/pallas_call | solution.py:79
  25.1 0.0 copy-start.3
  25.2 0.6 collective-permute-start.9
  25.8 0.8 shard_map.103.kept
  26.7 0.7 shard_map.104
  27.3 12.0 %collective-permute-done.9.arrived = bf16[256,1024]{1,0:T(8,128)(2,1)S(1)} collective-permute-done((bf16[256,1024]{1,0:T(8,128)(2,1)S(1)}, bf16[256,1024]{1,0:T(8,128)(2,1)S(1)}, u32[]{:S(2)}, u32[]{:S(2)}) %collective-permute-start.9) | collective-permute-done | bytes 524320 | tf_op jit(solution)/shard_map/ppermute | solution.py:419
  39.4 0.5 shard_map.105
  39.9 47.2 %all_to_all.5.got = bf16[128,2,2176]{2,1,0:T(2,128)(2,1)S(1)} all-to-all(bf16[128,2,2176]{2,1,0:T(2,128)(2,1)S(1)} %shard_map.105), channel_id=1, replica_groups=mesh['blk'=128,'map'=2] {'blk'}, dimensions={0} | all-to-all | bytes 2228224 | tf_op jit(solution)/shard_map/all_to_all | solution.py:447
  87.1 1.9 %shard_map.106 = f32[256,512]{1,0:T(8,128)} custom-call(bf16[128,2,2176]{2,1,0:T(2,128)(2,1)S(1)} %all_to_all.5.got, bf16[512,512]{1,0:T(8,128)(2,1)S(1)} %get-tuple-element.54.weights), custom_call_target="tpu_custom_call" | custom-call | flops 805306368 | bytes 2162688 | tf_op jit(solution)/shard_map/pallas_call | solution.py:79
  (20 shorter events, 0.1 us)
Async XLA Ops:
  0.0 8.1 %collective-permute-start.4 = (bf16[128,1024]{1,0:T(8,128)(2,1)}, bf16[128,1024]{1,0:T(8,128)(2,1)S(1)}, u32[]{:S(2)}, u32[]{:S(2)}) collective-permute-start(bf16[128,1024]{1,0:T(8,128)(2,1)} %bitcast.7), channel_id=1, source_target_pairs={{0,2},{2,0},{4,6},{6,4},{8,10},{10,8},{12,14},{14,12},{16,18},{18,... | collective-permute-start | bytes 786440 | tf_op jit(solution)/shard_map/ppermute | solution.py:344
  0.0 15.8 %collective-permute-start.3 = (bf16[128,1024]{1,0:T(8,128)(2,1)}, bf16[128,1024]{1,0:T(8,128)(2,1)S(1)}, u32[]{:S(2)}, u32[]{:S(2)}) collective-permute-start(bf16[128,1024]{1,0:T(8,128)(2,1)} %bitcast.8), channel_id=1, source_target_pairs={{4,8},{8,4},{12,16},{16,12},{20,24},{24,20},{28,32},{32,28},{36,40... | collective-permute-start | bytes 786440 | tf_op jit(solution)/shard_map/ppermute | solution.py:356
  5.0 15.2 %collective-permute-start.2 = (bf16[128,1024]{1,0:T(8,128)(2,1)}, bf16[128,1024]{1,0:T(8,128)(2,1)S(1)}, u32[]{:S(2)}, u32[]{:S(2)}) collective-permute-start(bf16[128,1024]{1,0:T(8,128)(2,1)} %bitcast.9), channel_id=1, source_target_pairs={{0,4},{4,0},{8,12},{12,8},{16,20},{20,16},{24,28},{28,24},{32,36},... | collective-permute-start | bytes 786440 | tf_op jit(solution)/shard_map/ppermute | solution.py:356
  5.0 15.2 %collective-permute-start.1 = (bf16[128,1024]{1,0:T(8,128)(2,1)}, bf16[128,1024]{1,0:T(8,128)(2,1)S(1)}, u32[]{:S(2)}, u32[]{:S(2)}) collective-permute-start(bf16[128,1024]{1,0:T(8,128)(2,1)} %bitcast.10), channel_id=1, source_target_pairs={{8,16},{16,8},{24,32},{32,24},{40,48},{48,40},{56,64},{64,56},{72,... | collective-permute-start | bytes 786440 | tf_op jit(solution)/shard_map/ppermute | solution.py:357
  7.1 13.1 %collective-permute-start = (bf16[128,1024]{1,0:T(8,128)(2,1)}, bf16[128,1024]{1,0:T(8,128)(2,1)S(1)}, u32[]{:S(2)}, u32[]{:S(2)}) collective-permute-start(bf16[128,1024]{1,0:T(8,128)(2,1)} %bitcast.11), channel_id=1, source_target_pairs={{0,8},{8,0},{16,24},{24,16},{32,40},{40,32},{48,56},{56,48},{64,72... | collective-permute-start | bytes 786440 | tf_op jit(solution)/shard_map/ppermute | solution.py:357
  8.1 13.1 %copy-start.1 = (bf16[1024,512]{1,0:T(8,128)(2,1)S(1)}, bf16[1024,512]{1,0:T(8,128)(2,1)}, u32[]{:S(2)}) copy-start(bf16[1024,512]{1,0:T(8,128)(2,1)} %constant.9.clone.ranges) | copy-start | bytes 3145732
  8.1 13.1 %copy-start.2 = (bf16[4,512,512]{2,1,0:T(8,128)(2,1)S(1)}, bf16[4,512,512]{2,1,0:T(8,128)(2,1)}, u32[]{:S(2)}) copy-start(bf16[4,512,512]{2,1,0:T(8,128)(2,1)} %constant.10.clone.tables) | copy-start | bytes 6291460
  8.1 1.1 %copy-start.4 = (bf16[1,1,128,1024]{3,2,1,0:T(8,128)(2,1)S(1)}, bf16[1,1,128,1024]{3,2,1,0:T(8,128)(2,1)}, u32[]{:S(2)}) copy-start(bf16[1,1,128,1024]{3,2,1,0:T(8,128)(2,1)} %param.10) | copy-start | bytes 786436
  20.2 2.3 %collective-permute-start.5 = (bf16[128,1024]{1,0:T(8,128)(2,1)S(1)}, bf16[128,1024]{1,0:T(8,128)(2,1)S(1)}, u32[]{:S(2)}, u32[]{:S(2)}) collective-permute-start(bf16[128,1024]{1,0:T(8,128)(2,1)S(1)} %collective-permute-done.2.near_a), channel_id=1, source_target_pairs={{0,2},{2,0},{4,6},{6,4},{8,10},{10,8},{12,14},{14,12},{16,18},{18,... | collective-permute-start | bytes 786440 | tf_op jit(solution)/shard_map/ppermute | solution.py:344
  20.2 2.3 %collective-permute-start.6 = (bf16[128,1024]{1,0:T(8,128)(2,1)S(1)}, bf16[128,1024]{1,0:T(8,128)(2,1)S(1)}, u32[]{:S(2)}, u32[]{:S(2)}) collective-permute-start(bf16[128,1024]{1,0:T(8,128)(2,1)S(1)} %collective-permute-done.3.near_b), channel_id=1, source_target_pairs={{0,2},{2,0},{4,6},{6,4},{8,10},{10,8},{12,14},{14,12},{16,18},{18,... | collective-permute-start | bytes 786440 | tf_op jit(solution)/shard_map/ppermute | solution.py:344
  20.7 1.8 %collective-permute-start.7 = (bf16[128,1024]{1,0:T(8,128)(2,1)S(1)}, bf16[128,1024]{1,0:T(8,128)(2,1)S(1)}, u32[]{:S(2)}, u32[]{:S(2)}) collective-permute-start(bf16[128,1024]{1,0:T(8,128)(2,1)S(1)} %collective-permute-done.far_a), channel_id=1, source_target_pairs={{0,2},{2,0},{4,6},{6,4},{8,10},{10,8},{12,14},{14,12},{16,18},{18,... | collective-permute-start | bytes 786440 | tf_op jit(solution)/shard_map/ppermute | solution.py:344
  20.8 2.1 %collective-permute-start.8 = (bf16[128,1024]{1,0:T(8,128)(2,1)S(1)}, bf16[128,1024]{1,0:T(8,128)(2,1)S(1)}, u32[]{:S(2)}, u32[]{:S(2)}) collective-permute-start(bf16[128,1024]{1,0:T(8,128)(2,1)S(1)} %collective-permute-done.1.far_b), channel_id=1, source_target_pairs={{0,2},{2,0},{4,6},{6,4},{8,10},{10,8},{12,14},{14,12},{16,18},{18,... | collective-permute-start | bytes 786440 | tf_op jit(solution)/shard_map/ppermute | solution.py:344
  21.2 2.2 %copy-start = (bf16[4,512,1024]{2,1,0:T(8,128)(2,1)S(1)}, bf16[4,512,1024]{2,1,0:T(8,128)(2,1)}, u32[]{:S(2)}) copy-start(bf16[4,512,1024]{2,1,0:T(8,128)(2,1)} %constant.11.clone.tables) | copy-start | bytes 12582916
  25.1 1.5 %copy-start.3 = (bf16[1,512,512]{2,1,0:T(8,128)(2,1)S(1)}, bf16[1,512,512]{2,1,0:T(8,128)(2,1)}, u32[]{:S(2)}) copy-start(bf16[1,512,512]{2,1,0:T(8,128)(2,1)} %param.12) | copy-start | bytes 1572868
  25.2 1.5 %copy-start.5 = (s32[1,1,256,1]{2,3,1,0:T(1,128)S(1)}, s32[1,1,256,1]{2,3,1,0:T(1,128)}, u32[]{:S(2)}) copy-start(s32[1,1,256,1]{2,3,1,0:T(1,128)} %param.13) | copy-start | bytes 3076
  25.2 1.5 %copy-start.6 = (s32[1,1,256]{2,1,0:T(1,128)S(1)}, s32[1,1,256]{2,1,0:T(1,128)}, u32[]{:S(2)}) copy-start(s32[1,1,256]{2,1,0:T(1,128)} %param.14) | copy-start | bytes 3076
  25.2 1.5 %copy-start.7 = (s32[128]{0:T(128)S(1)}, s32[128]{0:T(128)}, u32[]{:S(2)}) copy-start(s32[128]{0:T(128)} %param.15) | copy-start | bytes 1540
  25.2 14.2 %collective-permute-start.9 = (bf16[256,1024]{1,0:T(8,128)(2,1)S(1)}, bf16[256,1024]{1,0:T(8,128)(2,1)S(1)}, u32[]{:S(2)}, u32[]{:S(2)}) collective-permute-start(bf16[256,1024]{1,0:T(8,128)(2,1)S(1)} %get-tuple-element.48), channel_id=1, source_target_pairs={{0,1},{1,0},{2,3},{3,2},{4,5},{5,4},{6,7},{7,6},{8,9},{9,8},{10,11... | collective-permute-start | bytes 1572872 | tf_op jit(solution)/shard_map/ppermute | solution.py:419

commit v8 on v7

--- a/solution.py
+++ b/solution.py
@@ -171,28 +171,24 @@
             right_side[below, second] = real_part
 
 
-def fetch(tables, cross, arrival):
-    copy = pltpu.make_async_copy(tables.at[whereabouts()[4]], cross, arrival)
-    copy.start()
-    return copy
-
-
-def first_kernel(
-    map_count, span, curvature, own_far, twin, tables, total, *rest
-):
+def first_kernel(map_count, span, curvature, own_far, twin, tables, total, *rest):
     later = 2 * len(GROUPS) - 2
-    cosines, sines, phased, right_side, cross, own, ranges, arrival, own_here, ranges_here = rest[
-        later:
-    ]
+    ranges, second, last, cosines, sines, phased, right_side, cross, own, arrivals = rest[later:]
     index = whereabouts()[4]
+    depth, side = ranges.shape
+    rows = cross.shape[0]
+    left, right = slice(0, side), slice(side, 2 * side)
+    moves = [
+        (own_far, own),
+        (tables.at[index, :depth, left], ranges),
+        (tables.at[index, depth : depth + rows, left], cross),
+        (tables.at[index, depth : depth + rows, right], second),
+        (tables.at[index, :rows, right], last.at[:, left]),
+        (tables.at[index, rows : 2 * rows, right], last.at[:, right]),
+    ]
     copies = [
-        pltpu.make_async_copy(own_far, own, own_here),
-        pltpu.make_async_copy(
-            tables.at[index, : ranges.shape[0], : ranges.shape[1]], ranges, ranges_here
-        ),
-        pltpu.make_async_copy(
-            tables.at[index, ranges.shape[0] :, : cross.shape[1]], cross, arrival
-        ),
+        pltpu.make_async_copy(source, target, arrivals.at[n])
+        for n, (source, target) in enumerate(moves)
     ]
     for copy in copies:
         copy.start()
@@ -204,17 +200,14 @@
 
 
 def second_kernel(
-    near_a, near_b, cosines, sines, ranges, tables, before, total,
-    phased, right_side, cross, arrival,
+    near_a, near_b, cosines, sines, ranges, cross, before, total, phased, right_side
 ):
-    copy = fetch(tables, cross, arrival)
     chip_odd = whereabouts()[1] == 1
     blocks = [
         lambda: jnp.where(chip_odd, near_a[...], near_b[...]),
         lambda: jnp.where(chip_odd, near_b[...], near_a[...]),
     ]
     transform(blocks, cosines, sines, ranges, phased, right_side)
-    copy.wait()
     total[...] = before[...] + jnp.dot(
         cross[...], right_side[...], preferred_element_type=jnp.float32
     )
@@ -227,9 +220,8 @@
 
 def last_kernel(
     twin_near_a, twin_near_b, far_a, far_b, twin_far_a, twin_far_b,
-    cosines, sines, ranges, tables, before, sent, right_side, phased, cross, arrival,
+    cosines, sines, ranges, cross, before, sent, right_side, phased,
 ):
-    copy = fetch(tables, cross, arrival)
     core, chip, group, here_map, _ = whereabouts()
     chip_odd, group_odd, from_a = chip == 1, group == 1, core != group
     blocks = [
@@ -239,7 +231,6 @@
         lambda: jnp.where(group_odd, far_b[...], far_a[...]),
     ]
     transform(blocks, cosines, sines, ranges, phased, right_side)
-    copy.wait()
     other = 1 - here_map
     sent[...] = (
         part_rows(before, other)
@@ -249,9 +240,7 @@
     ).astype(sent.dtype)
 
 
-def kept_kernel(right_side, tables, before, kept, cross, arrival):
-    copy = fetch(tables, cross, arrival)
-    copy.wait()
+def kept_kernel(right_side, cross, before, kept):
     here_map = whereabouts()[3]
     kept[...] = part_rows(before, here_map) + jnp.dot(
         part_rows(cross, here_map), right_side[...], preferred_element_type=jnp.float32
@@ -344,7 +333,7 @@
     return lax.ppermute(block, "blk", [(i, i ^ 1) for i in range(count)])
 
 
-def body(ranges, crosses, phase_history, tile_curvature, interp_weights, strip_tiles, row_offsets, tile_owner):
+def body(tables, phase_history, tile_curvature, interp_weights, strip_tiles, row_offsets, tile_owner):
     blk_count = lax.axis_size("blk")
     map_count = lax.axis_size("map")
     own_block = phase_history[0, 0]
@@ -364,54 +353,55 @@
     half_shape = (rows_here, 2 * columns)
     right = lambda n: pltpu.VMEM((n * deep, 2 * columns), jnp.bfloat16)
     spread = lambda n: pltpu.VMEM((2, n * pulse_count, freq_count), jnp.bfloat16)
-    table = lambda n: [
-        pltpu.VMEM((map_count * rows_here, n * deep), jnp.bfloat16),
-        pltpu.SemaphoreType.DMA,
-    ]
+    cross = lambda n: (map_count * rows_here, n * deep)
     flops = lambda n: 2 * n * pulse_count * 4 * columns * (freq_count + map_count * rows_here)
     n = GROUPS[0]
     smem, vmem, hbm = (
         pl.BlockSpec(memory_space=kind) for kind in (pltpu.SMEM, pltpu.VMEM, pltpu.HBM)
     )
-    total, *curves = pl.pallas_call(
+    outs = [
+        f32(*image_shape),
+        *(f32(size, pulse_count, freq_count) for size in GROUPS[1:] for _ in range(2)),
+        b16(2 * freq_count, freq_count),
+        b16(*cross(GROUPS[1])),
+        b16(*cross(GROUPS[2])),
+    ]
+    total, *curves, ranges, second_cross, last_cross = pl.pallas_call(
         functools.partial(first_kernel, map_count, STOPS * map_count * pulse_count),
-        out_shape=[f32(*image_shape)]
-        + [f32(size, pulse_count, freq_count) for size in GROUPS[1:] for _ in range(2)],
+        out_shape=outs,
         in_specs=[smem, hbm, vmem, hbm],
-        out_specs=[vmem] * (2 * len(GROUPS) - 1),
+        out_specs=[vmem] * len(outs),
         scratch_shapes=[pltpu.VMEM((n, pulse_count, freq_count), jnp.float32)] * 2
         + [
             spread(n),
             right(n),
-            table(n)[0],
+            pltpu.VMEM(cross(n), jnp.bfloat16),
             pltpu.VMEM(own_block.shape, jnp.bfloat16),
-            pltpu.VMEM(ranges.shape, jnp.bfloat16),
-        ]
-        + [pltpu.SemaphoreType.DMA] * 3,
+            pltpu.SemaphoreType.DMA((6,)),
+        ],
         compiler_params=pltpu.CompilerParams(vmem_limit_bytes=44 * 2**20),
         cost_estimate=pl.CostEstimate(flops=flops(n), bytes_accessed=0, transcendentals=2**18),
-    )(tile_curvature, own_block, twin, crosses[0])
-    far, near, total = lax.optimization_barrier((far, near, total))
+    )(tile_curvature, own_block, twin, tables)
+    *others, total = lax.optimization_barrier((far[1], far[0], near[1], near[0], total))
+    far, near = others[1::-1], others[:1:-1]
     twin_near = [swap(block, blk_count) for block in near]
     twin_far = [swap(block, blk_count) for block in far]
     n = GROUPS[1]
     [total] = call(
         second_kernel,
         [f32(*image_shape)],
-        [*near, *curves[:2], ranges, crosses[1], total],
-        [spread(n), right(n), *table(n)],
+        [*near, *curves[:2], ranges, second_cross, total],
+        [spread(n), right(n)],
         flops(n),
-        far=(5,),
     )
     twin_near, twin_far, total = lax.optimization_barrier((twin_near, twin_far, total))
     n = GROUPS[2]
     sent, right_side = call(
         last_kernel,
         [b16(*half_shape), b16(n * deep, 2 * columns)],
-        [*twin_near, *far, *twin_far, *curves[2:], ranges, crosses[2], total],
-        [spread(n), *table(n)],
+        [*twin_near, *far, *twin_far, *curves[2:], ranges, last_cross, total],
+        [spread(n)],
         flops(n),
-        far=(9,),
     )
     sent, right_side, strip_tiles, row_offsets, interp_weights = lax.optimization_barrier(
         (sent, right_side, strip_tiles, row_offsets, interp_weights)
@@ -428,13 +418,7 @@
             interp_weights[0],
         ],
     )
-    [kept] = call(
-        kept_kernel,
-        [f32(*half_shape)],
-        [right_side, crosses[2], total],
-        table(n),
-        far=(1,),
-    )
+    [kept] = call(kept_kernel, [f32(*half_shape)], [right_side, last_cross, total])
 
     wide = 4 * columns + SIDE
     [packed] = call(
@@ -468,13 +452,17 @@
 
     def run(*args):
         map_count, pulse_count, width = args[0].shape[1:]
-        ranges = jnp.asarray(range_tables(width // 2))
-        crosses = cross_tables(map_count, map_count * args[3].shape[2], pulse_count)
-        first = np.zeros((len(crosses[0]), width + crosses[0].shape[1], width), crosses[0].dtype)
-        first[:, :width, : width // 2] = range_tables(width // 2)
-        first[:, width : , : crosses[0].shape[2]] = crosses[0]
-        crosses = [jnp.asarray(table) for table in (first, *crosses[1:])]
-        held = lambda *here: body(ranges, crosses, *here)
+        side = width // 2
+        first, second, last = cross_tables(map_count, map_count * args[3].shape[2], pulse_count)
+        rows = first.shape[1]
+        tables = np.zeros((len(first), width + rows, width), first.dtype)
+        tables[:, :width, :side] = range_tables(side)
+        tables[:, width:, :side] = first
+        tables[:, width:, side:] = second
+        tables[:, :rows, side:] = last[:, :, :side]
+        tables[:, rows : 2 * rows, side:] = last[:, :, side:]
+        tables = jnp.asarray(tables)
+        held = lambda *here: body(tables, *here)
         return jax.shard_map(
             held, mesh=mesh, in_specs=in_specs, out_specs=out_specs, check_vma=False
         )(*args)

time: 89.1 us -> 89 us (level)
  waiting for transfers between devices: 18.9 us -> 20 us
    ppermute x2, waiting for transfers between devices: 0.01 us -> 1.88 us  [body(): lax.ppermute(own_block, 'blk', matching(blk_count, 4, p))]
    ppermute x2, starting transfers between devices: 2.38 us -> 1.19 us  [body(): lax.ppermute(own_block, 'blk', matching(blk_count, 4, p))]
    pallas_call x1, Pallas kernels: 4.44 us -> 5.37 us  [body(): pl.pallas_call(functools.partial(first_kernel, map_count, STOPS * map_cou...]
  transfers between devices with their start and end apart: 10 -> 10, of which waited for: 4 -> 6; matrix products, arithmetic and copies ran while one was open for 0% -> 0% of each run, Pallas kernels for 8% -> 9%
where the time goes in v8:
time: 89 us; the launch traced here: 88.8 us
  blocking collectives  46.4 us (52%)
  waiting for transfers between devices  20 us (22%)
  Pallas kernels  11.8 us (13%)
  starting transfers between devices  8.88 us (10%)
  local copies, waits for them, and re-layouts  0.97 us (1%)
    all_to_all x1, blocking collectives, body(): got = lax.all_to_all(packed, 'blk', split_axis=0, concat_axis=0, tiled=True)  46.4 us
    ppermute x1, waiting for transfers between devices, body(): arrived = lax.ppermute(sent, 'map', [(0, 1), (1, 0)])  11.7 us
    pallas_call x6, Pallas kernels, call(): pl.pallas_call(kernel, out_shape=outs, in_specs=specs, out_specs=[pl.Bloc...  6.4 us
    ppermute x2, waiting for transfers between devices, body(): lax.ppermute(own_block, 'blk', matching(blk_count, 2, p))  6.04 us
    ppermute x2, starting transfers between devices, body(): lax.ppermute(own_block, 'blk', matching(blk_count, 2, p))  5.53 us
    pallas_call x1, Pallas kernels, body(): pl.pallas_call(functools.partial(first_kernel, map_count, STOPS * map_cou...  5.37 us
    ppermute x2, waiting for transfers between devices, body(): lax.ppermute(own_block, 'blk', matching(blk_count, 4, p))  1.88 us
  transfers between devices with their start and end apart: 10, of which 6 were waited for; matrix products, arithmetic and copies ran while one was open for 0% of the time, Pallas kernels for 9%

profile of v8, /device:TPU:32, one launch (start us, length us, event | category | flops | bytes accessed | tf_op | source)
XLA Modules:
  0.0 88.8 jit_solution(2610317262423371689)
XLA Ops:
  0.0 3.0 %collective-permute-start.3 = (bf16[128,1024]{1,0:T(8,128)(2,1)}, bf16[128,1024]{1,0:T(8,128)(2,1)S(1)}, u32[]{:S(2)}, u32[]{:S(2)}) collective-permute-start(bf16[128,1024]{1,0:T(8,128)(2,1)} %bitcast.8), channel_id=1, source_target_pairs={{0,4},{4,0},{8,12},{12,8},{16,20},{20,16},{24,28},{28,24},{32,36},... | collective-permute-start | bytes 786440 | tf_op jit(solution)/shard_map/ppermute | solution.py:345
  3.0 2.5 %collective-permute-start.2 = (bf16[128,1024]{1,0:T(8,128)(2,1)}, bf16[128,1024]{1,0:T(8,128)(2,1)S(1)}, u32[]{:S(2)}, u32[]{:S(2)}) collective-permute-start(bf16[128,1024]{1,0:T(8,128)(2,1)} %bitcast.9), channel_id=1, source_target_pairs={{4,8},{8,4},{12,16},{16,12},{20,24},{24,20},{28,32},{32,28},{36,40... | collective-permute-start | bytes 786440 | tf_op jit(solution)/shard_map/ppermute | solution.py:345
  5.5 1.2 %collective-permute-start = (bf16[128,1024]{1,0:T(8,128)(2,1)}, bf16[128,1024]{1,0:T(8,128)(2,1)S(1)}, u32[]{:S(2)}, u32[]{:S(2)}) collective-permute-start(bf16[128,1024]{1,0:T(8,128)(2,1)} %bitcast.11), channel_id=1, source_target_pairs={{8,16},{16,8},{24,32},{32,24},{40,48},{48,40},{56,64},{64,56},{72,... | collective-permute-start | bytes 786440 | tf_op jit(solution)/shard_map/ppermute | solution.py:346
  7.4 0.9 %copy-done.1 = bf16[1,1,128,1024]{3,2,1,0:T(8,128)(2,1)S(1)} copy-done((bf16[1,1,128,1024]{3,2,1,0:T(8,128)(2,1)S(1)}, bf16[1,1,128,1024]{3,2,1,0:T(8,128)(2,1)}, u32[]{:S(2)}) %copy-start.1) | copy-done | bytes 262168
  8.3 5.4 %shard_map.73 = (f32[512,1024]{1,0:T(8,128)S(1)}, f32[2,128,512]{2,1,0:T(8,128)S(1)}, f32[2,128,512]{2,1,0:T(8,128)S(1)}, f32[4,128,512]{2,1,0:T(8,128)S(1)}, f3...) custom-call(f32[1]{0:T(128)S(6)} %copy.8.curvature, ...), custom_call_target="tpu_custom_call" | custom-call | flops 1073741824 | tf_op jit(solution)/shard_map/pallas_call | solution.py:369
  13.7 3.9 %collective-permute-done.3.near_a = bf16[128,1024]{1,0:T(8,128)(2,1)S(1)} collective-permute-done((bf16[128,1024]{1,0:T(8,128)(2,1)}, bf16[128,1024]{1,0:T(8,128)(2,1)S(1)}, u32[]{:S(2)}, u32[]{:S(2)}) %collective-permute-start.3) | collective-permute-done | bytes 262176 | tf_op jit(solution)/shard_map/ppermute | solution.py:345
  17.6 2.1 %collective-permute-done.2.near_b = bf16[128,1024]{1,0:T(8,128)(2,1)S(1)} collective-permute-done((bf16[128,1024]{1,0:T(8,128)(2,1)}, bf16[128,1024]{1,0:T(8,128)(2,1)S(1)}, u32[]{:S(2)}, u32[]{:S(2)}) %collective-permute-start.2) | collective-permute-done | bytes 262176 | tf_op jit(solution)/shard_map/ppermute | solution.py:345
  19.8 1.9 %collective-permute-done.far_b = bf16[128,1024]{1,0:T(8,128)(2,1)S(1)} collective-permute-done((bf16[128,1024]{1,0:T(8,128)(2,1)}, bf16[128,1024]{1,0:T(8,128)(2,1)S(1)}, u32[]{:S(2)}, u32[]{:S(2)}) %collective-permute-start) | collective-permute-done | bytes 262176 | tf_op jit(solution)/shard_map/ppermute | solution.py:346
  21.6 0.5 collective-permute-start.6
  22.1 0.5 collective-permute-start.8
  22.7 1.2 %shard_map.74.before = f32[512,1024]{1,0:T(8,128)S(1)} custom-call(bf16[128,1024]{1,0:T(8,128)(2,1)S(1)} %collective-permute-done.3.near_a, bf16[128,1024]{1,0:T(8,128)(2,1)S(1)} %collective-permute-done.2.near_b, f32[2,128,512]{2,1,0:T(8,128)S(1)} %get-tuple-element.38.cosines, f32[2,128,512]{2,1,0:T(8,128)S(1)} %get-tuple-element.39.sines, ...), custom_call_target="tpu_custom_call" | custom-call | flops 1073741824 | bytes 7340032 | tf_op jit(solution)/shard_map/pallas_call | solution.py:79
  23.9 0.1 collective-permute-done.7.twin_far_a
  23.9 0.4 collective-permute-done.8.twin_far_b
  24.3 1.5 %shard_map.75 = (bf16[256,1024]{1,0:T(8,128)(2,1)S(1)}, bf16[1024,1024]{1,0:T(8,128)(2,1)S(1)}) custom-call(bf16[128,1024]{1,0:T(8,128)(2,1)S(1)} %collective-permute-done.5.twin_near_a, bf16[128,1024]{1,0:T(8,128)(2,1)S(1)} %collective-permute-done.6.twin_near_b, bf16[128,1024]{1,0:T(8,128)(2,1)S(1)} %collective-permute-done.1.far_a, ...), custom_call_target="tpu_custom_call" | custom-call | flops 2147483648 | bytes 10485760 | tf_op jit(solution)/shard_map/pallas_call | solution.py:79
  25.8 0.0 copy-start
  25.8 0.0 copy-start.2
  25.8 0.0 copy-start.3
  25.9 1.1 %collective-permute-start.9 = (bf16[256,1024]{1,0:T(8,128)(2,1)S(1)}, bf16[256,1024]{1,0:T(8,128)(2,1)S(1)}, u32[]{:S(2)}, u32[]{:S(2)}) collective-permute-start(bf16[256,1024]{1,0:T(8,128)(2,1)S(1)} %get-tuple-element.54), channel_id=1, source_target_pairs={{0,1},{1,0},{2,3},{3,2},{4,5},{5,4},{6,7},{7,6},{8,9},{9,8},{10,11... | collective-permute-start | bytes 1572872 | tf_op jit(solution)/shard_map/ppermute | solution.py:409
  27.0 0.7 shard_map.76.kept
  27.8 0.7 shard_map.77
  28.4 11.7 %collective-permute-done.9.arrived = bf16[256,1024]{1,0:T(8,128)(2,1)S(1)} collective-permute-done((bf16[256,1024]{1,0:T(8,128)(2,1)S(1)}, bf16[256,1024]{1,0:T(8,128)(2,1)S(1)}, u32[]{:S(2)}, u32[]{:S(2)}) %collective-permute-start.9) | collective-permute-done | bytes 524320 | tf_op jit(solution)/shard_map/ppermute | solution.py:409
  40.1 0.5 shard_map.78
  40.6 46.4 %all_to_all.5.got = bf16[128,2,2176]{2,1,0:T(2,128)(2,1)S(1)} all-to-all(bf16[128,2,2176]{2,1,0:T(2,128)(2,1)S(1)} %shard_map.78), channel_id=1, replica_groups=mesh['blk'=128,'map'=2] {'blk'}, dimensions={0} | all-to-all | bytes 2228224 | tf_op jit(solution)/shard_map/all_to_all | solution.py:431
  87.0 1.8 %shard_map.79 = f32[256,512]{1,0:T(8,128)} custom-call(bf16[128,2,2176]{2,1,0:T(2,128)(2,1)S(1)} %all_to_all.5.got, bf16[512,512]{1,0:T(8,128)(2,1)S(1)} %get-tuple-element.60.weights), custom_call_target="tpu_custom_call" | custom-call | flops 805306368 | bytes 2162688 | tf_op jit(solution)/shard_map/pallas_call | solution.py:79
  (14 shorter events, 0.0 us)
Async XLA Ops:
  0.0 7.4 %collective-permute-start.4 = (bf16[128,1024]{1,0:T(8,128)(2,1)}, bf16[128,1024]{1,0:T(8,128)(2,1)S(1)}, u32[]{:S(2)}, u32[]{:S(2)}) collective-permute-start(bf16[128,1024]{1,0:T(8,128)(2,1)} %bitcast.7), channel_id=1, source_target_pairs={{0,2},{2,0},{4,6},{6,4},{8,10},{10,8},{12,14},{14,12},{16,18},{18,... | collective-permute-start | bytes 786440 | tf_op jit(solution)/shard_map/ppermute | solution.py:333
  0.0 17.6 %collective-permute-start.3 = (bf16[128,1024]{1,0:T(8,128)(2,1)}, bf16[128,1024]{1,0:T(8,128)(2,1)S(1)}, u32[]{:S(2)}, u32[]{:S(2)}) collective-permute-start(bf16[128,1024]{1,0:T(8,128)(2,1)} %bitcast.8), channel_id=1, source_target_pairs={{0,4},{4,0},{8,12},{12,8},{16,20},{20,16},{24,28},{28,24},{32,36},... | collective-permute-start | bytes 786440 | tf_op jit(solution)/shard_map/ppermute | solution.py:345
  3.0 16.7 %collective-permute-start.2 = (bf16[128,1024]{1,0:T(8,128)(2,1)}, bf16[128,1024]{1,0:T(8,128)(2,1)S(1)}, u32[]{:S(2)}, u32[]{:S(2)}) collective-permute-start(bf16[128,1024]{1,0:T(8,128)(2,1)} %bitcast.9), channel_id=1, source_target_pairs={{4,8},{8,4},{12,16},{16,12},{20,24},{24,20},{28,32},{32,28},{36,40... | collective-permute-start | bytes 786440 | tf_op jit(solution)/shard_map/ppermute | solution.py:345
  5.5 14.2 %collective-permute-start.1 = (bf16[128,1024]{1,0:T(8,128)(2,1)}, bf16[128,1024]{1,0:T(8,128)(2,1)S(1)}, u32[]{:S(2)}, u32[]{:S(2)}) collective-permute-start(bf16[128,1024]{1,0:T(8,128)(2,1)} %bitcast.10), channel_id=1, source_target_pairs={{0,8},{8,0},{16,24},{24,16},{32,40},{40,32},{48,56},{56,48},{64,72... | collective-permute-start | bytes 786440 | tf_op jit(solution)/shard_map/ppermute | solution.py:346
  5.5 16.1 %collective-permute-start = (bf16[128,1024]{1,0:T(8,128)(2,1)}, bf16[128,1024]{1,0:T(8,128)(2,1)S(1)}, u32[]{:S(2)}, u32[]{:S(2)}) collective-permute-start(bf16[128,1024]{1,0:T(8,128)(2,1)} %bitcast.11), channel_id=1, source_target_pairs={{8,16},{16,8},{24,32},{32,24},{40,48},{48,40},{56,64},{64,56},{72,... | collective-permute-start | bytes 786440 | tf_op jit(solution)/shard_map/ppermute | solution.py:346
  7.4 1.0 %copy-start.1 = (bf16[1,1,128,1024]{3,2,1,0:T(8,128)(2,1)S(1)}, bf16[1,1,128,1024]{3,2,1,0:T(8,128)(2,1)}, u32[]{:S(2)}) copy-start(bf16[1,1,128,1024]{3,2,1,0:T(8,128)(2,1)} %param.7) | copy-start | bytes 786436
  21.6 2.2 %collective-permute-start.5 = (bf16[128,1024]{1,0:T(8,128)(2,1)S(1)}, bf16[128,1024]{1,0:T(8,128)(2,1)S(1)}, u32[]{:S(2)}, u32[]{:S(2)}) collective-permute-start(bf16[128,1024]{1,0:T(8,128)(2,1)S(1)} %collective-permute-done.3.near_a), channel_id=1, source_target_pairs={{0,2},{2,0},{4,6},{6,4},{8,10},{10,8},{12,14},{14,12},{16,18},{18,... | collective-permute-start | bytes 786440 | tf_op jit(solution)/shard_map/ppermute | solution.py:333
  21.6 2.2 %collective-permute-start.6 = (bf16[128,1024]{1,0:T(8,128)(2,1)S(1)}, bf16[128,1024]{1,0:T(8,128)(2,1)S(1)}, u32[]{:S(2)}, u32[]{:S(2)}) collective-permute-start(bf16[128,1024]{1,0:T(8,128)(2,1)S(1)} %collective-permute-done.2.near_b), channel_id=1, source_target_pairs={{0,2},{2,0},{4,6},{6,4},{8,10},{10,8},{12,14},{14,12},{16,18},{18,... | collective-permute-start | bytes 786440 | tf_op jit(solution)/shard_map/ppermute | solution.py:333
  22.1 1.8 %collective-permute-start.7 = (bf16[128,1024]{1,0:T(8,128)(2,1)S(1)}, bf16[128,1024]{1,0:T(8,128)(2,1)S(1)}, u32[]{:S(2)}, u32[]{:S(2)}) collective-permute-start(bf16[128,1024]{1,0:T(8,128)(2,1)S(1)} %collective-permute-done.1.far_a), channel_id=1, source_target_pairs={{0,2},{2,0},{4,6},{6,4},{8,10},{10,8},{12,14},{14,12},{16,18},{18,... | collective-permute-start | bytes 786440 | tf_op jit(solution)/shard_map/ppermute | solution.py:333
  22.1 2.1 %collective-permute-start.8 = (bf16[128,1024]{1,0:T(8,128)(2,1)S(1)}, bf16[128,1024]{1,0:T(8,128)(2,1)S(1)}, u32[]{:S(2)}, u32[]{:S(2)}) collective-permute-start(bf16[128,1024]{1,0:T(8,128)(2,1)S(1)} %collective-permute-done.far_b), channel_id=1, source_target_pairs={{0,2},{2,0},{4,6},{6,4},{8,10},{10,8},{12,14},{14,12},{16,18},{18,... | collective-permute-start | bytes 786440 | tf_op jit(solution)/shard_map/ppermute | solution.py:333
  25.8 1.9 %copy-start = (bf16[1,512,512]{2,1,0:T(8,128)(2,1)S(1)}, bf16[1,512,512]{2,1,0:T(8,128)(2,1)}, u32[]{:S(2)}) copy-start(bf16[1,512,512]{2,1,0:T(8,128)(2,1)} %param.9) | copy-start | bytes 1572868
  25.8 1.9 %copy-start.2 = (s32[1,1,256,1]{2,3,1,0:T(1,128)S(1)}, s32[1,1,256,1]{2,3,1,0:T(1,128)}, u32[]{:S(2)}) copy-start(s32[1,1,256,1]{2,3,1,0:T(1,128)} %param.10) | copy-start | bytes 3076
  25.8 1.9 %copy-start.3 = (s32[1,1,256]{2,1,0:T(1,128)S(1)}, s32[1,1,256]{2,1,0:T(1,128)}, u32[]{:S(2)}) copy-start(s32[1,1,256]{2,1,0:T(1,128)} %param.11) | copy-start | bytes 3076
  25.9 1.9 %copy-start.4 = (s32[128]{0:T(128)S(1)}, s32[128]{0:T(128)}, u32[]{:S(2)}) copy-start(s32[128]{0:T(128)} %param.12) | copy-start | bytes 1540
  25.9 14.2 %collective-permute-start.9 = (bf16[256,1024]{1,0:T(8,128)(2,1)S(1)}, bf16[256,1024]{1,0:T(8,128)(2,1)S(1)}, u32[]{:S(2)}, u32[]{:S(2)}) collective-permute-start(bf16[256,1024]{1,0:T(8,128)(2,1)S(1)} %get-tuple-element.54), channel_id=1, source_target_pairs={{0,1},{1,0},{2,3},{3,2},{4,5},{5,4},{6,7},{7,6},{8,9},{9,8},{10,11... | collective-permute-start | bytes 1572872 | tf_op jit(solution)/shard_map/ppermute | solution.py:409

commit v9 on v8

--- a/solution.py
+++ b/solution.py
@@ -193,10 +193,12 @@
     for copy in copies:
         copy.start()
     phase_factors(map_count, span, curvature, (cosines, sines, *rest[:later]))
-    for copy in copies:
+    for copy in copies[:3]:
         copy.wait()
     transform([lambda: own[...], lambda: twin[...]], cosines, sines, ranges, phased, right_side)
     total[...] = jnp.dot(cross[...], right_side[...], preferred_element_type=jnp.float32)
+    for copy in copies[3:]:
+        copy.wait()
 
 
 def second_kernel(
@@ -382,8 +384,8 @@
         compiler_params=pltpu.CompilerParams(vmem_limit_bytes=44 * 2**20),
         cost_estimate=pl.CostEstimate(flops=flops(n), bytes_accessed=0, transcendentals=2**18),
     )(tile_curvature, own_block, twin, tables)
-    *others, total = lax.optimization_barrier((far[1], far[0], near[1], near[0], total))
-    far, near = others[1::-1], others[:1:-1]
+    *others, total = lax.optimization_barrier((far[0], far[1], near[0], near[1], total))
+    far, near = [others[0], others[1]], [others[2], others[3]]
     twin_near = [swap(block, blk_count) for block in near]
     twin_far = [swap(block, blk_count) for block in far]
     n = GROUPS[1]

time: 89 us -> 88.4 us (level)
  waiting for transfers between devices: 20 us -> 18.9 us
    ppermute x2, waiting for transfers between devices: 1.88 us -> 0.01 us  [body(): lax.ppermute(own_block, 'blk', matching(blk_count, 4, p))]
    ppermute x2, starting transfers between devices: 1.19 us -> 2.38 us  [body(): lax.ppermute(own_block, 'blk', matching(blk_count, 4, p))]
  transfers between devices with their start and end apart: 10 -> 10, of which waited for: 6 -> 5; matrix products, arithmetic and copies ran while one was open for 0% -> 0% of each run, Pallas kernels for 9% -> 8%
where the time goes in v9:
time: 88.4 us; the launch traced here: 88.2 us
  blocking collectives  47.2 us (53%)
  waiting for transfers between devices  18.9 us (21%)
  Pallas kernels  11.3 us (13%)
  starting transfers between devices  9.07 us (10%)
  local copies, waits for them, and re-layouts  0.97 us (1%)
    all_to_all x1, blocking collectives, body(): got = lax.all_to_all(packed, 'blk', split_axis=0, concat_axis=0, tiled=True)  47.2 us
    ppermute x1, waiting for transfers between devices, body(): arrived = lax.ppermute(sent, 'map', [(0, 1), (1, 0)])  12.2 us
    pallas_call x6, Pallas kernels, call(): pl.pallas_call(kernel, out_shape=outs, in_specs=specs, out_specs=[pl.Bloc...  6.42 us
    ppermute x2, waiting for transfers between devices, body(): lax.ppermute(own_block, 'blk', matching(blk_count, 2, p))  6.24 us
    ppermute x2, starting transfers between devices, body(): lax.ppermute(own_block, 'blk', matching(blk_count, 2, p))  5.02 us
    pallas_call x1, Pallas kernels, body(): pl.pallas_call(functools.partial(first_kernel, map_count, STOPS * map_cou...  4.91 us
    ppermute x2, starting transfers between devices, body(): lax.ppermute(own_block, 'blk', matching(blk_count, 4, p))  2.38 us
  transfers between devices with their start and end apart: 10, of which 5 were waited for; matrix products, arithmetic and copies ran while one was open for 0% of the time, Pallas kernels for 8%

profile of v9, /device:TPU:32, one launch (start us, length us, event | category | flops | bytes accessed | tf_op | source)
XLA Modules:
  0.0 88.2 jit_solution(8750105746015277617)
XLA Ops:
  0.0 5.0 %collective-permute-start.3 = (bf16[128,1024]{1,0:T(8,128)(2,1)}, bf16[128,1024]{1,0:T(8,128)(2,1)S(1)}, u32[]{:S(2)}, u32[]{:S(2)}) collective-permute-start(bf16[128,1024]{1,0:T(8,128)(2,1)} %bitcast.8), channel_id=1, source_target_pairs={{4,8},{8,4},{12,16},{16,12},{20,24},{24,20},{28,32},{32,28},{36,40... | collective-permute-start | bytes 786440 | tf_op jit(solution)/shard_map/ppermute | solution.py:347
  5.0 2.1 %collective-permute-start.1 = (bf16[128,1024]{1,0:T(8,128)(2,1)}, bf16[128,1024]{1,0:T(8,128)(2,1)S(1)}, u32[]{:S(2)}, u32[]{:S(2)}) collective-permute-start(bf16[128,1024]{1,0:T(8,128)(2,1)} %bitcast.10), channel_id=1, source_target_pairs={{8,16},{16,8},{24,32},{32,24},{40,48},{48,40},{56,64},{64,56},{72,... | collective-permute-start | bytes 786440 | tf_op jit(solution)/shard_map/ppermute | solution.py:348
  7.1 0.3 collective-permute-start
  8.1 0.9 %copy-done.1 = bf16[1,1,128,1024]{3,2,1,0:T(8,128)(2,1)S(1)} copy-done((bf16[1,1,128,1024]{3,2,1,0:T(8,128)(2,1)S(1)}, bf16[1,1,128,1024]{3,2,1,0:T(8,128)(2,1)}, u32[]{:S(2)}) %copy-start.1) | copy-done | bytes 262168
  9.0 4.9 %shard_map.73 = (f32[512,1024]{1,0:T(8,128)S(1)}, f32[2,128,512]{2,1,0:T(8,128)S(1)}, f32[2,128,512]{2,1,0:T(8,128)S(1)}, f32[4,128,512]{2,1,0:T(8,128)S(1)}, f3...) custom-call(f32[1]{0:T(128)S(6)} %copy.8.curvature, ...), custom_call_target="tpu_custom_call" | custom-call | flops 1073741824 | tf_op jit(solution)/shard_map/pallas_call | solution.py:371
  13.9 1.9 %collective-permute-done.3.near_b = bf16[128,1024]{1,0:T(8,128)(2,1)S(1)} collective-permute-done((bf16[128,1024]{1,0:T(8,128)(2,1)}, bf16[128,1024]{1,0:T(8,128)(2,1)S(1)}, u32[]{:S(2)}, u32[]{:S(2)}) %collective-permute-start.3) | collective-permute-done | bytes 262176 | tf_op jit(solution)/shard_map/ppermute | solution.py:347
  15.8 4.4 %collective-permute-done.2.near_a = bf16[128,1024]{1,0:T(8,128)(2,1)S(1)} collective-permute-done((bf16[128,1024]{1,0:T(8,128)(2,1)}, bf16[128,1024]{1,0:T(8,128)(2,1)S(1)}, u32[]{:S(2)}, u32[]{:S(2)}) %collective-permute-start.2) | collective-permute-done | bytes 262176 | tf_op jit(solution)/shard_map/ppermute | solution.py:347
  20.2 0.5 collective-permute-start.6
  20.7 0.1 collective-permute-start.7
  20.8 0.4 collective-permute-start.8
  21.2 1.2 %shard_map.74.before = f32[512,1024]{1,0:T(8,128)S(1)} custom-call(bf16[128,1024]{1,0:T(8,128)(2,1)S(1)} %collective-permute-done.2.near_a, bf16[128,1024]{1,0:T(8,128)(2,1)S(1)} %collective-permute-done.3.near_b, f32[2,128,512]{2,1,0:T(8,128)S(1)} %get-tuple-element.38.cosines, f32[2,128,512]{2,1,0:T(8,128)S(1)} %get-tuple-element.39.sines, ...), custom_call_target="tpu_custom_call" | custom-call | flops 1073741824 | bytes 7340032 | tf_op jit(solution)/shard_map/pallas_call | solution.py:79
  22.4 0.1 collective-permute-done.7.twin_far_a
  22.5 0.4 collective-permute-done.8.twin_far_b
  22.8 1.5 %shard_map.75 = (bf16[256,1024]{1,0:T(8,128)(2,1)S(1)}, bf16[1024,1024]{1,0:T(8,128)(2,1)S(1)}) custom-call(bf16[128,1024]{1,0:T(8,128)(2,1)S(1)} %collective-permute-done.5.twin_near_a, bf16[128,1024]{1,0:T(8,128)(2,1)S(1)} %collective-permute-done.6.twin_near_b, bf16[128,1024]{1,0:T(8,128)(2,1)S(1)} %collective-permute-done.far_a, ...), custom_call_target="tpu_custom_call" | custom-call | flops 2147483648 | bytes 10485760 | tf_op jit(solution)/shard_map/pallas_call | solution.py:79
  24.4 0.0 copy-start
  24.4 0.0 copy-start.3
  24.4 0.0 copy-start.4
  24.4 0.6 collective-permute-start.9
  25.1 0.7 shard_map.76.kept
  25.8 0.7 shard_map.77
  26.5 12.2 %collective-permute-done.9.arrived = bf16[256,1024]{1,0:T(8,128)(2,1)S(1)} collective-permute-done((bf16[256,1024]{1,0:T(8,128)(2,1)S(1)}, bf16[256,1024]{1,0:T(8,128)(2,1)S(1)}, u32[]{:S(2)}, u32[]{:S(2)}) %collective-permute-start.9) | collective-permute-done | bytes 524320 | tf_op jit(solution)/shard_map/ppermute | solution.py:411
  38.6 0.5 shard_map.78
  39.1 47.2 %all_to_all.5.got = bf16[128,2,2176]{2,1,0:T(2,128)(2,1)S(1)} all-to-all(bf16[128,2,2176]{2,1,0:T(2,128)(2,1)S(1)} %shard_map.78), channel_id=1, replica_groups=mesh['blk'=128,'map'=2] {'blk'}, dimensions={0} | all-to-all | bytes 2228224 | tf_op jit(solution)/shard_map/all_to_all | solution.py:433
  86.4 1.9 %shard_map.79 = f32[256,512]{1,0:T(8,128)} custom-call(bf16[128,2,2176]{2,1,0:T(2,128)(2,1)S(1)} %all_to_all.5.got, bf16[512,512]{1,0:T(8,128)(2,1)S(1)} %get-tuple-element.60.weights), custom_call_target="tpu_custom_call" | custom-call | flops 805306368 | bytes 2162688 | tf_op jit(solution)/shard_map/pallas_call | solution.py:79
  (14 shorter events, 0.0 us)
Async XLA Ops:
  0.0 8.1 %collective-permute-start.4 = (bf16[128,1024]{1,0:T(8,128)(2,1)}, bf16[128,1024]{1,0:T(8,128)(2,1)S(1)}, u32[]{:S(2)}, u32[]{:S(2)}) collective-permute-start(bf16[128,1024]{1,0:T(8,128)(2,1)} %bitcast.7), channel_id=1, source_target_pairs={{0,2},{2,0},{4,6},{6,4},{8,10},{10,8},{12,14},{14,12},{16,18},{18,... | collective-permute-start | bytes 786440 | tf_op jit(solution)/shard_map/ppermute | solution.py:335
  0.0 15.8 %collective-permute-start.3 = (bf16[128,1024]{1,0:T(8,128)(2,1)}, bf16[128,1024]{1,0:T(8,128)(2,1)S(1)}, u32[]{:S(2)}, u32[]{:S(2)}) collective-permute-start(bf16[128,1024]{1,0:T(8,128)(2,1)} %bitcast.8), channel_id=1, source_target_pairs={{4,8},{8,4},{12,16},{16,12},{20,24},{24,20},{28,32},{32,28},{36,40... | collective-permute-start | bytes 786440 | tf_op jit(solution)/shard_map/ppermute | solution.py:347
  5.0 15.2 %collective-permute-start.2 = (bf16[128,1024]{1,0:T(8,128)(2,1)}, bf16[128,1024]{1,0:T(8,128)(2,1)S(1)}, u32[]{:S(2)}, u32[]{:S(2)}) collective-permute-start(bf16[128,1024]{1,0:T(8,128)(2,1)} %bitcast.9), channel_id=1, source_target_pairs={{0,4},{4,0},{8,12},{12,8},{16,20},{20,16},{24,28},{28,24},{32,36},... | collective-permute-start | bytes 786440 | tf_op jit(solution)/shard_map/ppermute | solution.py:347
  5.0 15.2 %collective-permute-start.1 = (bf16[128,1024]{1,0:T(8,128)(2,1)}, bf16[128,1024]{1,0:T(8,128)(2,1)S(1)}, u32[]{:S(2)}, u32[]{:S(2)}) collective-permute-start(bf16[128,1024]{1,0:T(8,128)(2,1)} %bitcast.10), channel_id=1, source_target_pairs={{8,16},{16,8},{24,32},{32,24},{40,48},{48,40},{56,64},{64,56},{72,... | collective-permute-start | bytes 786440 | tf_op jit(solution)/shard_map/ppermute | solution.py:348
  7.1 13.1 %collective-permute-start = (bf16[128,1024]{1,0:T(8,128)(2,1)}, bf16[128,1024]{1,0:T(8,128)(2,1)S(1)}, u32[]{:S(2)}, u32[]{:S(2)}) collective-permute-start(bf16[128,1024]{1,0:T(8,128)(2,1)} %bitcast.11), channel_id=1, source_target_pairs={{0,8},{8,0},{16,24},{24,16},{32,40},{40,32},{48,56},{56,48},{64,72... | collective-permute-start | bytes 786440 | tf_op jit(solution)/shard_map/ppermute | solution.py:348
  8.1 1.0 %copy-start.1 = (bf16[1,1,128,1024]{3,2,1,0:T(8,128)(2,1)S(1)}, bf16[1,1,128,1024]{3,2,1,0:T(8,128)(2,1)}, u32[]{:S(2)}) copy-start(bf16[1,1,128,1024]{3,2,1,0:T(8,128)(2,1)} %param.7) | copy-start | bytes 786436
  20.2 2.2 %collective-permute-start.5 = (bf16[128,1024]{1,0:T(8,128)(2,1)S(1)}, bf16[128,1024]{1,0:T(8,128)(2,1)S(1)}, u32[]{:S(2)}, u32[]{:S(2)}) collective-permute-start(bf16[128,1024]{1,0:T(8,128)(2,1)S(1)} %collective-permute-done.2.near_a), channel_id=1, source_target_pairs={{0,2},{2,0},{4,6},{6,4},{8,10},{10,8},{12,14},{14,12},{16,18},{18,... | collective-permute-start | bytes 786440 | tf_op jit(solution)/shard_map/ppermute | solution.py:335
  20.2 2.2 %collective-permute-start.6 = (bf16[128,1024]{1,0:T(8,128)(2,1)S(1)}, bf16[128,1024]{1,0:T(8,128)(2,1)S(1)}, u32[]{:S(2)}, u32[]{:S(2)}) collective-permute-start(bf16[128,1024]{1,0:T(8,128)(2,1)S(1)} %collective-permute-done.3.near_b), channel_id=1, source_target_pairs={{0,2},{2,0},{4,6},{6,4},{8,10},{10,8},{12,14},{14,12},{16,18},{18,... | collective-permute-start | bytes 786440 | tf_op jit(solution)/shard_map/ppermute | solution.py:335
  20.7 1.8 %collective-permute-start.7 = (bf16[128,1024]{1,0:T(8,128)(2,1)S(1)}, bf16[128,1024]{1,0:T(8,128)(2,1)S(1)}, u32[]{:S(2)}, u32[]{:S(2)}) collective-permute-start(bf16[128,1024]{1,0:T(8,128)(2,1)S(1)} %collective-permute-done.far_a), channel_id=1, source_target_pairs={{0,2},{2,0},{4,6},{6,4},{8,10},{10,8},{12,14},{14,12},{16,18},{18,... | collective-permute-start | bytes 786440 | tf_op jit(solution)/shard_map/ppermute | solution.py:335
  20.8 2.1 %collective-permute-start.8 = (bf16[128,1024]{1,0:T(8,128)(2,1)S(1)}, bf16[128,1024]{1,0:T(8,128)(2,1)S(1)}, u32[]{:S(2)}, u32[]{:S(2)}) collective-permute-start(bf16[128,1024]{1,0:T(8,128)(2,1)S(1)} %collective-permute-done.1.far_b), channel_id=1, source_target_pairs={{0,2},{2,0},{4,6},{6,4},{8,10},{10,8},{12,14},{14,12},{16,18},{18,... | collective-permute-start | bytes 786440 | tf_op jit(solution)/shard_map/ppermute | solution.py:335
  24.4 1.4 %copy-start = (bf16[1,512,512]{2,1,0:T(8,128)(2,1)S(1)}, bf16[1,512,512]{2,1,0:T(8,128)(2,1)}, u32[]{:S(2)}) copy-start(bf16[1,512,512]{2,1,0:T(8,128)(2,1)} %param.9) | copy-start | bytes 1572868
  24.4 1.4 %copy-start.2 = (s32[1,1,256,1]{2,3,1,0:T(1,128)S(1)}, s32[1,1,256,1]{2,3,1,0:T(1,128)}, u32[]{:S(2)}) copy-start(s32[1,1,256,1]{2,3,1,0:T(1,128)} %param.10) | copy-start | bytes 3076
  24.4 1.4 %copy-start.3 = (s32[1,1,256]{2,1,0:T(1,128)S(1)}, s32[1,1,256]{2,1,0:T(1,128)}, u32[]{:S(2)}) copy-start(s32[1,1,256]{2,1,0:T(1,128)} %param.11) | copy-start | bytes 3076
  24.4 1.4 %copy-start.4 = (s32[128]{0:T(128)S(1)}, s32[128]{0:T(128)}, u32[]{:S(2)}) copy-start(s32[128]{0:T(128)} %param.12) | copy-start | bytes 1540
  24.4 14.2 %collective-permute-start.9 = (bf16[256,1024]{1,0:T(8,128)(2,1)S(1)}, bf16[256,1024]{1,0:T(8,128)(2,1)S(1)}, u32[]{:S(2)}, u32[]{:S(2)}) collective-permute-start(bf16[256,1024]{1,0:T(8,128)(2,1)S(1)} %get-tuple-element.54), channel_id=1, source_target_pairs={{0,1},{1,0},{2,3},{3,2},{4,5},{5,4},{6,7},{7,6},{8,9},{9,8},{10,11... | collective-permute-start | bytes 1572872 | tf_op jit(solution)/shard_map/ppermute | solution.py:411

commit v10 on v9

--- a/solution.py
+++ b/solution.py
@@ -384,8 +384,7 @@
         compiler_params=pltpu.CompilerParams(vmem_limit_bytes=44 * 2**20),
         cost_estimate=pl.CostEstimate(flops=flops(n), bytes_accessed=0, transcendentals=2**18),
     )(tile_curvature, own_block, twin, tables)
-    *others, total = lax.optimization_barrier((far[0], far[1], near[0], near[1], total))
-    far, near = [others[0], others[1]], [others[2], others[3]]
+    near[0], near[1], total = lax.optimization_barrier((near[0], near[1], total))
     twin_near = [swap(block, blk_count) for block in near]
     twin_far = [swap(block, blk_count) for block in far]
     n = GROUPS[1]

time: 88.4 us -> 87.9 us (level)
  waiting for transfers between devices: 18.9 us -> 19.9 us
  blocking collectives: 47.2 us -> 46.3 us
    ppermute x2, waiting for transfers between devices: 0.01 us -> 1.36 us  [body(): lax.ppermute(own_block, 'blk', matching(blk_count, 4, p))]
    ppermute x2, starting transfers between devices: 2.38 us -> 1.19 us  [body(): lax.ppermute(own_block, 'blk', matching(blk_count, 4, p))]
where the time goes in v10:
time: 87.9 us; the launch traced here: 87.8 us
  blocking collectives  46.3 us (53%)
  waiting for transfers between devices  19.9 us (23%)
  Pallas kernels  11.3 us (13%)
  starting transfers between devices  8.38 us (10%)
  local copies, waits for them, and re-layouts  0.97 us (1%)
    all_to_all x1, blocking collectives, body(): got = lax.all_to_all(packed, 'blk', split_axis=0, concat_axis=0, tiled=True)  46.3 us
    ppermute x1, waiting for transfers between devices, body(): arrived = lax.ppermute(sent, 'map', [(0, 1), (1, 0)])  11.8 us
    ppermute x2, waiting for transfers between devices, body(): lax.ppermute(own_block, 'blk', matching(blk_count, 2, p))  6.51 us
    pallas_call x6, Pallas kernels, call(): pl.pallas_call(kernel, out_shape=outs, in_specs=specs, out_specs=[pl.Bloc...  6.41 us
    ppermute x2, starting transfers between devices, body(): lax.ppermute(own_block, 'blk', matching(blk_count, 2, p))  5.53 us
    pallas_call x1, Pallas kernels, body(): pl.pallas_call(functools.partial(first_kernel, map_count, STOPS * map_cou...  4.9 us
  transfers between devices with their start and end apart: 10, of which 5 were waited for; matrix products, arithmetic and copies ran while one was open for 0% of the time, Pallas kernels for 8%

profile of v10, /device:TPU:32, one launch (start us, length us, event | category | flops | bytes accessed | tf_op | source)
XLA Modules:
  0.0 87.8 jit_solution(9335691304917174535)
XLA Ops:
  0.0 3.0 %collective-permute-start = (bf16[128,1024]{1,0:T(8,128)(2,1)}, bf16[128,1024]{1,0:T(8,128)(2,1)S(1)}, u32[]{:S(2)}, u32[]{:S(2)}) collective-permute-start(bf16[128,1024]{1,0:T(8,128)(2,1)} %bitcast.8), channel_id=1, source_target_pairs={{0,4},{4,0},{8,12},{12,8},{16,20},{20,16},{24,28},{28,24},{32,36},... | collective-permute-start | bytes 786440 | tf_op jit(solution)/shard_map/ppermute | solution.py:347
  3.0 2.5 %collective-permute-start.1 = (bf16[128,1024]{1,0:T(8,128)(2,1)}, bf16[128,1024]{1,0:T(8,128)(2,1)S(1)}, u32[]{:S(2)}, u32[]{:S(2)}) collective-permute-start(bf16[128,1024]{1,0:T(8,128)(2,1)} %bitcast.9), channel_id=1, source_target_pairs={{4,8},{8,4},{12,16},{16,12},{20,24},{24,20},{28,32},{32,28},{36,40... | collective-permute-start | bytes 786440 | tf_op jit(solution)/shard_map/ppermute | solution.py:347
  5.5 1.2 %collective-permute-start.7 = (bf16[128,1024]{1,0:T(8,128)(2,1)}, bf16[128,1024]{1,0:T(8,128)(2,1)S(1)}, u32[]{:S(2)}, u32[]{:S(2)}) collective-permute-start(bf16[128,1024]{1,0:T(8,128)(2,1)} %bitcast.11), channel_id=1, source_target_pairs={{8,16},{16,8},{24,32},{32,24},{40,48},{48,40},{56,64},{64,56},{72,... | collective-permute-start | bytes 786440 | tf_op jit(solution)/shard_map/ppermute | solution.py:348
  7.4 0.9 %copy-done.1 = bf16[1,1,128,1024]{3,2,1,0:T(8,128)(2,1)S(1)} copy-done((bf16[1,1,128,1024]{3,2,1,0:T(8,128)(2,1)S(1)}, bf16[1,1,128,1024]{3,2,1,0:T(8,128)(2,1)}, u32[]{:S(2)}) %copy-start.1) | copy-done | bytes 262168
  8.3 4.9 %shard_map.73 = (f32[512,1024]{1,0:T(8,128)S(1)}, f32[2,128,512]{2,1,0:T(8,128)S(1)}, f32[2,128,512]{2,1,0:T(8,128)S(1)}, f32[4,128,512]{2,1,0:T(8,128)S(1)}, f3...) custom-call(f32[1]{0:T(128)S(6)} %copy.8.curvature, ...), custom_call_target="tpu_custom_call" | custom-call | flops 1073741824 | tf_op jit(solution)/shard_map/pallas_call | solution.py:371
  13.2 4.4 %collective-permute-done.near_a = bf16[128,1024]{1,0:T(8,128)(2,1)S(1)} collective-permute-done((bf16[128,1024]{1,0:T(8,128)(2,1)}, bf16[128,1024]{1,0:T(8,128)(2,1)S(1)}, u32[]{:S(2)}, u32[]{:S(2)}) %collective-permute-start) | collective-permute-done | bytes 262176 | tf_op jit(solution)/shard_map/ppermute | solution.py:347
  17.6 2.1 %collective-permute-done.1.near_b = bf16[128,1024]{1,0:T(8,128)(2,1)S(1)} collective-permute-done((bf16[128,1024]{1,0:T(8,128)(2,1)}, bf16[128,1024]{1,0:T(8,128)(2,1)S(1)}, u32[]{:S(2)}, u32[]{:S(2)}) %collective-permute-start.1) | collective-permute-done | bytes 262176 | tf_op jit(solution)/shard_map/ppermute | solution.py:347
  19.8 0.5 collective-permute-start.4
  20.3 0.0 collective-permute-start.6
  20.3 1.4 %collective-permute-done.7.far_b = bf16[128,1024]{1,0:T(8,128)(2,1)S(1)} collective-permute-done((bf16[128,1024]{1,0:T(8,128)(2,1)}, bf16[128,1024]{1,0:T(8,128)(2,1)S(1)}, u32[]{:S(2)}, u32[]{:S(2)}) %collective-permute-start.7) | collective-permute-done | bytes 262176 | tf_op jit(solution)/shard_map/ppermute | solution.py:348
  21.6 1.2 %shard_map.74.before = f32[512,1024]{1,0:T(8,128)S(1)} custom-call(bf16[128,1024]{1,0:T(8,128)(2,1)S(1)} %collective-permute-done.near_a, bf16[128,1024]{1,0:T(8,128)(2,1)S(1)} %collective-permute-done.1.near_b, f32[2,128,512]{2,1,0:T(8,128)S(1)} %get-tuple-element.34.cosines, f32[2,128,512]{2,1,0:T(8,128)S(1)} %get-tuple-element.35.sines, ...), custom_call_target="tpu_custom_call" | custom-call | flops 1073741824 | bytes 7340032 | tf_op jit(solution)/shard_map/pallas_call | solution.py:79
  22.8 0.3 collective-permute-done.8.twin_far_b
  23.2 1.5 %shard_map.75 = (bf16[256,1024]{1,0:T(8,128)(2,1)S(1)}, bf16[1024,1024]{1,0:T(8,128)(2,1)S(1)}) custom-call(bf16[128,1024]{1,0:T(8,128)(2,1)S(1)} %collective-permute-done.3.twin_near_a, bf16[128,1024]{1,0:T(8,128)(2,1)S(1)} %collective-permute-done.4.twin_near_b, bf16[128,1024]{1,0:T(8,128)(2,1)S(1)} %collective-permute-done.5.far_a, ...), custom_call_target="tpu_custom_call" | custom-call | flops 2147483648 | bytes 10485760 | tf_op jit(solution)/shard_map/pallas_call | solution.py:79
  24.7 0.0 copy-start
  24.7 0.0 copy-start.2
  24.7 0.0 copy-start.3
  24.7 0.0 copy-start.4
  24.7 1.1 %collective-permute-start.9 = (bf16[256,1024]{1,0:T(8,128)(2,1)S(1)}, bf16[256,1024]{1,0:T(8,128)(2,1)S(1)}, u32[]{:S(2)}, u32[]{:S(2)}) collective-permute-start(bf16[256,1024]{1,0:T(8,128)(2,1)S(1)} %get-tuple-element.50), channel_id=1, source_target_pairs={{0,1},{1,0},{2,3},{3,2},{4,5},{5,4},{6,7},{7,6},{8,9},{9,8},{10,11... | collective-permute-start | bytes 1572872 | tf_op jit(solution)/shard_map/ppermute | solution.py:410
  25.9 0.7 shard_map.76.kept
  26.6 0.7 shard_map.77
  27.3 11.8 %collective-permute-done.9.arrived = bf16[256,1024]{1,0:T(8,128)(2,1)S(1)} collective-permute-done((bf16[256,1024]{1,0:T(8,128)(2,1)S(1)}, bf16[256,1024]{1,0:T(8,128)(2,1)S(1)}, u32[]{:S(2)}, u32[]{:S(2)}) %collective-permute-start.9) | collective-permute-done | bytes 524320 | tf_op jit(solution)/shard_map/ppermute | solution.py:410
  39.0 0.5 shard_map.78
  39.5 46.3 %all_to_all.5.got = bf16[128,2,2176]{2,1,0:T(2,128)(2,1)S(1)} all-to-all(bf16[128,2,2176]{2,1,0:T(2,128)(2,1)S(1)} %shard_map.78), channel_id=1, replica_groups=mesh['blk'=128,'map'=2] {'blk'}, dimensions={0} | all-to-all | bytes 2228224 | tf_op jit(solution)/shard_map/all_to_all | solution.py:432
  85.9 1.9 %shard_map.79 = f32[256,512]{1,0:T(8,128)} custom-call(bf16[128,2,2176]{2,1,0:T(2,128)(2,1)S(1)} %all_to_all.5.got, bf16[512,512]{1,0:T(8,128)(2,1)S(1)} %get-tuple-element.56.weights), custom_call_target="tpu_custom_call" | custom-call | flops 805306368 | bytes 2162688 | tf_op jit(solution)/shard_map/pallas_call | solution.py:79
  (14 shorter events, 0.0 us)
Async XLA Ops:
  0.0 7.4 %collective-permute-start.2 = (bf16[128,1024]{1,0:T(8,128)(2,1)}, bf16[128,1024]{1,0:T(8,128)(2,1)S(1)}, u32[]{:S(2)}, u32[]{:S(2)}) collective-permute-start(bf16[128,1024]{1,0:T(8,128)(2,1)} %bitcast.7), channel_id=1, source_target_pairs={{0,2},{2,0},{4,6},{6,4},{8,10},{10,8},{12,14},{14,12},{16,18},{18,... | collective-permute-start | bytes 786440 | tf_op jit(solution)/shard_map/ppermute | solution.py:335
  0.0 17.6 %collective-permute-start = (bf16[128,1024]{1,0:T(8,128)(2,1)}, bf16[128,1024]{1,0:T(8,128)(2,1)S(1)}, u32[]{:S(2)}, u32[]{:S(2)}) collective-permute-start(bf16[128,1024]{1,0:T(8,128)(2,1)} %bitcast.8), channel_id=1, source_target_pairs={{0,4},{4,0},{8,12},{12,8},{16,20},{20,16},{24,28},{28,24},{32,36},... | collective-permute-start | bytes 786440 | tf_op jit(solution)/shard_map/ppermute | solution.py:347
  3.0 16.7 %collective-permute-start.1 = (bf16[128,1024]{1,0:T(8,128)(2,1)}, bf16[128,1024]{1,0:T(8,128)(2,1)S(1)}, u32[]{:S(2)}, u32[]{:S(2)}) collective-permute-start(bf16[128,1024]{1,0:T(8,128)(2,1)} %bitcast.9), channel_id=1, source_target_pairs={{4,8},{8,4},{12,16},{16,12},{20,24},{24,20},{28,32},{32,28},{36,40... | collective-permute-start | bytes 786440 | tf_op jit(solution)/shard_map/ppermute | solution.py:347
  5.5 14.7 %collective-permute-start.5 = (bf16[128,1024]{1,0:T(8,128)(2,1)}, bf16[128,1024]{1,0:T(8,128)(2,1)S(1)}, u32[]{:S(2)}, u32[]{:S(2)}) collective-permute-start(bf16[128,1024]{1,0:T(8,128)(2,1)} %bitcast.10), channel_id=1, source_target_pairs={{0,8},{8,0},{16,24},{24,16},{32,40},{40,32},{48,56},{56,48},{64,72... | collective-permute-start | bytes 786440 | tf_op jit(solution)/shard_map/ppermute | solution.py:348
  5.5 16.1 %collective-permute-start.7 = (bf16[128,1024]{1,0:T(8,128)(2,1)}, bf16[128,1024]{1,0:T(8,128)(2,1)S(1)}, u32[]{:S(2)}, u32[]{:S(2)}) collective-permute-start(bf16[128,1024]{1,0:T(8,128)(2,1)} %bitcast.11), channel_id=1, source_target_pairs={{8,16},{16,8},{24,32},{32,24},{40,48},{48,40},{56,64},{64,56},{72,... | collective-permute-start | bytes 786440 | tf_op jit(solution)/shard_map/ppermute | solution.py:348
  7.4 1.0 %copy-start.1 = (bf16[1,1,128,1024]{3,2,1,0:T(8,128)(2,1)S(1)}, bf16[1,1,128,1024]{3,2,1,0:T(8,128)(2,1)}, u32[]{:S(2)}) copy-start(bf16[1,1,128,1024]{3,2,1,0:T(8,128)(2,1)} %param.7) | copy-start | bytes 786436
  19.8 3.1 %collective-permute-start.3 = (bf16[128,1024]{1,0:T(8,128)(2,1)S(1)}, bf16[128,1024]{1,0:T(8,128)(2,1)S(1)}, u32[]{:S(2)}, u32[]{:S(2)}) collective-permute-start(bf16[128,1024]{1,0:T(8,128)(2,1)S(1)} %collective-permute-done.near_a), channel_id=1, source_target_pairs={{0,2},{2,0},{4,6},{6,4},{8,10},{10,8},{12,14},{14,12},{16,18},{18,... | collective-permute-start | bytes 786440 | tf_op jit(solution)/shard_map/ppermute | solution.py:335
  19.8 3.1 %collective-permute-start.4 = (bf16[128,1024]{1,0:T(8,128)(2,1)S(1)}, bf16[128,1024]{1,0:T(8,128)(2,1)S(1)}, u32[]{:S(2)}, u32[]{:S(2)}) collective-permute-start(bf16[128,1024]{1,0:T(8,128)(2,1)S(1)} %collective-permute-done.1.near_b), channel_id=1, source_target_pairs={{0,2},{2,0},{4,6},{6,4},{8,10},{10,8},{12,14},{14,12},{16,18},{18,... | collective-permute-start | bytes 786440 | tf_op jit(solution)/shard_map/ppermute | solution.py:335
  20.3 2.6 %collective-permute-start.6 = (bf16[128,1024]{1,0:T(8,128)(2,1)S(1)}, bf16[128,1024]{1,0:T(8,128)(2,1)S(1)}, u32[]{:S(2)}, u32[]{:S(2)}) collective-permute-start(bf16[128,1024]{1,0:T(8,128)(2,1)S(1)} %collective-permute-done.5.far_a), channel_id=1, source_target_pairs={{0,2},{2,0},{4,6},{6,4},{8,10},{10,8},{12,14},{14,12},{16,18},{18,... | collective-permute-start | bytes 786440 | tf_op jit(solution)/shard_map/ppermute | solution.py:335
  21.6 1.5 %collective-permute-start.8 = (bf16[128,1024]{1,0:T(8,128)(2,1)S(1)}, bf16[128,1024]{1,0:T(8,128)(2,1)S(1)}, u32[]{:S(2)}, u32[]{:S(2)}) collective-permute-start(bf16[128,1024]{1,0:T(8,128)(2,1)S(1)} %collective-permute-done.7.far_b), channel_id=1, source_target_pairs={{0,2},{2,0},{4,6},{6,4},{8,10},{10,8},{12,14},{14,12},{16,18},{18,... | collective-permute-start | bytes 786440 | tf_op jit(solution)/shard_map/ppermute | solution.py:335
  24.7 1.9 %copy-start = (bf16[1,512,512]{2,1,0:T(8,128)(2,1)S(1)}, bf16[1,512,512]{2,1,0:T(8,128)(2,1)}, u32[]{:S(2)}) copy-start(bf16[1,512,512]{2,1,0:T(8,128)(2,1)} %param.9) | copy-start | bytes 1572868
  24.7 1.9 %copy-start.2 = (s32[1,1,256,1]{2,3,1,0:T(1,128)S(1)}, s32[1,1,256,1]{2,3,1,0:T(1,128)}, u32[]{:S(2)}) copy-start(s32[1,1,256,1]{2,3,1,0:T(1,128)} %param.10) | copy-start | bytes 3076
  24.7 1.9 %copy-start.3 = (s32[1,1,256]{2,1,0:T(1,128)S(1)}, s32[1,1,256]{2,1,0:T(1,128)}, u32[]{:S(2)}) copy-start(s32[1,1,256]{2,1,0:T(1,128)} %param.11) | copy-start | bytes 3076
  24.7 1.9 %copy-start.4 = (s32[128]{0:T(128)S(1)}, s32[128]{0:T(128)}, u32[]{:S(2)}) copy-start(s32[128]{0:T(128)} %param.12) | copy-start | bytes 1540
  24.7 14.3 %collective-permute-start.9 = (bf16[256,1024]{1,0:T(8,128)(2,1)S(1)}, bf16[256,1024]{1,0:T(8,128)(2,1)S(1)}, u32[]{:S(2)}, u32[]{:S(2)}) collective-permute-start(bf16[256,1024]{1,0:T(8,128)(2,1)S(1)} %get-tuple-element.50), channel_id=1, source_target_pairs={{0,1},{1,0},{2,3},{3,2},{4,5},{5,4},{6,7},{7,6},{8,9},{9,8},{10,11... | collective-permute-start | bytes 1572872 | tf_op jit(solution)/shard_map/ppermute | solution.py:410

commit v11 on v10

--- a/solution.py
+++ b/solution.py
@@ -13,7 +13,7 @@
 STOPS = 8
 MAPH = 256
 SIDE = 128
-GROUPS = (2, 2, 4)
+GROUPS = (2, 3, 3)
 
 
 def matching(count, distance, parity):
@@ -45,7 +45,7 @@
 
 
 def stop_order(core):
-    return [3, 4 - 2 * core, 1, 5, 2 - 2 * core, 6 - 2 * core, 6 * core, 7]
+    return [3, 4 - 2 * core, 1, 5, 7, 2 - 2 * core, 6 - 2 * core, 6 * core]
 
 
 def cross_tables(map_count, row_count, pulse_count):
@@ -178,13 +178,15 @@
     depth, side = ranges.shape
     rows = cross.shape[0]
     left, right = slice(0, side), slice(side, 2 * side)
+    rest_side = side // 2
     moves = [
         (own_far, own),
         (tables.at[index, :depth, left], ranges),
         (tables.at[index, depth : depth + rows, left], cross),
-        (tables.at[index, depth : depth + rows, right], second),
+        (tables.at[index, depth : depth + rows, right], second.at[:, left]),
         (tables.at[index, :rows, right], last.at[:, left]),
-        (tables.at[index, rows : 2 * rows, right], last.at[:, right]),
+        (tables.at[index, rows : 2 * rows, side : side + rest_side], second.at[:, side:]),
+        (tables.at[index, rows : 2 * rows, side + rest_side :], last.at[:, side:]),
     ]
     copies = [
         pltpu.make_async_copy(source, target, arrivals.at[n])
@@ -202,12 +204,14 @@
 
 
 def second_kernel(
-    near_a, near_b, cosines, sines, ranges, cross, before, total, phased, right_side
+    near_a, near_b, far_a, far_b, cosines, sines, ranges, cross, before, total, phased, right_side
 ):
-    chip_odd = whereabouts()[1] == 1
+    _, chip, group, _, _ = whereabouts()
+    chip_odd, group_odd = chip == 1, group == 1
     blocks = [
         lambda: jnp.where(chip_odd, near_a[...], near_b[...]),
         lambda: jnp.where(chip_odd, near_b[...], near_a[...]),
+        lambda: jnp.where(group_odd, far_b[...], far_a[...]),
     ]
     transform(blocks, cosines, sines, ranges, phased, right_side)
     total[...] = before[...] + jnp.dot(
@@ -221,16 +225,15 @@
 
 
 def last_kernel(
-    twin_near_a, twin_near_b, far_a, far_b, twin_far_a, twin_far_b,
+    twin_near_a, twin_near_b, twin_far_a, twin_far_b,
     cosines, sines, ranges, cross, before, sent, right_side, phased,
 ):
     core, chip, group, here_map, _ = whereabouts()
-    chip_odd, group_odd, from_a = chip == 1, group == 1, core != group
+    chip_odd, from_a = chip == 1, core != group
     blocks = [
         lambda: jnp.where(chip_odd, twin_near_a[...], twin_near_b[...]),
         lambda: jnp.where(chip_odd, twin_near_b[...], twin_near_a[...]),
         lambda: jnp.where(from_a, twin_far_a[...], twin_far_b[...]),
-        lambda: jnp.where(group_odd, far_b[...], far_a[...]),
     ]
     transform(blocks, cosines, sines, ranges, phased, right_side)
     other = 1 - here_map
@@ -379,7 +382,7 @@
             right(n),
             pltpu.VMEM(cross(n), jnp.bfloat16),
             pltpu.VMEM(own_block.shape, jnp.bfloat16),
-            pltpu.SemaphoreType.DMA((6,)),
+            pltpu.SemaphoreType.DMA((7,)),
         ],
         compiler_params=pltpu.CompilerParams(vmem_limit_bytes=44 * 2**20),
         cost_estimate=pl.CostEstimate(flops=flops(n), bytes_accessed=0, transcendentals=2**18),
@@ -391,7 +394,7 @@
     [total] = call(
         second_kernel,
         [f32(*image_shape)],
-        [*near, *curves[:2], ranges, second_cross, total],
+        [*near, *far, *curves[:2], ranges, second_cross, total],
         [spread(n), right(n)],
         flops(n),
     )
@@ -400,7 +403,7 @@
     sent, right_side = call(
         last_kernel,
         [b16(*half_shape), b16(n * deep, 2 * columns)],
-        [*twin_near, *far, *twin_far, *curves[2:], ranges, last_cross, total],
+        [*twin_near, *twin_far, *curves[2:], ranges, last_cross, total],
         [spread(n)],
         flops(n),
     )
@@ -459,9 +462,11 @@
         tables = np.zeros((len(first), width + rows, width), first.dtype)
         tables[:, :width, :side] = range_tables(side)
         tables[:, width:, :side] = first
-        tables[:, width:, side:] = second
+        tables[:, width:, side:] = second[:, :, :side]
         tables[:, :rows, side:] = last[:, :, :side]
-        tables[:, rows : 2 * rows, side:] = last[:, :, side:]
+        tables[:, rows : 2 * rows, side:] = np.concatenate(
+            [second[:, :, side:], last[:, :, side:]], axis=2
+        )
         tables = jnp.asarray(tables)
         held = lambda *here: body(tables, *here)
         return jax.shard_map(

time: 87.9 us -> 88 us (level)
  transfers between devices with their start and end apart: 10 -> 10, of which waited for: 5 -> 4; matrix products, arithmetic and copies ran while one was open for 0% -> 0% of each run, Pallas kernels for 8% -> 9%
where the time goes in v11:
time: 88 us; the launch traced here: 87.9 us
  blocking collectives  46.4 us (53%)
  waiting for transfers between devices  20.1 us (23%)
  Pallas kernels  11.3 us (13%)
  starting transfers between devices  8.38 us (10%)
  local copies, waits for them, and re-layouts  0.97 us (1%)
    all_to_all x1, blocking collectives, body(): got = lax.all_to_all(packed, 'blk', split_axis=0, concat_axis=0, tiled=True)  46.4 us
    ppermute x1, waiting for transfers between devices, body(): arrived = lax.ppermute(sent, 'map', [(0, 1), (1, 0)])  12.2 us
    ppermute x2, waiting for transfers between devices, body(): lax.ppermute(own_block, 'blk', matching(blk_count, 2, p))  6.52 us
    pallas_call x6, Pallas kernels, call(): pl.pallas_call(kernel, out_shape=outs, in_specs=specs, out_specs=[pl.Bloc...  6.39 us
    ppermute x2, starting transfers between devices, body(): lax.ppermute(own_block, 'blk', matching(blk_count, 2, p))  5.53 us
    pallas_call x1, Pallas kernels, body(): pl.pallas_call(functools.partial(first_kernel, map_count, STOPS * map_cou...  4.89 us
  transfers between devices with their start and end apart: 10, of which 4 were waited for; matrix products, arithmetic and copies ran while one was open for 0% of the time, Pallas kernels for 9%

profile of v11, /device:TPU:32, one launch (start us, length us, event | category | flops | bytes accessed | tf_op | source)
XLA Modules:
  0.0 87.9 jit_solution(3400520140634541826)
XLA Ops:
  0.0 0.0 collective-permute-start.2
  0.0 3.0 %collective-permute-start = (bf16[128,1024]{1,0:T(8,128)(2,1)}, bf16[128,1024]{1,0:T(8,128)(2,1)S(1)}, u32[]{:S(2)}, u32[]{:S(2)}) collective-permute-start(bf16[128,1024]{1,0:T(8,128)(2,1)} %bitcast.8), channel_id=1, source_target_pairs={{0,4},{4,0},{8,12},{12,8},{16,20},{20,16},{24,28},{28,24},{32,36},... | collective-permute-start | bytes 786440 | tf_op jit(solution)/shard_map/ppermute | solution.py:350
  3.0 2.5 %collective-permute-start.1 = (bf16[128,1024]{1,0:T(8,128)(2,1)}, bf16[128,1024]{1,0:T(8,128)(2,1)S(1)}, u32[]{:S(2)}, u32[]{:S(2)}) collective-permute-start(bf16[128,1024]{1,0:T(8,128)(2,1)} %bitcast.9), channel_id=1, source_target_pairs={{4,8},{8,4},{12,16},{16,12},{20,24},{24,20},{28,32},{32,28},{36,40... | collective-permute-start | bytes 786440 | tf_op jit(solution)/shard_map/ppermute | solution.py:350
  5.5 1.2 %collective-permute-start.7 = (bf16[128,1024]{1,0:T(8,128)(2,1)}, bf16[128,1024]{1,0:T(8,128)(2,1)S(1)}, u32[]{:S(2)}, u32[]{:S(2)}) collective-permute-start(bf16[128,1024]{1,0:T(8,128)(2,1)} %bitcast.11), channel_id=1, source_target_pairs={{8,16},{16,8},{24,32},{32,24},{40,48},{48,40},{56,64},{64,56},{72,... | collective-permute-start | bytes 786440 | tf_op jit(solution)/shard_map/ppermute | solution.py:351
  7.4 0.9 %copy-done.1 = bf16[1,1,128,1024]{3,2,1,0:T(8,128)(2,1)S(1)} copy-done((bf16[1,1,128,1024]{3,2,1,0:T(8,128)(2,1)S(1)}, bf16[1,1,128,1024]{3,2,1,0:T(8,128)(2,1)}, u32[]{:S(2)}) %copy-start.1) | copy-done | bytes 262168
  8.3 4.9 %shard_map.73 = (f32[512,1024]{1,0:T(8,128)S(1)}, f32[3,128,512]{2,1,0:T(8,128)S(1)}, f32[3,128,512]{2,1,0:T(8,128)S(1)}, f32[3,128,512]{2,1,0:T(8,128)S(1)}, f3...) custom-call(f32[1]{0:T(128)S(6)} %copy.8.curvature, ...), custom_call_target="tpu_custom_call" | custom-call | flops 1073741824 | tf_op jit(solution)/shard_map/pallas_call | solution.py:374
  13.2 4.4 %collective-permute-done.near_a = bf16[128,1024]{1,0:T(8,128)(2,1)S(1)} collective-permute-done((bf16[128,1024]{1,0:T(8,128)(2,1)}, bf16[128,1024]{1,0:T(8,128)(2,1)S(1)}, u32[]{:S(2)}, u32[]{:S(2)}) %collective-permute-start) | collective-permute-done | bytes 262176 | tf_op jit(solution)/shard_map/ppermute | solution.py:350
  17.6 2.1 %collective-permute-done.1.near_b = bf16[128,1024]{1,0:T(8,128)(2,1)S(1)} collective-permute-done((bf16[128,1024]{1,0:T(8,128)(2,1)}, bf16[128,1024]{1,0:T(8,128)(2,1)S(1)}, u32[]{:S(2)}, u32[]{:S(2)}) %collective-permute-start.1) | collective-permute-done | bytes 262176 | tf_op jit(solution)/shard_map/ppermute | solution.py:350
  19.8 0.5 collective-permute-start.4
  20.3 0.0 collective-permute-start.6
  20.3 1.4 %collective-permute-done.7.far_b = bf16[128,1024]{1,0:T(8,128)(2,1)S(1)} collective-permute-done((bf16[128,1024]{1,0:T(8,128)(2,1)}, bf16[128,1024]{1,0:T(8,128)(2,1)S(1)}, u32[]{:S(2)}, u32[]{:S(2)}) %collective-permute-start.7) | collective-permute-done | bytes 262176 | tf_op jit(solution)/shard_map/ppermute | solution.py:351
  21.6 1.6 %shard_map.74.before = f32[512,1024]{1,0:T(8,128)S(1)} custom-call(bf16[128,1024]{1,0:T(8,128)(2,1)S(1)} %collective-permute-done.near_a, bf16[128,1024]{1,0:T(8,128)(2,1)S(1)} %collective-permute-done.1.near_b, bf16[128,1024]{1,0:T(8,128)(2,1)S(1)} %collective-permute-done.5.far_a, bf16[128,1024]{1,0:T(8,128)(2,1)S(1)} %collective-permute-done.7.far_b, ...), custom_call_target="tpu_custom_call" | custom-call | flops 1610612736 | bytes 8650752 | tf_op jit(solution)/shard_map/pallas_call | solution.py:79
  23.3 1.2 %shard_map.75 = (bf16[256,1024]{1,0:T(8,128)(2,1)S(1)}, bf16[768,1024]{1,0:T(8,128)(2,1)S(1)}) custom-call(bf16[128,1024]{1,0:T(8,128)(2,1)S(1)} %collective-permute-done.3.twin_near_a, bf16[128,1024]{1,0:T(8,128)(2,1)S(1)} %collective-permute-done.4.twin_near_b, bf16[128,1024]{1,0:T(8,128)(2,1)S(1)} %collective-permute-done.6.twin_far_a, ...), custom_call_target="tpu_custom_call" | custom-call | flops 1610612736 | bytes 8650752 | tf_op jit(solution)/shard_map/pallas_call | solution.py:79
  24.5 0.0 copy-start
  24.5 0.0 copy-start.2
  24.5 0.0 copy-start.3
  24.5 0.0 copy-start.4
  24.5 1.1 %collective-permute-start.9 = (bf16[256,1024]{1,0:T(8,128)(2,1)S(1)}, bf16[256,1024]{1,0:T(8,128)(2,1)S(1)}, u32[]{:S(2)}, u32[]{:S(2)}) collective-permute-start(bf16[256,1024]{1,0:T(8,128)(2,1)S(1)} %get-tuple-element.50), channel_id=1, source_target_pairs={{0,1},{1,0},{2,3},{3,2},{4,5},{5,4},{6,7},{7,6},{8,9},{9,8},{10,11... | collective-permute-start | bytes 1572872 | tf_op jit(solution)/shard_map/ppermute | solution.py:413
  25.7 0.6 shard_map.76.kept
  26.3 0.7 shard_map.77
  26.9 12.2 %collective-permute-done.9.arrived = bf16[256,1024]{1,0:T(8,128)(2,1)S(1)} collective-permute-done((bf16[256,1024]{1,0:T(8,128)(2,1)S(1)}, bf16[256,1024]{1,0:T(8,128)(2,1)S(1)}, u32[]{:S(2)}, u32[]{:S(2)}) %collective-permute-start.9) | collective-permute-done | bytes 524320 | tf_op jit(solution)/shard_map/ppermute | solution.py:413
  39.1 0.5 shard_map.78
  39.6 46.4 %all_to_all.5.got = bf16[128,2,2176]{2,1,0:T(2,128)(2,1)S(1)} all-to-all(bf16[128,2,2176]{2,1,0:T(2,128)(2,1)S(1)} %shard_map.78), channel_id=1, replica_groups=mesh['blk'=128,'map'=2] {'blk'}, dimensions={0} | all-to-all | bytes 2228224 | tf_op jit(solution)/shard_map/all_to_all | solution.py:435
  86.0 1.9 %shard_map.79 = f32[256,512]{1,0:T(8,128)} custom-call(bf16[128,2,2176]{2,1,0:T(2,128)(2,1)S(1)} %all_to_all.5.got, bf16[512,512]{1,0:T(8,128)(2,1)S(1)} %get-tuple-element.56.weights), custom_call_target="tpu_custom_call" | custom-call | flops 805306368 | bytes 2162688 | tf_op jit(solution)/shard_map/pallas_call | solution.py:79
  (14 shorter events, 0.0 us)
Async XLA Ops:
  0.0 7.4 %collective-permute-start.2 = (bf16[128,1024]{1,0:T(8,128)(2,1)}, bf16[128,1024]{1,0:T(8,128)(2,1)S(1)}, u32[]{:S(2)}, u32[]{:S(2)}) collective-permute-start(bf16[128,1024]{1,0:T(8,128)(2,1)} %bitcast.7), channel_id=1, source_target_pairs={{0,2},{2,0},{4,6},{6,4},{8,10},{10,8},{12,14},{14,12},{16,18},{18,... | collective-permute-start | bytes 786440 | tf_op jit(solution)/shard_map/ppermute | solution.py:338
  0.0 17.6 %collective-permute-start = (bf16[128,1024]{1,0:T(8,128)(2,1)}, bf16[128,1024]{1,0:T(8,128)(2,1)S(1)}, u32[]{:S(2)}, u32[]{:S(2)}) collective-permute-start(bf16[128,1024]{1,0:T(8,128)(2,1)} %bitcast.8), channel_id=1, source_target_pairs={{0,4},{4,0},{8,12},{12,8},{16,20},{20,16},{24,28},{28,24},{32,36},... | collective-permute-start | bytes 786440 | tf_op jit(solution)/shard_map/ppermute | solution.py:350
  3.0 16.7 %collective-permute-start.1 = (bf16[128,1024]{1,0:T(8,128)(2,1)}, bf16[128,1024]{1,0:T(8,128)(2,1)S(1)}, u32[]{:S(2)}, u32[]{:S(2)}) collective-permute-start(bf16[128,1024]{1,0:T(8,128)(2,1)} %bitcast.9), channel_id=1, source_target_pairs={{4,8},{8,4},{12,16},{16,12},{20,24},{24,20},{28,32},{32,28},{36,40... | collective-permute-start | bytes 786440 | tf_op jit(solution)/shard_map/ppermute | solution.py:350
  5.5 14.7 %collective-permute-start.5 = (bf16[128,1024]{1,0:T(8,128)(2,1)}, bf16[128,1024]{1,0:T(8,128)(2,1)S(1)}, u32[]{:S(2)}, u32[]{:S(2)}) collective-permute-start(bf16[128,1024]{1,0:T(8,128)(2,1)} %bitcast.10), channel_id=1, source_target_pairs={{0,8},{8,0},{16,24},{24,16},{32,40},{40,32},{48,56},{56,48},{64,72... | collective-permute-start | bytes 786440 | tf_op jit(solution)/shard_map/ppermute | solution.py:351
  5.5 16.1 %collective-permute-start.7 = (bf16[128,1024]{1,0:T(8,128)(2,1)}, bf16[128,1024]{1,0:T(8,128)(2,1)S(1)}, u32[]{:S(2)}, u32[]{:S(2)}) collective-permute-start(bf16[128,1024]{1,0:T(8,128)(2,1)} %bitcast.11), channel_id=1, source_target_pairs={{8,16},{16,8},{24,32},{32,24},{40,48},{48,40},{56,64},{64,56},{72,... | collective-permute-start | bytes 786440 | tf_op jit(solution)/shard_map/ppermute | solution.py:351
  7.4 1.0 %copy-start.1 = (bf16[1,1,128,1024]{3,2,1,0:T(8,128)(2,1)S(1)}, bf16[1,1,128,1024]{3,2,1,0:T(8,128)(2,1)}, u32[]{:S(2)}) copy-start(bf16[1,1,128,1024]{3,2,1,0:T(8,128)(2,1)} %param.7) | copy-start | bytes 786436
  19.8 3.5 %collective-permute-start.3 = (bf16[128,1024]{1,0:T(8,128)(2,1)S(1)}, bf16[128,1024]{1,0:T(8,128)(2,1)S(1)}, u32[]{:S(2)}, u32[]{:S(2)}) collective-permute-start(bf16[128,1024]{1,0:T(8,128)(2,1)S(1)} %collective-permute-done.near_a), channel_id=1, source_target_pairs={{0,2},{2,0},{4,6},{6,4},{8,10},{10,8},{12,14},{14,12},{16,18},{18,... | collective-permute-start | bytes 786440 | tf_op jit(solution)/shard_map/ppermute | solution.py:338
  19.8 3.5 %collective-permute-start.4 = (bf16[128,1024]{1,0:T(8,128)(2,1)S(1)}, bf16[128,1024]{1,0:T(8,128)(2,1)S(1)}, u32[]{:S(2)}, u32[]{:S(2)}) collective-permute-start(bf16[128,1024]{1,0:T(8,128)(2,1)S(1)} %collective-permute-done.1.near_b), channel_id=1, source_target_pairs={{0,2},{2,0},{4,6},{6,4},{8,10},{10,8},{12,14},{14,12},{16,18},{18,... | collective-permute-start | bytes 786440 | tf_op jit(solution)/shard_map/ppermute | solution.py:338
  20.3 3.0 %collective-permute-start.6 = (bf16[128,1024]{1,0:T(8,128)(2,1)S(1)}, bf16[128,1024]{1,0:T(8,128)(2,1)S(1)}, u32[]{:S(2)}, u32[]{:S(2)}) collective-permute-start(bf16[128,1024]{1,0:T(8,128)(2,1)S(1)} %collective-permute-done.5.far_a), channel_id=1, source_target_pairs={{0,2},{2,0},{4,6},{6,4},{8,10},{10,8},{12,14},{14,12},{16,18},{18,... | collective-permute-start | bytes 786440 | tf_op jit(solution)/shard_map/ppermute | solution.py:338
  21.6 1.6 %collective-permute-start.8 = (bf16[128,1024]{1,0:T(8,128)(2,1)S(1)}, bf16[128,1024]{1,0:T(8,128)(2,1)S(1)}, u32[]{:S(2)}, u32[]{:S(2)}) collective-permute-start(bf16[128,1024]{1,0:T(8,128)(2,1)S(1)} %collective-permute-done.7.far_b), channel_id=1, source_target_pairs={{0,2},{2,0},{4,6},{6,4},{8,10},{10,8},{12,14},{14,12},{16,18},{18,... | collective-permute-start | bytes 786440 | tf_op jit(solution)/shard_map/ppermute | solution.py:338
  24.5 1.8 %copy-start = (bf16[1,512,512]{2,1,0:T(8,128)(2,1)S(1)}, bf16[1,512,512]{2,1,0:T(8,128)(2,1)}, u32[]{:S(2)}) copy-start(bf16[1,512,512]{2,1,0:T(8,128)(2,1)} %param.9) | copy-start | bytes 1572868
  24.5 1.8 %copy-start.2 = (s32[1,1,256,1]{2,3,1,0:T(1,128)S(1)}, s32[1,1,256,1]{2,3,1,0:T(1,128)}, u32[]{:S(2)}) copy-start(s32[1,1,256,1]{2,3,1,0:T(1,128)} %param.10) | copy-start | bytes 3076
  24.5 1.8 %copy-start.3 = (s32[1,1,256]{2,1,0:T(1,128)S(1)}, s32[1,1,256]{2,1,0:T(1,128)}, u32[]{:S(2)}) copy-start(s32[1,1,256]{2,1,0:T(1,128)} %param.11) | copy-start | bytes 3076
  24.5 1.8 %copy-start.4 = (s32[128]{0:T(128)S(1)}, s32[128]{0:T(128)}, u32[]{:S(2)}) copy-start(s32[128]{0:T(128)} %param.12) | copy-start | bytes 1540
  24.5 14.6 %collective-permute-start.9 = (bf16[256,1024]{1,0:T(8,128)(2,1)S(1)}, bf16[256,1024]{1,0:T(8,128)(2,1)S(1)}, u32[]{:S(2)}, u32[]{:S(2)}) collective-permute-start(bf16[256,1024]{1,0:T(8,128)(2,1)S(1)} %get-tuple-element.50), channel_id=1, source_target_pairs={{0,1},{1,0},{2,3},{3,2},{4,5},{5,4},{6,7},{7,6},{8,9},{9,8},{10,11... | collective-permute-start | bytes 1572872 | tf_op jit(solution)/shard_map/ppermute | solution.py:413

commit v12 on v11

--- a/solution.py
+++ b/solution.py
@@ -387,7 +387,7 @@
         compiler_params=pltpu.CompilerParams(vmem_limit_bytes=44 * 2**20),
         cost_estimate=pl.CostEstimate(flops=flops(n), bytes_accessed=0, transcendentals=2**18),
     )(tile_curvature, own_block, twin, tables)
-    near[0], near[1], total = lax.optimization_barrier((near[0], near[1], total))
+    near[1], near[0], total = lax.optimization_barrier((near[1], near[0], total))
     twin_near = [swap(block, blk_count) for block in near]
     twin_far = [swap(block, blk_count) for block in far]
     n = GROUPS[1]

time: 88 us -> 87.9 us (level)
  waiting for transfers between devices: 20.1 us -> 18.6 us
    ppermute x2, waiting for transfers between devices: 1.36 us -> 0.01 us  [body(): lax.ppermute(own_block, 'blk', matching(blk_count, 4, p))]
    ppermute x2, starting transfers between devices: 1.19 us -> 2.53 us  [body(): lax.ppermute(own_block, 'blk', matching(blk_count, 4, p))]
  transfers between devices with their start and end apart: 10 -> 10, of which waited for: 4 -> 3; matrix products, arithmetic and copies ran while one was open for 0% -> 0% of each run, Pallas kernels for 9% -> 9%
where the time goes in v12:
time: 87.9 us; the launch traced here: 87.8 us
  blocking collectives  47.2 us (54%)
  waiting for transfers between devices  18.6 us (21%)
  Pallas kernels  11.3 us (13%)
  starting transfers between devices  8.85 us (10%)
  local copies, waits for them, and re-layouts  1.1 us (1%)
    all_to_all x1, blocking collectives, body(): got = lax.all_to_all(packed, 'blk', split_axis=0, concat_axis=0, tiled=True)  47.2 us
    ppermute x1, waiting for transfers between devices, body(): arrived = lax.ppermute(sent, 'map', [(0, 1), (1, 0)])  12.6 us
    pallas_call x6, Pallas kernels, call(): pl.pallas_call(kernel, out_shape=outs, in_specs=specs, out_specs=[pl.Bloc...  6.37 us
    ppermute x2, waiting for transfers between devices, body(): lax.ppermute(own_block, 'blk', matching(blk_count, 2, p))  6 us
    ppermute x2, starting transfers between devices, body(): lax.ppermute(own_block, 'blk', matching(blk_count, 2, p))  5.02 us
    pallas_call x1, Pallas kernels, body(): pl.pallas_call(functools.partial(first_kernel, map_count, STOPS * map_cou...  4.89 us
    ppermute x2, starting transfers between devices, body(): lax.ppermute(own_block, 'blk', matching(blk_count, 4, p))  2.53 us
  transfers between devices with their start and end apart: 10, of which 3 were waited for; matrix products, arithmetic and copies ran while one was open for 0% of the time, Pallas kernels for 9%

profile of v12, /device:TPU:32, one launch (start us, length us, event | category | flops | bytes accessed | tf_op | source)
XLA Modules:
  0.0 87.8 jit_solution(1585210707542338221)
XLA Ops:
  0.0 5.0 %collective-permute-start = (bf16[128,1024]{1,0:T(8,128)(2,1)}, bf16[128,1024]{1,0:T(8,128)(2,1)S(1)}, u32[]{:S(2)}, u32[]{:S(2)}) collective-permute-start(bf16[128,1024]{1,0:T(8,128)(2,1)} %bitcast.8), channel_id=1, source_target_pairs={{4,8},{8,4},{12,16},{16,12},{20,24},{24,20},{28,32},{32,28},{36,40... | collective-permute-start | bytes 786440 | tf_op jit(solution)/shard_map/ppermute | solution.py:350
  5.0 1.1 %collective-permute-start.5 = (bf16[128,1024]{1,0:T(8,128)(2,1)}, bf16[128,1024]{1,0:T(8,128)(2,1)S(1)}, u32[]{:S(2)}, u32[]{:S(2)}) collective-permute-start(bf16[128,1024]{1,0:T(8,128)(2,1)} %bitcast.10), channel_id=1, source_target_pairs={{0,8},{8,0},{16,24},{24,16},{32,40},{40,32},{48,56},{56,48},{64,72... | collective-permute-start | bytes 786440 | tf_op jit(solution)/shard_map/ppermute | solution.py:351
  6.1 1.4 %collective-permute-start.7 = (bf16[128,1024]{1,0:T(8,128)(2,1)}, bf16[128,1024]{1,0:T(8,128)(2,1)S(1)}, u32[]{:S(2)}, u32[]{:S(2)}) collective-permute-start(bf16[128,1024]{1,0:T(8,128)(2,1)} %bitcast.11), channel_id=1, source_target_pairs={{8,16},{16,8},{24,32},{32,24},{40,48},{48,40},{56,64},{64,56},{72,... | collective-permute-start | bytes 786440 | tf_op jit(solution)/shard_map/ppermute | solution.py:351
  8.2 0.9 %copy-done.1 = bf16[1,1,128,1024]{3,2,1,0:T(8,128)(2,1)S(1)} copy-done((bf16[1,1,128,1024]{3,2,1,0:T(8,128)(2,1)S(1)}, bf16[1,1,128,1024]{3,2,1,0:T(8,128)(2,1)}, u32[]{:S(2)}) %copy-start.1) | copy-done | bytes 262168
  9.2 4.9 %shard_map.73 = (f32[512,1024]{1,0:T(8,128)S(1)}, f32[3,128,512]{2,1,0:T(8,128)S(1)}, f32[3,128,512]{2,1,0:T(8,128)S(1)}, f32[3,128,512]{2,1,0:T(8,128)S(1)}, f3...) custom-call(f32[1]{0:T(128)S(6)} %copy.8.curvature, ...), custom_call_target="tpu_custom_call" | custom-call | flops 1073741824 | tf_op jit(solution)/shard_map/pallas_call | solution.py:374
  14.1 1.5 %collective-permute-done.near_b = bf16[128,1024]{1,0:T(8,128)(2,1)S(1)} collective-permute-done((bf16[128,1024]{1,0:T(8,128)(2,1)}, bf16[128,1024]{1,0:T(8,128)(2,1)S(1)}, u32[]{:S(2)}, u32[]{:S(2)}) %collective-permute-start) | collective-permute-done | bytes 262176 | tf_op jit(solution)/shard_map/ppermute | solution.py:350
  15.6 4.5 %collective-permute-done.1.near_a = bf16[128,1024]{1,0:T(8,128)(2,1)S(1)} collective-permute-done((bf16[128,1024]{1,0:T(8,128)(2,1)}, bf16[128,1024]{1,0:T(8,128)(2,1)S(1)}, u32[]{:S(2)}, u32[]{:S(2)}) %collective-permute-start.1) | collective-permute-done | bytes 262176 | tf_op jit(solution)/shard_map/ppermute | solution.py:350
  20.1 0.5 collective-permute-start.4
  20.6 0.0 collective-permute-start.6
  20.6 0.5 collective-permute-start.8
  21.1 1.6 %shard_map.74.before = f32[512,1024]{1,0:T(8,128)S(1)} custom-call(bf16[128,1024]{1,0:T(8,128)(2,1)S(1)} %collective-permute-done.1.near_a, bf16[128,1024]{1,0:T(8,128)(2,1)S(1)} %collective-permute-done.near_b, bf16[128,1024]{1,0:T(8,128)(2,1)S(1)} %collective-permute-done.5.far_a, bf16[128,1024]{1,0:T(8,128)(2,1)S(1)} %collective-permute-done.7.far_b, ...), custom_call_target="tpu_custom_call" | custom-call | flops 1610612736 | bytes 8650752 | tf_op jit(solution)/shard_map/pallas_call | solution.py:79
  22.7 1.2 %shard_map.75 = (bf16[256,1024]{1,0:T(8,128)(2,1)S(1)}, bf16[768,1024]{1,0:T(8,128)(2,1)S(1)}) custom-call(bf16[128,1024]{1,0:T(8,128)(2,1)S(1)} %collective-permute-done.3.twin_near_a, bf16[128,1024]{1,0:T(8,128)(2,1)S(1)} %collective-permute-done.4.twin_near_b, bf16[128,1024]{1,0:T(8,128)(2,1)S(1)} %collective-permute-done.6.twin_far_a, ...), custom_call_target="tpu_custom_call" | custom-call | flops 1610612736 | bytes 8650752 | tf_op jit(solution)/shard_map/pallas_call | solution.py:79
  23.9 0.0 copy-start
  24.0 0.0 copy-start.2
  24.0 0.0 copy-start.3
  24.0 0.0 copy-start.4
  24.0 0.3 collective-permute-start.9
  24.3 0.6 shard_map.76.kept
  24.9 0.1 copy-done
  25.0 0.6 shard_map.77
  25.7 12.6 %collective-permute-done.9.arrived = bf16[256,1024]{1,0:T(8,128)(2,1)S(1)} collective-permute-done((bf16[256,1024]{1,0:T(8,128)(2,1)S(1)}, bf16[256,1024]{1,0:T(8,128)(2,1)S(1)}, u32[]{:S(2)}, u32[]{:S(2)}) %collective-permute-start.9) | collective-permute-done | bytes 524320 | tf_op jit(solution)/shard_map/ppermute | solution.py:413
  38.2 0.5 shard_map.78
  38.7 47.2 %all_to_all.5.got = bf16[128,2,2176]{2,1,0:T(2,128)(2,1)S(1)} all-to-all(bf16[128,2,2176]{2,1,0:T(2,128)(2,1)S(1)} %shard_map.78), channel_id=1, replica_groups=mesh['blk'=128,'map'=2] {'blk'}, dimensions={0} | all-to-all | bytes 2228224 | tf_op jit(solution)/shard_map/all_to_all | solution.py:435
  85.9 1.9 %shard_map.79 = f32[256,512]{1,0:T(8,128)} custom-call(bf16[128,2,2176]{2,1,0:T(2,128)(2,1)S(1)} %all_to_all.5.got, bf16[512,512]{1,0:T(8,128)(2,1)S(1)} %get-tuple-element.56.weights), custom_call_target="tpu_custom_call" | custom-call | flops 805306368 | bytes 2162688 | tf_op jit(solution)/shard_map/pallas_call | solution.py:79
  (14 shorter events, 0.0 us)
Async XLA Ops:
  0.0 8.2 %collective-permute-start.2 = (bf16[128,1024]{1,0:T(8,128)(2,1)}, bf16[128,1024]{1,0:T(8,128)(2,1)S(1)}, u32[]{:S(2)}, u32[]{:S(2)}) collective-permute-start(bf16[128,1024]{1,0:T(8,128)(2,1)} %bitcast.7), channel_id=1, source_target_pairs={{0,2},{2,0},{4,6},{6,4},{8,10},{10,8},{12,14},{14,12},{16,18},{18,... | collective-permute-start | bytes 786440 | tf_op jit(solution)/shard_map/ppermute | solution.py:338
  0.0 15.6 %collective-permute-start = (bf16[128,1024]{1,0:T(8,128)(2,1)}, bf16[128,1024]{1,0:T(8,128)(2,1)S(1)}, u32[]{:S(2)}, u32[]{:S(2)}) collective-permute-start(bf16[128,1024]{1,0:T(8,128)(2,1)} %bitcast.8), channel_id=1, source_target_pairs={{4,8},{8,4},{12,16},{16,12},{20,24},{24,20},{28,32},{32,28},{36,40... | collective-permute-start | bytes 786440 | tf_op jit(solution)/shard_map/ppermute | solution.py:350
  5.0 15.0 %collective-permute-start.1 = (bf16[128,1024]{1,0:T(8,128)(2,1)}, bf16[128,1024]{1,0:T(8,128)(2,1)S(1)}, u32[]{:S(2)}, u32[]{:S(2)}) collective-permute-start(bf16[128,1024]{1,0:T(8,128)(2,1)} %bitcast.9), channel_id=1, source_target_pairs={{0,4},{4,0},{8,12},{12,8},{16,20},{20,16},{24,28},{28,24},{32,36},... | collective-permute-start | bytes 786440 | tf_op jit(solution)/shard_map/ppermute | solution.py:350
  5.0 15.6 %collective-permute-start.5 = (bf16[128,1024]{1,0:T(8,128)(2,1)}, bf16[128,1024]{1,0:T(8,128)(2,1)S(1)}, u32[]{:S(2)}, u32[]{:S(2)}) collective-permute-start(bf16[128,1024]{1,0:T(8,128)(2,1)} %bitcast.10), channel_id=1, source_target_pairs={{0,8},{8,0},{16,24},{24,16},{32,40},{40,32},{48,56},{56,48},{64,72... | collective-permute-start | bytes 786440 | tf_op jit(solution)/shard_map/ppermute | solution.py:351
  6.1 14.5 %collective-permute-start.7 = (bf16[128,1024]{1,0:T(8,128)(2,1)}, bf16[128,1024]{1,0:T(8,128)(2,1)S(1)}, u32[]{:S(2)}, u32[]{:S(2)}) collective-permute-start(bf16[128,1024]{1,0:T(8,128)(2,1)} %bitcast.11), channel_id=1, source_target_pairs={{8,16},{16,8},{24,32},{32,24},{40,48},{48,40},{56,64},{64,56},{72,... | collective-permute-start | bytes 786440 | tf_op jit(solution)/shard_map/ppermute | solution.py:351
  8.2 1.0 %copy-start.1 = (bf16[1,1,128,1024]{3,2,1,0:T(8,128)(2,1)S(1)}, bf16[1,1,128,1024]{3,2,1,0:T(8,128)(2,1)}, u32[]{:S(2)}) copy-start(bf16[1,1,128,1024]{3,2,1,0:T(8,128)(2,1)} %param.7) | copy-start | bytes 786436
  20.1 2.6 %collective-permute-start.3 = (bf16[128,1024]{1,0:T(8,128)(2,1)S(1)}, bf16[128,1024]{1,0:T(8,128)(2,1)S(1)}, u32[]{:S(2)}, u32[]{:S(2)}) collective-permute-start(bf16[128,1024]{1,0:T(8,128)(2,1)S(1)} %collective-permute-done.1.near_a), channel_id=1, source_target_pairs={{0,2},{2,0},{4,6},{6,4},{8,10},{10,8},{12,14},{14,12},{16,18},{18,... | collective-permute-start | bytes 786440 | tf_op jit(solution)/shard_map/ppermute | solution.py:338
  20.1 2.6 %collective-permute-start.4 = (bf16[128,1024]{1,0:T(8,128)(2,1)S(1)}, bf16[128,1024]{1,0:T(8,128)(2,1)S(1)}, u32[]{:S(2)}, u32[]{:S(2)}) collective-permute-start(bf16[128,1024]{1,0:T(8,128)(2,1)S(1)} %collective-permute-done.near_b), channel_id=1, source_target_pairs={{0,2},{2,0},{4,6},{6,4},{8,10},{10,8},{12,14},{14,12},{16,18},{18,... | collective-permute-start | bytes 786440 | tf_op jit(solution)/shard_map/ppermute | solution.py:338
  20.6 2.1 %collective-permute-start.6 = (bf16[128,1024]{1,0:T(8,128)(2,1)S(1)}, bf16[128,1024]{1,0:T(8,128)(2,1)S(1)}, u32[]{:S(2)}, u32[]{:S(2)}) collective-permute-start(bf16[128,1024]{1,0:T(8,128)(2,1)S(1)} %collective-permute-done.5.far_a), channel_id=1, source_target_pairs={{0,2},{2,0},{4,6},{6,4},{8,10},{10,8},{12,14},{14,12},{16,18},{18,... | collective-permute-start | bytes 786440 | tf_op jit(solution)/shard_map/ppermute | solution.py:338
  20.6 2.1 %collective-permute-start.8 = (bf16[128,1024]{1,0:T(8,128)(2,1)S(1)}, bf16[128,1024]{1,0:T(8,128)(2,1)S(1)}, u32[]{:S(2)}, u32[]{:S(2)}) collective-permute-start(bf16[128,1024]{1,0:T(8,128)(2,1)S(1)} %collective-permute-done.7.far_b), channel_id=1, source_target_pairs={{0,2},{2,0},{4,6},{6,4},{8,10},{10,8},{12,14},{14,12},{16,18},{18,... | collective-permute-start | bytes 786440 | tf_op jit(solution)/shard_map/ppermute | solution.py:338
  23.9 1.0 %copy-start = (bf16[1,512,512]{2,1,0:T(8,128)(2,1)S(1)}, bf16[1,512,512]{2,1,0:T(8,128)(2,1)}, u32[]{:S(2)}) copy-start(bf16[1,512,512]{2,1,0:T(8,128)(2,1)} %param.9) | copy-start | bytes 1572868
  24.0 1.0 %copy-start.2 = (s32[1,1,256,1]{2,3,1,0:T(1,128)S(1)}, s32[1,1,256,1]{2,3,1,0:T(1,128)}, u32[]{:S(2)}) copy-start(s32[1,1,256,1]{2,3,1,0:T(1,128)} %param.10) | copy-start | bytes 3076
  24.0 1.0 %copy-start.3 = (s32[1,1,256]{2,1,0:T(1,128)S(1)}, s32[1,1,256]{2,1,0:T(1,128)}, u32[]{:S(2)}) copy-start(s32[1,1,256]{2,1,0:T(1,128)} %param.11) | copy-start | bytes 3076
  24.0 1.0 %copy-start.4 = (s32[128]{0:T(128)S(1)}, s32[128]{0:T(128)}, u32[]{:S(2)}) copy-start(s32[128]{0:T(128)} %param.12) | copy-start | bytes 1540
  24.0 14.2 %collective-permute-start.9 = (bf16[256,1024]{1,0:T(8,128)(2,1)S(1)}, bf16[256,1024]{1,0:T(8,128)(2,1)S(1)}, u32[]{:S(2)}, u32[]{:S(2)}) collective-permute-start(bf16[256,1024]{1,0:T(8,128)(2,1)S(1)} %get-tuple-element.50), channel_id=1, source_target_pairs={{0,1},{1,0},{2,3},{3,2},{4,5},{5,4},{6,7},{7,6},{8,9},{9,8},{10,11... | collective-permute-start | bytes 1572872 | tf_op jit(solution)/shard_map/ppermute | solution.py:413
